TPU v7x, 512 devices: a whole 4x8x8 slice. The times are simulated.
512 devices in a mesh: dp: 64 (over y, x, core), proto: 8 (over z).
Axes of the slice: x: 4, y: 8, z: 8, core: 2. Of those that a mesh axis runs over, the one named last changes fastest.
Arguments:
- embeddings: bfloat16 [2, 131072, 128], P(None, ('dp', 'proto')), may hold values from -1 to 1
- prototypes: bfloat16 [128, 4096], P(None, 'proto'), may hold values from -1 to 1
Outputs:
- grad_embed: float32 [2, 131072, 128], P(None, ('dp', 'proto'))
- grad_proto: float32 [128, 4096], P(None, 'proto')
All inputs are finite; a program needn't handle non-finite values.
Results may differ from a plain program's by a relative error of at most 0.02.
Values may be sent and summed in bfloat16 or wider, within the bound.
No kernel may reach another device: no remote copies, remote signals or barrier semaphores. Data moves between devices by JAX's collectives and lax.ppermute only.
A program may use at most 64 MiB of HBM per device.

v0:
```python
import jax
import jax.numpy as jnp
from jax import lax
from jax.sharding import PartitionSpec as P

K = 4096
ITERS = 3


sink_eps = 0.05
sharpness_divisor = 0.1


def col_mass_sum(portion_result):
    return lax.psum(portion_result, "dp")


def row_mass_sum(portion_result):
    return lax.psum(portion_result, "proto")


def body(embeddings, prototypes):
    floats = embeddings.astype(jnp.float32)
    inverse = lax.rsqrt(jnp.sum(floats * floats, -1, keepdims=True) + 1e-06)
    unit_rows = floats * inverse
    normed_halfprecision = unit_rows.astype(jnp.bfloat16)
    proto_f = prototypes.astype(jnp.float32)
    unit_proto = (proto_f * lax.rsqrt(jnp.sum(proto_f * proto_f, 0, keepdims=True) + 1e-06)).astype(
        jnp.bfloat16
    )
    own_rows = embeddings.shape[1]
    users_all = own_rows * lax.axis_size("dp") * lax.axis_size("proto")
    group_rows = lax.all_gather(normed_halfprecision, "proto", axis=1, tiled=True)
    raw_similarity = jnp.einsum(
        "vrd,dk->vrk", group_rows, unit_proto, preferred_element_type=jnp.float32
    )
    kernel = jnp.exp(raw_similarity / sink_eps)
    powered_entries = jnp.exp(raw_similarity / sharpness_divisor)
    soft_partial = jnp.sum(powered_entries, 2)
    col_scale = 1.0 / (K * col_mass_sum(jnp.sum(kernel, 1)))
    first_partial = jnp.einsum("vrk,vk->vr", kernel, col_scale)
    soft_total = lax.psum(soft_partial, "proto")
    row_sum_value = row_mass_sum(first_partial)
    for sweep in range(ITERS - 1):
        row_scale = 1.0 / (users_all * row_sum_value)
        col_scale = 1.0 / (K * col_mass_sum(jnp.einsum("vrk,vr->vk", kernel, row_scale)))
        row_sum_value = row_mass_sum(jnp.einsum("vrk,vk->vr", kernel, col_scale))
    cluster_labels = kernel * col_scale[:, None, :] / row_sum_value[:, :, None]
    likelihood_matrix = powered_entries / soft_total[:, :, None]
    similarity_slope = ((likelihood_matrix - cluster_labels[::-1]) / sharpness_divisor).astype(
        jnp.bfloat16
    )
    grad_unit = (
        lax.psum_scatter(
            jnp.einsum(
                "vrk,dk->rvd", similarity_slope, unit_proto, preferred_element_type=jnp.float32
            ).astype(jnp.bfloat16),
            "proto",
            scatter_dimension=0,
            tiled=True,
        )
        .astype(jnp.float32)
        .transpose(1, 0, 2)
    )
    grad_part = jnp.einsum(
        "vrd,vrk->dk", group_rows, similarity_slope, preferred_element_type=jnp.float32
    )
    grad_proto = lax.psum(grad_part, "dp")
    grad_embed = inverse * (
        grad_unit - unit_rows * jnp.sum(unit_rows * grad_unit, -1, keepdims=True)
    )
    return (grad_embed, grad_proto)


def solution(mesh):
    placed = (P(None, ("dp", "proto"), None), P(None, "proto"))
    return jax.shard_map(
        body,
        mesh=mesh,
        in_specs=placed,
        out_specs=(P(None, ("dp", "proto"), None), P(None, "proto")),
        check_vma=False,
    )
```

profile of v0, /device:TPU:1, one launch (start us, length us, event | category | flops | bytes accessed | tf_op | source)
XLA Modules:
  0.0 792.5 jit_solution(9750238235399383490)
XLA Ops:
  7.2 1.1 fusion.16
  8.3 1.7 fusion.13
  11.0 42.7 %all-gather.2.cloned.1.call-done = bf16[2,2048,128]{2,1,0:T(8,128)(2,1)} async-done(((bf16[2,256,128]{2,1,0:T(8,128)(2,1)}), bf16[2,2048,128]{2,1,0:T(8,128)(2,1)}) %all-gather.2.cloned.1.call-update) | async-done | bytes 1048592 | tf_op jit(solution)/shard_map/all_gather | solution.py:33
  53.8 6.7 fusion.1
  60.5 128.7 %psum.57 = f32[2,512]{1,0:T(2,128)S(1)} all-reduce(f32[2,512]{1,0:T(2,128)S(1)} %get-tuple-element.3), channel_id=1, replica_groups=mesh['dp'=64,'proto'=8] {'dp'}, use_global_device_ids=true, to_apply=%region_5.0 | all-reduce | flops 1024 | bytes 8192 | tf_op jit(solution)/shard_map/psum | solution.py:15
  189.2 4.6 fusion.7
  193.8 21.0 %psum.58 = f32[2,2048]{1,0:T(2,128)S(1)} all-reduce(f32[2,2048]{1,0:T(2,128)S(1)} %bitcast.46), channel_id=1, replica_groups=mesh['dp'=64,'proto'=8] {'proto'}, use_global_device_ids=true, to_apply=%region_6.0 | all-reduce | flops 4096 | bytes 32768 | tf_op jit(solution)/shard_map/psum | solution.py:19
  214.9 4.6 fusion.6
  219.5 131.1 %psum.59 = f32[2,512]{1,0:T(2,128)S(1)} all-reduce(f32[2,512]{1,0:T(2,128)S(1)} %bitcast.48), channel_id=1, replica_groups=mesh['dp'=64,'proto'=8] {'dp'}, use_global_device_ids=true, to_apply=%region_7.0 | all-reduce | flops 1024 | bytes 8192 | tf_op jit(solution)/shard_map/psum | solution.py:15
  350.6 4.6 fusion.5
  355.2 20.4 %psum.60 = f32[2,2048]{1,0:T(2,128)S(1)} all-reduce(f32[2,2048]{1,0:T(2,128)S(1)} %bitcast.47), channel_id=1, replica_groups=mesh['dp'=64,'proto'=8] {'proto'}, use_global_device_ids=true, to_apply=%region_8.0 | all-reduce | flops 4096 | bytes 32768 | tf_op jit(solution)/shard_map/psum | solution.py:19
  375.5 4.6 fusion.4
  380.1 130.7 %psum.61 = f32[2,512]{1,0:T(2,128)S(1)} all-reduce(f32[2,512]{1,0:T(2,128)S(1)} %bitcast.49), channel_id=1, replica_groups=mesh['dp'=64,'proto'=8] {'dp'}, use_global_device_ids=true, to_apply=%region_9.0 | all-reduce | flops 1024 | bytes 8192 | tf_op jit(solution)/shard_map/psum | solution.py:15
  510.9 4.6 fusion.3
  515.5 21.1 %all-reduce = (f32[2,2048]{1,0:T(2,128)S(1)}, f32[2,2048]{1,0:T(2,128)S(1)}) all-reduce(f32[2,2048]{1,0:T(2,128)S(1)} %bitcast.45, f32[2,2048]{1,0:T(2,128)S(1)} %get-tuple-element.2), channel_id=1, replica_groups=mesh['dp'=64,'proto'=8] {'proto'}, use_global_device_ids=true, to_apply=%region_10.0 | all-reduce | flops 8192 | bytes 65536 | tf_op jit(solution)/shard_map/psum | solution.py:19
  536.6 4.2 multiply_divide_fusion
  540.9 4.6 multiply_convert_fusion
  545.5 1.9 copy-done
  547.5 2.2 fusion.2
  549.8 3.6 convolution_bitcast_fusion
  553.4 37.4 %reduce-scatter.2.cloned.1.call-done = bf16[256,2,128]{2,0,1:T(8,128)(2,1)} async-done(((bf16[2048,2,128]{2,0,1:T(8,128)(2,1)}), bf16[256,2,128]{2,0,1:T(8,128)(2,1)}) %reduce-scatter.2.cloned.1.call-update) | async-done | bytes 131088 | tf_op jit(solution)/shard_map/reduce_scatter | solution.py:54
  590.8 4.2 fusion.11
  595.0 189.2 %all-reduce.3.cloned.1.call-done = f32[128,512]{1,0:T(8,128)} async-done(((f32[128,512]{1,0:T(8,128)}), f32[128,512]{1,0:T(8,128)}) %all-reduce.3.cloned.1.call-update) | async-done | bytes 262160 | tf_op jit(solution)/shard_map/psum | solution.py:68
  784.3 1.7 copy.39
  (27 shorter events, 1.3 us)
Async XLA Ops:
  7.2 46.6 %all-gather.2.cloned.1.call-start = ((), (), s32[]{:S(2)}) async-start(), calls=%async_computation.1 | async-start | bytes 1179648 | tf_op jit(solution)/shard_map/all_gather | solution.py:33
  10.0 580.8 %reduce-scatter.2.cloned.1.call-start = ((), (), s32[]{:S(2)}) async-start(), calls=%async_computation.2 | async-start | bytes 1179648 | tf_op jit(solution)/shard_map/reduce_scatter | solution.py:54
  540.9 6.6 copy-start.2
  540.9 8.9 %copy-start.1 = (bf16[2,2048,128]{2,1,0:T(8,128)(2,1)S(1)}, bf16[2,2048,128]{2,1,0:T(8,128)(2,1)}, u32[]{:S(2)}) copy-start(bf16[2,2048,128]{2,1,0:T(8,128)(2,1)} %all-gather.2.cloned.1.call-done) | copy-start | bytes 3145732
  545.5 1.9 copy-start
  547.5 43.4 %copy-start.3 = (bf16[2,256,128]{2,1,0:T(8,128)(2,1)S(1)}, bf16[2,256,128]{2,1,0:T(8,128)(2,1)}, u32[]{:S(2)}) copy-start(bf16[2,256,128]{2,1,0:T(8,128)(2,1)} %param.2) | copy-start | bytes 393220
  549.7 234.6 %all-reduce.3.cloned.1.call-start = ((), (), s32[]{:S(2)}) async-start(), calls=%async_computation.3 | async-start | bytes 524288 | tf_op jit(solution)/shard_map/psum | solution.py:68
Sparse Core Ops, SparseCore 0:
  10.7 43.0 all-gather.1
  549.8 40.9 reduce-scatter.1
  594.9 189.3 all-reduce.2
where the time goes:
time: 793 us; the launch traced here: 792 us
  blocking collectives  453 us (57%)
  waiting for transfers between devices  269 us (34%)
  matrix products  35.6 us (4%)
  other arithmetic  16.9 us (2%)
  between operations  13.8 us (2%)
    psum x3, blocking collectives, col_mass_sum(): return lax.psum(portion_result, 'dp')  390 us
    psum x1, waiting for transfers between devices, body(): grad_proto = lax.psum(grad_part, 'dp')  189 us
    psum x3, blocking collectives, row_mass_sum(): return lax.psum(portion_result, 'proto')  62.5 us
    all_gather x1, waiting for transfers between devices, body(): lax.all_gather(normed_halfprecision, 'proto', axis=1, tiled=True)  42.7 us
    reduce_scatter x1, waiting for transfers between devices, body(): lax.psum_scatter(jnp.einsum('vrk,dk->rvd', similarity_slope, unit_proto,...  37.4 us
  transfers between devices with their start and end apart: 3, of which 3 were waited for; matrix products, arithmetic and copies ran while one was open for 1% of the time, Pallas kernels for 0%

commit v1 on v0

v1 whole, which is shorter than its diff:
```python
import jax
import jax.numpy as jnp
from jax import lax
from jax.sharding import PartitionSpec as P

K = 4096
ITERS = 3


sink_eps = 0.05
sharpness_divisor = 0.1


def share(x, axis):
    n = lax.axis_size(axis)
    return lax.all_to_all(jnp.broadcast_to(x[None], (n, *x.shape)), axis, 0, 0)


def total(x, axis):
    return jnp.sum(share(x, axis), 0)


def body(embeddings, prototypes):
    floats = embeddings.astype(jnp.float32)
    inverse = lax.rsqrt(jnp.sum(floats * floats, -1, keepdims=True) + 1e-06)
    unit_rows = floats * inverse
    normed_halfprecision = unit_rows.astype(jnp.bfloat16)
    proto_f = prototypes.astype(jnp.float32)
    unit_proto = (proto_f * lax.rsqrt(jnp.sum(proto_f * proto_f, 0, keepdims=True) + 1e-06)).astype(
        jnp.bfloat16
    )
    own_rows = embeddings.shape[1]
    n_dp, n_proto = lax.axis_size("dp"), lax.axis_size("proto")
    users_all = own_rows * n_dp * n_proto
    group_rows = share(normed_halfprecision, "proto")
    raw_similarity = jnp.einsum(
        "gvrd,dk->vgrk", group_rows, unit_proto, preferred_element_type=jnp.float32
    )
    kernel = jnp.exp(raw_similarity / sink_eps)
    powered_entries = jnp.exp(raw_similarity / sharpness_divisor)
    soft_partial = jnp.sum(powered_entries, 3)
    col_scale = 1.0 / (K * total(jnp.sum(kernel, (1, 2)), "dp"))
    first_partial = jnp.einsum("vgrk,vk->vgr", kernel, col_scale)
    row_sum_value, soft_total = total(jnp.stack([first_partial, soft_partial]), "proto")
    for sweep in range(ITERS - 1):
        row_scale = 1.0 / (users_all * row_sum_value)
        col_scale = 1.0 / (K * total(jnp.einsum("vgrk,vgr->vk", kernel, row_scale), "dp"))
        row_sum_value = total(jnp.einsum("vgrk,vk->vgr", kernel, col_scale), "proto")
    cluster_labels = kernel * col_scale[:, None, None, :] / row_sum_value[..., None]
    likelihood_matrix = powered_entries / soft_total[..., None]
    similarity_slope = ((likelihood_matrix - cluster_labels[::-1]) / sharpness_divisor).astype(
        jnp.bfloat16
    )
    unit_part = jnp.einsum(
        "vgrk,dk->gvrd", similarity_slope, unit_proto, preferred_element_type=jnp.float32
    ).astype(jnp.bfloat16)
    grad_unit = jnp.sum(lax.all_to_all(unit_part, "proto", 0, 0).astype(jnp.float32), 0)
    grad_part = jnp.einsum(
        "gvrd,vgrk->dk", group_rows, similarity_slope, preferred_element_type=jnp.float32
    )
    pieces = grad_part.reshape(n_dp, -1, 512)
    grad_proto = share(jnp.sum(lax.all_to_all(pieces, "dp", 0, 0), 0), "dp").reshape(grad_part.shape)
    grad_embed = inverse * (
        grad_unit - unit_rows * jnp.sum(unit_rows * grad_unit, -1, keepdims=True)
    )
    return (grad_embed, grad_proto)


def solution(mesh):
    placed = (P(None, ("dp", "proto"), None), P(None, "proto"))
    return jax.shard_map(
        body,
        mesh=mesh,
        in_specs=placed,
        out_specs=(P(None, ("dp", "proto"), None), P(None, "proto")),
        check_vma=False,
    )
```

time: 793 us -> 251 us (0.32)
  blocking collectives: 453 us -> 80.4 us
  waiting for transfers between devices: 269 us -> 80.7 us
  starting transfers between devices: 0.12 us -> 33.3 us
  between operations: 13.8 us -> 0.88 us
    psum x6 -> x0, blocking collectives: 453 us -> none  [the longest x3 390 us: col_mass_sum(): return lax.psum(portion_result, 'dp')]
    psum x1 -> x0, waiting for transfers between devices: 189 us -> none  [body(): grad_proto = lax.psum(grad_part, 'dp')]
    all_to_all x0 -> x5, waiting for transfers between devices: none -> 80.7 us  [the longest x4 52.4 us: share(): return lax.all_to_all(jnp.broadcast_to(x[None], (n, *x.shape)), axis, 0, 0)]
    all_to_all x0 -> x5, blocking collectives: none -> 80.4 us  [the longest x4 61.9 us: share(): return lax.all_to_all(jnp.broadcast_to(x[None], (n, *x.shape)), axis, 0, 0)]
    all_gather x1 -> x0, waiting for transfers between devices: 42.7 us -> none  [body(): lax.all_gather(normed_halfprecision, 'proto', axis=1, tiled=True)]
    reduce_scatter x1 -> x0, waiting for transfers between devices: 37.4 us -> none  [body(): lax.psum_scatter(jnp.einsum('vrk,dk->rvd', similarity_slope, unit_proto,...]
    all_to_all x0 -> x5, starting transfers between devices: none -> 33.3 us  [the longest x4 29.7 us: share(): return lax.all_to_all(jnp.broadcast_to(x[None], (n, *x.shape)), axis, 0, 0)]
  transfers between devices with their start and end apart: 3 -> 5, of which waited for: 3 -> 5; matrix products, arithmetic and copies ran while one was open for 1% -> 5% of each run, Pallas kernels for 0% -> 0%
where the time goes in v1:
time: 251 us; the launch traced here: 250 us
  waiting for transfers between devices  80.7 us (32%)
  blocking collectives  80.4 us (32%)
  starting transfers between devices  33.3 us (13%)
  matrix products  27.9 us (11%)
  other arithmetic  17.3 us (7%)
  local copies, waits for them, and re-layouts  9.63 us (4%)
    all_to_all x4, blocking collectives, share(): return lax.all_to_all(jnp.broadcast_to(x[None], (n, *x.shape)), axis, 0, 0)  61.9 us
    all_to_all x4, waiting for transfers between devices, share(): return lax.all_to_all(jnp.broadcast_to(x[None], (n, *x.shape)), axis, 0, 0)  52.4 us
    all_to_all x4, starting transfers between devices, share(): return lax.all_to_all(jnp.broadcast_to(x[None], (n, *x.shape)), axis, 0, 0)  29.7 us
    all_to_all x1, waiting for transfers between devices, body(): lax.all_to_all(unit_part, 'proto', 0, 0).astype(jnp.float32)  28.3 us
    all_to_all x1, blocking collectives, body(): lax.all_to_all(pieces, 'dp', 0, 0)  18.5 us
    dot_general x2, matrix products, body(): jnp.einsum('vgrk,vgr->vk', kernel, row_scale)  9.17 us
    exp x1, other arithmetic, body(): kernel = jnp.exp(raw_similarity / sink_eps)  6.48 us
    dot_general x1, matrix products, body(): jnp.einsum('gvrd,dk->vgrk', group_rows, unit_proto, preferred_element_typ...  5.82 us
  transfers between devices with their start and end apart: 5, of which 5 were waited for; matrix products, arithmetic and copies ran while one was open for 5% of the time, Pallas kernels for 0%

profile of v1, /device:TPU:1, one launch (start us, length us, event | category | flops | bytes accessed | tf_op | source)
XLA Modules:
  0.0 250.2 jit_solution(11727138634087664014)
XLA Ops:
  3.1 10.9 %all-to-all-start = ((bf16[8,2,256,128]{3,2,1,0:T(8,128)(2,1)}), bf16[8,2,256,128]{3,2,1,0:T(8,128)(2,1)S(1)}, u32[]{:S(2)}, u32[]{:S(2)}) async-start(bf16[8,2,256,128]{3,2,1,0:T(8,128)(2,1)} %broadcast_in_dim.16), calls=%async_computation | async-start | bytes 2097152 | tf_op jit(solution)/shard_map/all_to_all | solution.py:16
  14.9 28.2 %all-to-all-done = bf16[8,2,256,128]{3,2,1,0:T(8,128)(2,1)S(1)} async-done(((bf16[8,2,256,128]{3,2,1,0:T(8,128)(2,1)}), bf16[8,2,256,128]{3,2,1,0:T(8,128)(2,1)S(1)}, u32[]{:S(2)}, u32[]{:S(2)}) %all-to-all-start) | async-done | bytes 1048608 | tf_op jit(solution)/shard_map/all_to_all | solution.py:16
  43.1 5.8 %fusion.42 = (f32[2,512]{1,0:T(2,128)S(1)}, f32[2,8,256]{2,0,1:T(2,128)S(1)}, f32[512,8,2,256]{3,0,2,1:T(8,128)}) fusion(bf16[8,2,256,128]{3,2,1,0:T(8,128)(2,1)S(1)} %all-to-all-done, bf16[128,512]{1,0:T(8,128)(2,1)} %param.3, f32[512]{0:T(512)S(1)} %add_rsqrt_fusion), kind=kOutput, calls=%fused_computation.60 | convolution fusion | flops 545451008 | bytes 9590784 | tf_op jit(solution)/shard_map/gvrd,dk->vgrk/dot_general | solution.py:36
  49.7 10.6 %all-to-all-start.1 = ((f32[64,2,512]{2,1,0:T(2,128)}), f32[64,2,512]{2,1,0:T(2,128)S(1)}, u32[]{:S(2)}, u32[]{:S(2)}) async-start(f32[64,2,512]{2,1,0:T(2,128)} %broadcast_in_dim.17), calls=%async_computation.1 | async-start | bytes 524288 | tf_op jit(solution)/shard_map/all_to_all | solution.py:16
  60.3 6.5 %exponential_bitcast_fusion = bf16[2,8,256,512]{2,3,0,1:T(8,128)(2,1)} fusion(f32[512,8,2,256]{3,0,2,1:T(8,128)} %get-tuple-element.10), kind=kLoop, calls=%fused_computation.7 | loop fusion | flops 4194304 | bytes 12582912 | tf_op jit(solution)/shard_map/exp | solution.py:39
  66.8 6.7 %all-to-all-done.1 = f32[64,2,512]{2,1,0:T(2,128)S(1)} async-done(((f32[64,2,512]{2,1,0:T(2,128)}), f32[64,2,512]{2,1,0:T(2,128)S(1)}, u32[]{:S(2)}, u32[]{:S(2)}) %all-to-all-start.1) | async-done | bytes 262176 | tf_op jit(solution)/shard_map/all_to_all | solution.py:16
  73.6 2.8 %fusion.8 = f32[2,1,8,256]{3,1,2,0:T(1,128)S(1)} fusion(bf16[2,8,256,512]{2,3,0,1:T(8,128)(2,1)} %exponential_bitcast_fusion, bf16[2,512,1,1]{1,0,2,3:T(2,128)(2,1)S(1)} %divide_bitcast_fusion.2), kind=kOutput, calls=%fused_computation.13 | convolution fusion | flops 4194304 | bytes 4212736 | tf_op jit(solution)/shard_map/vgrk,vk->vgr/dot_general | solution.py:43
  76.5 14.8 %all_to_all.50 = f32[8,2,2,8,256]{4,3,2,1,0:T(8,128)S(1)} all-to-all(f32[8,2,2,8,256]{4,3,2,1,0:T(8,128)S(1)} %broadcast_in_dim.18), channel_id=1, replica_groups=mesh['dp'=64,'proto'=8] {'proto'}, dimensions={0} | all-to-all | bytes 524288 | tf_op jit(solution)/shard_map/all_to_all | solution.py:16
  91.3 4.6 %fusion.37 = f32[2,1,512,1]{2,1,0,3:T(1,128)S(1)} fusion(bf16[2,8,256,1]{2,1,0,3:T(8,128)(2,1)S(1)} %fusion.34, f32[512,8,2,256]{3,0,2,1:T(8,128)} %get-tuple-element.10), kind=kOutput, calls=%fused_computation.46 | convolution fusion | flops 6291456 | bytes 8400896 | tf_op jit(solution)/shard_map/vgrk,vgr->vk/dot_general | solution.py:47
  96.0 17.6 %all_to_all.51 = f32[64,2,512]{2,1,0:T(2,128)S(1)} all-to-all(f32[64,2,512]{2,1,0:T(2,128)S(1)} %broadcast_in_dim.19), channel_id=1, replica_groups=mesh['dp'=64,'proto'=8] {'dp'}, dimensions={0} | all-to-all | bytes 524288 | tf_op jit(solution)/shard_map/all_to_all | solution.py:16
  116.6 10.9 %all_to_all.52 = f32[8,2,8,256]{3,2,1,0:T(8,128)S(1)} all-to-all(f32[8,2,8,256]{3,2,1,0:T(8,128)S(1)} %broadcast_in_dim.20), channel_id=1, replica_groups=mesh['dp'=64,'proto'=8] {'proto'}, dimensions={0} | all-to-all | bytes 262144 | tf_op jit(solution)/shard_map/all_to_all | solution.py:16
  127.6 4.6 %fusion.35 = f32[2,1,512,1]{2,1,0,3:T(1,128)S(1)} fusion(bf16[2,8,256,1]{2,1,0,3:T(8,128)(2,1)S(1)} %divide_bitcast_fusion, f32[512,8,2,256]{3,0,2,1:T(8,128)} %get-tuple-element.10), kind=kOutput, calls=%fused_computation.43 | convolution fusion | flops 6291456 | bytes 8400896 | tf_op jit(solution)/shard_map/vgrk,vgr->vk/dot_general | solution.py:47
  132.3 18.6 %all_to_all.53 = f32[64,2,512]{2,1,0:T(2,128)S(1)} all-to-all(f32[64,2,512]{2,1,0:T(2,128)S(1)} %broadcast_in_dim.21), channel_id=1, replica_groups=mesh['dp'=64,'proto'=8] {'dp'}, dimensions={0} | all-to-all | bytes 524288 | tf_op jit(solution)/shard_map/all_to_all | solution.py:16
  151.0 2.8 %fusion.4 = f32[2,1,8,256]{3,1,2,0:T(1,128)S(1)} fusion(bf16[2,8,256,512]{2,3,0,1:T(8,128)(2,1)} %exponential_bitcast_fusion, f32[2,512,1,1]{1,0,2,3:T(2,128)S(1)} %fusion.46), kind=kOutput, calls=%fused_computation.9 | convolution fusion | flops 4194304 | bytes 4214784 | tf_op jit(solution)/shard_map/vgrk,vk->vgr/dot_general | solution.py:48
  154.5 3.6 %all-to-all-start.6 = ((f32[8,2,8,256]{3,2,1,0:T(8,128)}), f32[8,2,8,256]{3,2,1,0:T(8,128)S(1)}, u32[]{:S(2)}, u32[]{:S(2)}) async-start(f32[8,2,8,256]{3,2,1,0:T(8,128)} %broadcast_in_dim.22), calls=%async_computation.6 | async-start | bytes 262144 | tf_op jit(solution)/shard_map/all_to_all | solution.py:16
  158.1 8.3 %all-to-all-done.6 = f32[8,2,8,256]{3,2,1,0:T(8,128)S(1)} async-done(((f32[8,2,8,256]{3,2,1,0:T(8,128)}), f32[8,2,8,256]{3,2,1,0:T(8,128)S(1)}, u32[]{:S(2)}, u32[]{:S(2)}) %all-to-all-start.6) | async-done | bytes 131104 | tf_op jit(solution)/shard_map/all_to_all | solution.py:16
  166.4 4.2 %multiply_divide_fusion = f32[2,8,256,512]{2,3,0,1:T(8,128)S(1)} fusion(f32[2,8,256]{2,0,1:T(2,128)S(1)} %copy.38, f32[2,512]{1,0:T(2,128)S(1)} %multiply_divide_fusion.1, f32[512,8,2,256]{3,0,2,1:T(8,128)} %get-tuple-element.10), kind=kLoop, calls=%fused_computation.6 | loop fusion | flops 6291456 | bytes 16797696 | tf_op jit(solution)/shard_map/div | solution.py:49
  170.7 4.6 %fusion.3 = bf16[2,8,256,512]{2,3,0,1:T(8,128)(2,1)S(1)} fusion(f32[2,8,256,512]{2,3,0,1:T(8,128)S(1)} %multiply_divide_fusion, f32[512,8,2,256]{3,0,2,1:T(8,128)} %get-tuple-element.10, f32[2,8,256]{2,0,1:T(2,128)S(1)} %copy.35), kind=kLoop, calls=%fused_computation.5 | loop fusion | flops 10485760 | bytes 20987904 | tf_op jit(solution)/shard_map/convert_element_type | solution.py:51
  178.9 18.5 %all_to_all.54 = f32[64,2,512]{2,1,0:T(2,128)S(1)} all-to-all(f32[64,2,512]{2,1,0:T(2,128)S(1)} %reshape.41), channel_id=1, replica_groups=mesh['dp'=64,'proto'=8] {'dp'}, dimensions={0} | all-to-all | bytes 524288 | tf_op jit(solution)/shard_map/all_to_all | solution.py:62
  198.3 4.7 %all-to-all-start.9 = ((f32[64,2,512]{2,1,0:T(2,128)}), f32[64,2,512]{2,1,0:T(2,128)S(1)}, u32[]{:S(2)}, u32[]{:S(2)}) async-start(f32[64,2,512]{2,1,0:T(2,128)} %broadcast_in_dim.23), calls=%async_computation.9 | async-start | bytes 524288 | tf_op jit(solution)/shard_map/all_to_all | solution.py:16
  203.1 2.9 %fusion.15 = bf16[8,2,256,128]{2,3,0,1:T(8,128)(2,1)S(1)} fusion(bf16[2,8,256,512]{2,3,0,1:T(8,128)(2,1)} %copy-done, bf16[128,512]{1,0:T(8,128)(2,1)S(1)} %copy-done.1, f32[512]{0:T(512)S(1)} %add_rsqrt_fusion), kind=kOutput, calls=%fused_computation.19 | convolution fusion | flops 537591808 | bytes 5376000 | tf_op jit(solution)/shard_map/vgrk,dk->gvrd/dot_general | solution.py:54
  207.1 9.2 %all-to-all-done.9 = f32[64,2,512]{2,1,0:T(2,128)S(1)} async-done(((f32[64,2,512]{2,1,0:T(2,128)}), f32[64,2,512]{2,1,0:T(2,128)S(1)}, u32[]{:S(2)}, u32[]{:S(2)}) %all-to-all-start.9) | async-done | bytes 262176 | tf_op jit(solution)/shard_map/all_to_all | solution.py:16
  216.2 3.6 %all-to-all-start.7 = ((bf16[8,2,256,128]{2,3,1,0:T(8,128)(2,1)}), bf16[8,2,256,128]{2,3,1,0:T(8,128)(2,1)S(1)}, u32[]{:S(2)}, u32[]{:S(2)}) async-start(bf16[8,2,256,128]{2,3,1,0:T(8,128)(2,1)} %copy.40), calls=%async_computation.7 | async-start | bytes 2097152 | tf_op jit(solution)/shard_map/all_to_all | solution.py:57
  220.7 28.3 %all-to-all-done.7 = bf16[8,2,256,128]{2,3,1,0:T(8,128)(2,1)S(1)} async-done(((bf16[8,2,256,128]{2,3,1,0:T(8,128)(2,1)}), bf16[8,2,256,128]{2,3,1,0:T(8,128)(2,1)S(1)}, u32[]{:S(2)}, u32[]{:S(2)}) %all-to-all-start.7) | async-done | bytes 1048608 | tf_op jit(solution)/shard_map/all_to_all | solution.py:57
  (50 shorter events, 15.9 us)
Async XLA Ops:
  3.1 40.1 %all-to-all-start = ((bf16[8,2,256,128]{3,2,1,0:T(8,128)(2,1)}), bf16[8,2,256,128]{3,2,1,0:T(8,128)(2,1)S(1)}, u32[]{:S(2)}, u32[]{:S(2)}) async-start(bf16[8,2,256,128]{3,2,1,0:T(8,128)(2,1)} %broadcast_in_dim.16), calls=%async_computation | async-start | bytes 2097152 | tf_op jit(solution)/shard_map/all_to_all | solution.py:16
  49.7 23.8 %all-to-all-start.1 = ((f32[64,2,512]{2,1,0:T(2,128)}), f32[64,2,512]{2,1,0:T(2,128)S(1)}, u32[]{:S(2)}, u32[]{:S(2)}) async-start(f32[64,2,512]{2,1,0:T(2,128)} %broadcast_in_dim.17), calls=%async_computation.1 | async-start | bytes 524288 | tf_op jit(solution)/shard_map/all_to_all | solution.py:16
  154.5 11.9 %all-to-all-start.6 = ((f32[8,2,8,256]{3,2,1,0:T(8,128)}), f32[8,2,8,256]{3,2,1,0:T(8,128)S(1)}, u32[]{:S(2)}, u32[]{:S(2)}) async-start(f32[8,2,8,256]{3,2,1,0:T(8,128)} %broadcast_in_dim.22), calls=%async_computation.6 | async-start | bytes 262144 | tf_op jit(solution)/shard_map/all_to_all | solution.py:16
  170.7 32.4 %copy-start.1 = (bf16[128,512]{1,0:T(8,128)(2,1)S(1)}, bf16[128,512]{1,0:T(8,128)(2,1)}, u32[]{:S(2)}) copy-start(bf16[128,512]{1,0:T(8,128)(2,1)} %param.3) | copy-start | bytes 393220
  175.3 1.9 copy-start
  198.3 17.9 %all-to-all-start.9 = ((f32[64,2,512]{2,1,0:T(2,128)}), f32[64,2,512]{2,1,0:T(2,128)S(1)}, u32[]{:S(2)}, u32[]{:S(2)}) async-start(f32[64,2,512]{2,1,0:T(2,128)} %broadcast_in_dim.23), calls=%async_computation.9 | async-start | bytes 524288 | tf_op jit(solution)/shard_map/all_to_all | solution.py:16
  216.2 32.7 %all-to-all-start.7 = ((bf16[8,2,256,128]{2,3,1,0:T(8,128)(2,1)}), bf16[8,2,256,128]{2,3,1,0:T(8,128)(2,1)S(1)}, u32[]{:S(2)}, u32[]{:S(2)}) async-start(bf16[8,2,256,128]{2,3,1,0:T(8,128)(2,1)} %copy.40), calls=%async_computation.7 | async-start | bytes 2097152 | tf_op jit(solution)/shard_map/all_to_all | solution.py:57

commit v2 on v1

v2 whole, which is shorter than its diff:
```python
import functools

import jax
import jax.numpy as jnp
from jax import lax
from jax.experimental import pallas as pl
from jax.experimental.pallas import tpu as pltpu
from jax.sharding import Mesh, PartitionSpec as P

K = 4096
ITERS = 3
SINK = 0.05
SHARP = 0.1

NY, NX, NC, NZ = 8, 4, 2, 8
G = NX * NC
U = 256
SUB = 512 // G
COLS = NZ * SUB
Q = COLS // 128
f32, bf16 = jnp.float32, jnp.bfloat16
VM = pl.BlockSpec(memory_space=pltpu.VMEM)


def call(kernel, outs, *args):
    return pl.pallas_call(
        kernel,
        out_shape=outs,
        in_specs=[VM] * len(args),
        out_specs=jax.tree.map(lambda _: VM, outs),
        compiler_params=pltpu.CompilerParams(vmem_limit_bytes=20 * 1024 * 1024),
    )(*args)


def fold(x):
    return jnp.sum(x.reshape(-1, 8, x.shape[-1]), 0)


def send_columns(acc, out):
    rows = [jnp.sum(acc[i].T, 0, keepdims=True) for i in range(2 * Q)]
    part = jnp.concatenate(rows, 0)
    out[...] = jnp.concatenate([part] * (NY * NZ), 0).astype(out.dtype)


def groups(step, mine, other):
    core = lax.axis_index("c")
    for half, rows in enumerate((mine, other)):
        def member(x, _):
            step(lax.rem(core + half, NC) * NX + x, x, rows)
            return 0

        lax.fori_loop(0, NX, member, 0)


def scores_kernel(mine, other, proto, powered, masses, soft, columns, acc):
    acc[...] = jnp.zeros_like(acc)

    def group(g, x, rows):
        for v in range(2):
            rowsum = jnp.zeros((8, U), f32)
            for q in range(Q):
                s = lax.dot_general(
                    proto[q * 128 : (q + 1) * 128, :],
                    rows[x, v],
                    (((1,), (1,)), ((), ())),
                    preferred_element_type=f32,
                )
                e = jnp.exp(s * (1.0 / SHARP))
                k = e * e
                powered[g, v, q * 128 : (q + 1) * 128, :] = e
                masses[g, v, q * 128 : (q + 1) * 128, :] = k
                rowsum += fold(e)
                acc[v * Q + q] += k[:, :128] + k[:, 128:]
            soft[g, v : v + 1, :] = jnp.sum(rowsum, 0, keepdims=True)

    groups(group, mine, other)
    send_columns(acc, columns)


def rows_kernel(with_soft, masses, columns, *refs):
    soft, (out, scale) = (refs[0], refs[1:]) if with_soft else (None, refs)
    got = columns[...].astype(f32)
    c = 1.0 / (K * fold(got))
    scale[...] = c
    turned = jnp.concatenate([c] * 16, 0).T
    n = 4 if with_soft else 2

    def group(g, _):
        lines = []
        for v in range(2):
            total = jnp.zeros((8, U), f32)
            for q in range(Q):
                i = v * Q + q
                total += fold(masses[g, v, q * 128 : (q + 1) * 128, :] * turned[:, i : i + 1])
            lines.append(jnp.sum(total, 0, keepdims=True))
        for v in range(2):
            out[0, g, v : v + 1, :] = lines[v]
        if with_soft:
            out[0, g, 2:4, :] = soft[g]
        return 0

    lax.fori_loop(0, G, group, 0)
    for i in range(1, G):
        out[i] = out[0]


def columns_kernel(masses, rowmass, columns, acc):
    acc[...] = jnp.zeros_like(acc)

    def group(g, _):
        total = rowmass[0, g, 0:2, :]
        for i in range(1, G):
            total += rowmass[i, g, 0:2, :]
        r = 1.0 / (NY * NX * NC * NZ * U * total)
        for v in range(2):
            for q in range(Q):
                k = masses[g, v, q * 128 : (q + 1) * 128, :] * r[v : v + 1, :]
                acc[v * Q + q] += k[:, :128] + k[:, 128:]
        return 0

    lax.fori_loop(0, G, group, 0)
    send_columns(acc, columns)


def slopes_kernel(mine, other, proto, powered, masses, scale, first, last, unit, parts, acc):
    acc[...] = jnp.zeros_like(acc)
    turned = jnp.concatenate([scale[...] * (1.0 / SHARP)] * 16, 0).T

    def group(g, x, rows):
        soft, mass = first[0, g, 2:4, :], last[0, g, 0:2, :]
        for i in range(1, G):
            soft += first[i, g, 2:4, :]
            mass += last[i, g, 0:2, :]
        a = (1.0 / SHARP) / soft
        b = 1.0 / mass
        place = lax.rem(g, NX) * NC + lax.div(g, NX)
        for v in range(2):
            w = 1 - v
            made = jnp.zeros((U, 128), f32)
            for q in range(Q):
                at = slice(q * 128, (q + 1) * 128)
                i = w * Q + q
                slope = (
                    powered[g, v, at, :] * a[v : v + 1, :]
                    - masses[g, w, at, :] * turned[:, i : i + 1] * b[w : w + 1, :]
                ).astype(bf16)
                made += lax.dot_general(
                    slope, proto[at, :], (((0,), (0,)), ((), ())), preferred_element_type=f32
                )
                acc[at, :] += jnp.dot(slope, rows[x, v], preferred_element_type=f32)
            unit[place, v] = made.astype(bf16)

    groups(group, mine, other)
    parts[...] = acc[...].astype(bf16)


def share(x, axis):
    n = lax.axis_size(axis)
    return lax.all_to_all(jnp.broadcast_to(x[None], (n, *x.shape)), axis, 0, 0)


def body(embeddings, prototypes):
    floats = embeddings.astype(f32)
    inverse = lax.rsqrt(jnp.sum(floats * floats, -1, keepdims=True) + 1e-06)
    unit_rows = floats * inverse
    j = lax.axis_index("x") * NC + lax.axis_index("c")
    proto_f = lax.dynamic_slice(prototypes, (0, j * SUB), (128, SUB)).astype(f32).T
    proto_own = (proto_f * lax.rsqrt(jnp.sum(proto_f * proto_f, 1, keepdims=True) + 1e-06)).astype(bf16)
    proto = share(proto_own, "z").reshape(COLS, 128)
    mine = share(unit_rows.astype(bf16), "x")
    other = lax.ppermute(mine, "c", [(0, 1), (1, 0)])

    kept = pltpu.VMEM((G, 2, COLS, U), f32)
    sums = jax.ShapeDtypeStruct((NY * NZ * 8, 128), bf16)
    acc = pltpu.VMEM((2 * Q, 128, 128), f32)

    def with_acc(kernel, outs, *args, scratch=acc):
        return pl.pallas_call(
            kernel,
            out_shape=outs,
            in_specs=[VM] * len(args),
            out_specs=jax.tree.map(lambda _: VM, outs),
            scratch_shapes=[scratch],
            compiler_params=pltpu.CompilerParams(vmem_limit_bytes=20 * 1024 * 1024),
        )(*args)

    powered, masses, soft, columns = with_acc(
        scores_kernel, (kept, kept, jax.ShapeDtypeStruct((G, 2, U), f32), sums), mine, other, proto
    )
    first = None
    for sweep in range(ITERS):
        columns = lax.all_to_all(columns, ("y", "z"), 0, 0, tiled=True)
        more = (soft,) if sweep == 0 else ()
        lines = jax.ShapeDtypeStruct((G, G, 4 if more else 2, U), f32)
        mass, scale = call(
            functools.partial(rows_kernel, bool(more)),
            (lines, jax.ShapeDtypeStruct((8, 128), f32)),
            masses,
            columns,
            *more,
        )
        mass = lax.all_to_all(mass, ("x", "c"), 0, 0)
        first = mass if first is None else first
        if sweep < ITERS - 1:
            columns = with_acc(columns_kernel, sums, masses, mass)
    unit, parts = with_acc(
        slopes_kernel,
        (jax.ShapeDtypeStruct((G, 2, U, 128), bf16), jax.ShapeDtypeStruct((COLS, 128), bf16)),
        mine,
        other,
        proto,
        powered,
        masses,
        scale,
        first,
        mass,
        scratch=pltpu.VMEM((COLS, 128), f32),
    )
    grad_unit = lax.psum_scatter(unit, ("x", "c"), scatter_dimension=0, tiled=True)[0].astype(f32)
    grad_embed = inverse * (
        grad_unit - unit_rows * jnp.sum(unit_rows * grad_unit, -1, keepdims=True)
    )
    pieces = parts.reshape(NZ, NY, SUB // NY, 128).transpose(1, 0, 2, 3)
    pieces = pieces.reshape(NY * NZ, SUB // NY, 128)
    piece = jnp.sum(lax.all_to_all(pieces, ("y", "z"), 0, 0).astype(f32), 0).astype(bf16)
    whole = share(piece, ("y", "x", "c")).reshape(NY, G, SUB // NY, 128).transpose(1, 0, 2, 3)
    grad_proto = whole.reshape(NZ * SUB, 128).astype(f32).T
    return (grad_embed, grad_proto)


def solution(mesh):
    fine = Mesh(mesh.devices.reshape(NY, NX, NC, NZ), ("y", "x", "c", "z"))
    placed = (P(None, ("y", "x", "c", "z"), None), P(None, "z"))
    return jax.shard_map(
        body, mesh=fine, in_specs=placed, out_specs=placed, check_vma=False
    )
```

time: 251 us -> 193 us (0.77)
  waiting for transfers between devices: 80.7 us -> 6.09 us
  blocking collectives: 80.4 us -> 129 us
  matrix products: 27.9 us -> 0 us
  Pallas kernels: 0 us -> 19.9 us
  starting transfers between devices: 33.3 us -> 13.4 us
  between operations: 0.88 us -> 14.1 us
  other arithmetic: 17.3 us -> 8.09 us
  local copies, waits for them, and re-layouts: 9.63 us -> 1.87 us
    all_to_all x1 -> x7, blocking collectives: 18.5 us -> 96.7 us  [the longest x3 50.6 us: body(): columns = lax.all_to_all(columns, ('y', 'z'), 0, 0, tiled=True)]
    all_to_all x4 -> x1, waiting for transfers between devices: 52.4 us -> 6.07 us  [share(): return lax.all_to_all(jnp.broadcast_to(x[None], (n, *x.shape)), axis, 0, 0)]
    all_to_all x4 -> x2, blocking collectives: 61.9 us -> 31.9 us  [share(): return lax.all_to_all(jnp.broadcast_to(x[None], (n, *x.shape)), axis, 0, 0)]
    all_to_all x1 -> x0, waiting for transfers between devices: 28.3 us -> none  [body(): lax.all_to_all(unit_part, 'proto', 0, 0).astype(jnp.float32)]
    dot_general x8 -> x0, matrix products: 27.9 us -> none  [the longest x2 9.17 us: body(): jnp.einsum('vgrk,vgr->vk', kernel, row_scale)]
    all_to_all x4 -> x1, starting transfers between devices: 29.7 us -> 4.84 us  [share(): return lax.all_to_all(jnp.broadcast_to(x[None], (n, *x.shape)), axis, 0, 0)]
    pallas_call x0 -> x7, Pallas kernels: none -> 19.9 us  [the longest x4 12.8 us: with_acc(): pl.pallas_call(kernel, out_shape=outs, in_specs=[VM] * len(args), out_spe...]
    ppermute x0 -> x1, starting transfers between devices: none -> 8.52 us  [body(): other = lax.ppermute(mine, 'c', [(0, 1), (1, 0)])]
  transfers between devices with their start and end apart: 5 -> 3, of which waited for: 5 -> 1; matrix products, arithmetic and copies ran while one was open for 5% -> 1% of each run, Pallas kernels for 0% -> 0%
where the time goes in v2:
time: 193 us; the launch traced here: 192 us
  blocking collectives  129 us (67%)
  Pallas kernels  19.9 us (10%)
  between operations  14.1 us (7%)
  starting transfers between devices  13.4 us (7%)
  other arithmetic  8.09 us (4%)
  waiting for transfers between devices  6.09 us (3%)
    all_to_all x3, blocking collectives, body(): columns = lax.all_to_all(columns, ('y', 'z'), 0, 0, tiled=True)  50.6 us
    all_to_all x2, blocking collectives, share(): return lax.all_to_all(jnp.broadcast_to(x[None], (n, *x.shape)), axis, 0, 0)  31.9 us
    all_to_all x3, blocking collectives, body(): mass = lax.all_to_all(mass, ('x', 'c'), 0, 0)  30.7 us
    all_to_all x1, blocking collectives, body(): lax.all_to_all(pieces, ('y', 'z'), 0, 0).astype(f32)  15.4 us
    pallas_call x4, Pallas kernels, with_acc(): pl.pallas_call(kernel, out_shape=outs, in_specs=[VM] * len(args), out_spe...  12.8 us
    ppermute x1, starting transfers between devices, body(): other = lax.ppermute(mine, 'c', [(0, 1), (1, 0)])  8.52 us
    pallas_call x3, Pallas kernels, call(): pl.pallas_call(kernel, out_shape=outs, in_specs=[VM] * len(args), out_spe...  7.02 us
    all_to_all x1, waiting for transfers between devices, share(): return lax.all_to_all(jnp.broadcast_to(x[None], (n, *x.shape)), axis, 0, 0)  6.07 us
  transfers between devices with their start and end apart: 3, of which 1 were waited for; matrix products, arithmetic and copies ran while one was open for 1% of the time, Pallas kernels for 0%

profile of v2, /device:TPU:1, one launch (start us, length us, event | category | flops | bytes accessed | tf_op | source)
XLA Modules:
  0.0 192.1 jit_solution(7119774098587272040)
XLA Ops:
  7.2 1.1 fusion.6
  8.2 1.0 fusion.5
  9.3 0.9 broadcast_in_dim.6
  10.1 4.8 %all-to-all-start = ((bf16[4,2,256,128]{3,2,1,0:T(8,128)(2,1)}), bf16[4,2,256,128]{3,2,1,0:T(8,128)(2,1)S(1)}, u32[]{:S(2)}, u32[]{:S(2)}) async-start(bf16[4,2,256,128]{3,2,1,0:T(8,128)(2,1)} %broadcast_in_dim.6), calls=%async_computation | async-start | bytes 1048576 | tf_op jit(solution)/shard_map/all_to_all | solution.py:159
  15.0 0.9 fusion.9
  15.8 6.1 %all-to-all-done.mine = bf16[4,2,256,128]{3,2,1,0:T(8,128)(2,1)S(1)} async-done(((bf16[4,2,256,128]{3,2,1,0:T(8,128)(2,1)}), bf16[4,2,256,128]{3,2,1,0:T(8,128)(2,1)S(1)}, u32[]{:S(2)}, u32[]{:S(2)}) %all-to-all-start) | async-done | bytes 524320 | tf_op jit(solution)/shard_map/all_to_all | solution.py:159
  21.9 8.5 %collective-permute-start = (bf16[4,2,256,128]{3,2,1,0:T(8,128)(2,1)S(1)}, bf16[4,2,256,128]{3,2,1,0:T(8,128)(2,1)S(1)}, u32[]{:S(2)}, u32[]{:S(2)}) collective-permute-start(bf16[4,2,256,128]{3,2,1,0:T(8,128)(2,1)S(1)} %all-to-all-done.mine), channel_id=1, source_target_pairs={{0,8},{8,0},{1,9},{9,1},{2,10},{10,2},{3,11},{11,3},{4,12},{12,4},... | collective-permute-start | bytes 1572872 | tf_op jit(solution)/shard_map/ppermute | solution.py:171
  31.4 15.2 %all_to_all.68 = bf16[8,64,128]{2,1,0:T(8,128)(2,1)S(1)} all-to-all(bf16[8,64,128]{2,1,0:T(8,128)(2,1)S(1)} %broadcast_in_dim.7), channel_id=1, replica_groups=mesh['y'=8,'x'=4,'c'=2,'z'=8] {'z'}, dimensions={0} | all-to-all | bytes 262144 | tf_op jit(solution)/shard_map/all_to_all | solution.py:159
  46.7 3.4 %shard_map.41 = (f32[8,2,512,256]{3,2,1,0:T(8,128)S(1)}, f32[8,2,512,256]{3,2,1,0:T(8,128)S(1)}, f32[8,2,256]{2,1,0:T(2,128)S(1)}, bf16[512,128]{1,0:T(8,128)(2,1)S(1)}) custom-call(bf16[4,2,256,128]{3,2,1,0:T(8,128)(2,1)S(1)} %all-to-all-done.mine, bf16[4,2,256,128]{3,2,1,0:T(8,128)(2,1)S(1)} %collective-permute-done.other, bf16[512,128]{1,0:T(8,128)(2,1)S(1)} %bitcast.27), custom_call_target="tpu_custom_call" | custom-call | tf_op jit(solution)/shard_map/pallas_call | solution.py:178
  50.1 19.8 %all_to_all.69 = bf16[64,8,128]{2,1,0:T(8,128)(2,1)S(1)} all-to-all(bf16[64,8,128]{2,1,0:T(8,128)(2,1)S(1)} %bitcast.35), channel_id=1, replica_groups=mesh['y'=8,'x'=4,'c'=2,'z'=8] {'y','z'}, dimensions={0} | all-to-all | bytes 262144 | tf_op jit(solution)/shard_map/all_to_all | solution.py:192
  69.9 2.5 %shard_map.42 = (f32[8,8,4,256]{3,2,1,0:T(4,128)S(1)}, f32[8,128]{1,0:T(8,128)}) custom-call(f32[8,2,512,256]{3,2,1,0:T(8,128)S(1)} %get-tuple-element.13.masses, bf16[512,128]{1,0:T(8,128)(2,1)S(1)} %bitcast.29, f32[8,2,256]{2,1,0:T(2,128)S(1)} %get-tuple-element.15.refs_0_), custom_call_target="tpu_custom_call" | custom-call | tf_op jit(solution)/shard_map/pallas_call | solution.py:26
  72.3 11.1 %all_to_all.70.rowmass.first = f32[8,8,4,256]{3,2,1,0:T(4,128)S(1)} all-to-all(f32[8,8,4,256]{3,2,1,0:T(4,128)S(1)} %get-tuple-element.16), channel_id=1, replica_groups=mesh['y'=8,'x'=4,'c'=2,'z'=8] {'x','c'}, dimensions={0} | all-to-all | bytes 524288 | tf_op jit(solution)/shard_map/all_to_all | solution.py:202
  83.4 1.2 shard_map.43
  84.6 15.4 %all_to_all.71 = bf16[64,8,128]{2,1,0:T(8,128)(2,1)S(1)} all-to-all(bf16[64,8,128]{2,1,0:T(8,128)(2,1)S(1)} %bitcast.33), channel_id=1, replica_groups=mesh['y'=8,'x'=4,'c'=2,'z'=8] {'y','z'}, dimensions={0} | all-to-all | bytes 262144 | tf_op jit(solution)/shard_map/all_to_all | solution.py:192
  100.0 2.5 %shard_map.44 = (f32[8,8,2,256]{3,2,1,0:T(2,128)S(1)}, f32[8,128]{1,0:T(8,128)}) custom-call(f32[8,2,512,256]{3,2,1,0:T(8,128)S(1)} %get-tuple-element.13.masses, bf16[512,128]{1,0:T(8,128)(2,1)S(1)} %bitcast.30), custom_call_target="tpu_custom_call" | custom-call | tf_op jit(solution)/shard_map/pallas_call | solution.py:26
  102.5 9.9 %all_to_all.72.rowmass = f32[8,8,2,256]{3,2,1,0:T(2,128)S(1)} all-to-all(f32[8,8,2,256]{3,2,1,0:T(2,128)S(1)} %get-tuple-element.17), channel_id=1, replica_groups=mesh['y'=8,'x'=4,'c'=2,'z'=8] {'x','c'}, dimensions={0} | all-to-all | bytes 262144 | tf_op jit(solution)/shard_map/all_to_all | solution.py:202
  112.4 1.2 shard_map.45
  113.6 15.4 %all_to_all.73 = bf16[64,8,128]{2,1,0:T(8,128)(2,1)S(1)} all-to-all(bf16[64,8,128]{2,1,0:T(8,128)(2,1)S(1)} %bitcast.32), channel_id=1, replica_groups=mesh['y'=8,'x'=4,'c'=2,'z'=8] {'y','z'}, dimensions={0} | all-to-all | bytes 262144 | tf_op jit(solution)/shard_map/all_to_all | solution.py:192
  129.0 2.1 %shard_map.46 = (f32[8,8,2,256]{3,2,1,0:T(2,128)S(1)}, f32[8,128]{1,0:T(8,128)S(1)}) custom-call(f32[8,2,512,256]{3,2,1,0:T(8,128)S(1)} %get-tuple-element.13.masses, bf16[512,128]{1,0:T(8,128)(2,1)S(1)} %bitcast.31), custom_call_target="tpu_custom_call" | custom-call | tf_op jit(solution)/shard_map/pallas_call | solution.py:26
  131.1 9.7 %all_to_all.74.last = f32[8,8,2,256]{3,2,1,0:T(2,128)S(1)} all-to-all(f32[8,8,2,256]{3,2,1,0:T(2,128)S(1)} %get-tuple-element.19), channel_id=1, replica_groups=mesh['y'=8,'x'=4,'c'=2,'z'=8] {'x','c'}, dimensions={0} | all-to-all | bytes 262144 | tf_op jit(solution)/shard_map/all_to_all | solution.py:202
  140.8 7.0 %shard_map.47 = (bf16[8,2,256,128]{3,2,1,0:T(8,128)(2,1)}, bf16[512,128]{1,0:T(8,128)(2,1)S(1)}) custom-call(bf16[4,2,256,128]{3,2,1,0:T(8,128)(2,1)S(1)} %all-to-all-done.mine, bf16[4,2,256,128]{3,2,1,0:T(8,128)(2,1)S(1)} %collective-permute-done.other, bf16[512,128]{1,0:T(8,128)(2,1)S(1)} %bitcast.28, f32[8,2,512,256]{3,2,1,0:T(8,128)S(1)} %get-tuple-element.12.powered, ...), custom_call_target="tpu_custom_call" | custom-call | tf_op jit(solution)/shard_map/pallas_call | solution.py:178
  147.9 15.4 %all_to_all.75 = bf16[64,8,128]{2,1,0:T(8,128)(2,1)S(1)} all-to-all(bf16[64,8,128]{2,1,0:T(8,128)(2,1)S(1)} %bitcast.38), channel_id=1, replica_groups=mesh['y'=8,'x'=4,'c'=2,'z'=8] {'y','z'}, dimensions={0} | all-to-all | bytes 262144 | tf_op jit(solution)/shard_map/all_to_all | solution.py:225
  163.4 16.7 %all_to_all.76 = bf16[64,8,128]{2,1,0:T(8,128)(2,1)S(1)} all-to-all(bf16[64,8,128]{2,1,0:T(8,128)(2,1)S(1)} %broadcast_in_dim.8), channel_id=1, replica_groups=mesh['y'=8,'x'=4,'c'=2,'z'=8] {'y','x','c'}, dimensions={0} | all-to-all | bytes 262144 | tf_op jit(solution)/shard_map/all_to_all | solution.py:159
  181.0 4.2 %fusion.3 = f32[2,256,128]{2,1,0:T(8,128)} fusion(bf16[2,256,128]{2,1,0:T(8,128)(2,1)S(1)} %copy-done, bf16[1,2,256,128]{3,2,1,0:T(8,128)(2,1)} %reduce-scatter.2.cloned.1.call-done, f32[2,256]{1,0:T(2,128)S(1)} %add_rsqrt_fusion), kind=kOutput, calls=%fused_computation.3 | output fusion | flops 655999 | bytes 526336 | tf_op jit(solution)/shard_map/mul | solution.py:221
  (17 shorter events, 2.0 us)
Async XLA Ops:
  10.1 11.8 %all-to-all-start = ((bf16[4,2,256,128]{3,2,1,0:T(8,128)(2,1)}), bf16[4,2,256,128]{3,2,1,0:T(8,128)(2,1)S(1)}, u32[]{:S(2)}, u32[]{:S(2)}) async-start(bf16[4,2,256,128]{3,2,1,0:T(8,128)(2,1)} %broadcast_in_dim.6), calls=%async_computation | async-start | bytes 1048576 | tf_op jit(solution)/shard_map/all_to_all | solution.py:159
  15.0 166.0 %reduce-scatter.2.cloned.1.call-start = ((), (), s32[]{:S(2)}) async-start(), calls=%async_computation.11 | async-start | bytes 1179648 | tf_op jit(solution)/shard_map/reduce_scatter | solution.py:219
  21.9 24.7 %collective-permute-start = (bf16[4,2,256,128]{3,2,1,0:T(8,128)(2,1)S(1)}, bf16[4,2,256,128]{3,2,1,0:T(8,128)(2,1)S(1)}, u32[]{:S(2)}, u32[]{:S(2)}) collective-permute-start(bf16[4,2,256,128]{3,2,1,0:T(8,128)(2,1)S(1)} %all-to-all-done.mine), channel_id=1, source_target_pairs={{0,8},{8,0},{1,9},{9,1},{2,10},{10,2},{3,11},{11,3},{4,12},{12,4},... | collective-permute-start | bytes 1572872 | tf_op jit(solution)/shard_map/ppermute | solution.py:171
  140.8 40.2 %copy-start = (bf16[2,256,128]{2,1,0:T(8,128)(2,1)S(1)}, bf16[2,256,128]{2,1,0:T(8,128)(2,1)}, u32[]{:S(2)}) copy-start(bf16[2,256,128]{2,1,0:T(8,128)(2,1)} %param.2) | copy-start | bytes 393220
Sparse Core Ops, SparseCore 0:
  148.0 25.4 reduce-scatter.1

commit v3 on v2

v3 whole, which is shorter than its diff:
```python
import functools

import jax
import jax.numpy as jnp
from jax import lax
from jax.experimental import pallas as pl
from jax.experimental.pallas import tpu as pltpu
from jax.sharding import Mesh, PartitionSpec as P

K = 4096
ITERS = 3
SINK = 0.05
SHARP = 0.1

NY, NX, NC, NZ = 8, 4, 2, 8
G = NX * NC
U = 256
SUB = 512 // G
COLS = NZ * SUB
Q = COLS // 128
USERS = NY * NX * NC * NZ * U
EPS = 1e-06
f32, bf16 = jnp.float32, jnp.bfloat16
VM = pl.BlockSpec(memory_space=pltpu.VMEM)
shape = jax.ShapeDtypeStruct


def call(kernel, outs, *args, scratch=()):
    return pl.pallas_call(
        kernel,
        out_shape=outs,
        in_specs=[VM] * len(args),
        out_specs=jax.tree.map(lambda _: VM, outs),
        scratch_shapes=list(scratch),
        compiler_params=pltpu.CompilerParams(vmem_limit_bytes=20 * 1024 * 1024),
    )(*args)


def fold(x):
    return jnp.sum(x.reshape(-1, 8, x.shape[-1]), 0)


def prepare_kernel(embeddings, prototypes, rows, inverse, proto, turned):
    for v in range(2):
        e = embeddings[v].astype(f32)
        inv = lax.rsqrt(jnp.sum(e * e, -1, keepdims=True) + EPS)
        inverse[v] = inv
        unit = (e * inv).astype(bf16)
        for i in range(NX):
            rows[i, v] = unit
    turned[...] = prototypes[...].astype(f32).T
    j = lax.axis_index("x") * NC + lax.axis_index("c")
    own = turned[pl.ds(pl.multiple_of(j * SUB, SUB), SUB), :]
    own = (own * lax.rsqrt(jnp.sum(own * own, -1, keepdims=True) + EPS)).astype(bf16)
    for i in range(NZ):
        proto[i] = own


def send_columns(acc, out):
    rows = [jnp.sum(acc[i * 128 : (i + 1) * 128, :].T, 0, keepdims=True) for i in range(2 * Q)]
    part = jnp.concatenate(rows, 0)
    out[...] = jnp.concatenate([part] * (NY * NZ), 0).astype(out.dtype)


def groups(step, mine, other):
    for half, rows in enumerate((mine, other)):

        def member(x, _):
            step(half, x, rows)
            return 0

        lax.fori_loop(0, NX, member, 0)


def place(half, x):
    return lax.rem(lax.axis_index("c") + half, NC) * NX + x


def scores_kernel(mine, other, proto, powered, masses, soft, columns, acc):
    acc[...] = jnp.zeros_like(acc)

    def group(half, x, rows):
        g = place(half, x)
        for v in range(2):
            rowsum = jnp.zeros((8, U), f32)
            for q in range(Q):
                at = slice(q * 128, (q + 1) * 128)
                s = lax.dot_general(
                    proto[at, :], rows[x, v], (((1,), (1,)), ((), ())), preferred_element_type=f32
                )
                e = jnp.exp(s * (1.0 / SHARP))
                k = e * e
                powered[g, v, at, :] = e.astype(bf16)
                masses[g, v, at, :] = k
                rowsum += fold(e)
                i = v * Q + q
                acc[i * 128 : (i + 1) * 128, :] += k[:, :128] + k[:, 128:]
            soft[pl.ds(v * G + g, 1), :] = jnp.sum(rowsum, 0, keepdims=True)

    groups(group, mine, other)
    send_columns(acc, columns)


def rows_kernel(masses, columns, *refs):
    soft, (out, scale, wide) = (refs[0], refs[1:]) if len(refs) == 4 else (None, refs)
    c = 1.0 / (K * fold(columns[...].astype(f32)))
    scale[...] = c
    turned = jnp.concatenate([c] * 16, 0).T
    for i in range(2 * Q):
        wide[i * 128 : (i + 1) * 128, :] = jnp.broadcast_to(turned[:, i : i + 1], (128, 128))
    lines = []
    for v in range(2):

        def eight(s, acc):
            at = pl.multiple_of(s * 8, 8)
            cc = wide[pl.ds(v * COLS + at, 8), :]
            cc = jnp.concatenate([cc, cc], 1)
            return tuple(acc[g] + masses[g, v, pl.ds(at, 8), :] * cc for g in range(G))

        acc = lax.fori_loop(0, COLS // 8, eight, (jnp.zeros((8, U), f32),) * G, unroll=4)
        lines += [jnp.sum(a, 0, keepdims=True) for a in acc]
    if soft is not None:
        lines.append(soft[...])
    out[0] = jnp.concatenate(lines, 0).astype(bf16)
    for i in range(1, G):
        out[i] = out[0]


def row_total(ref, first, n):
    return jnp.sum(ref[:, first : first + n, :].astype(f32), 0)


def columns_kernel(masses, rowmass, columns, acc):
    r = 1.0 / (USERS * row_total(rowmass, 0, 2 * G))
    for v in range(2):
        scale = [jnp.broadcast_to(r[v * G + g : v * G + g + 1, :], (8, U)) for g in range(G)]

        def eight(s, _):
            at = pl.multiple_of(s * 8, 8)
            total = masses[0, v, pl.ds(at, 8), :] * scale[0]
            for g in range(1, G):
                total += masses[g, v, pl.ds(at, 8), :] * scale[g]
            acc[pl.ds(v * COLS + at, 8), :] = total[:, :128] + total[:, 128:]
            return 0

        lax.fori_loop(0, COLS // 8, eight, 0, unroll=4)
    send_columns(acc, columns)


def slopes_kernel(
    mine, other, proto, powered, masses, scale, first, last, keep, give, parts, acc, wide, ab, slopes
):
    acc[...] = jnp.zeros_like(acc)
    turned = jnp.concatenate([scale[...] * (1.0 / SHARP)] * 16, 0).T
    for i in range(2 * Q):
        wide[i * 128 : (i + 1) * 128, :] = jnp.broadcast_to(turned[:, i : i + 1], (128, 128))
    ab[0 : 2 * G, :] = (1.0 / SHARP) / row_total(first, 2 * G, 2 * G)
    ab[2 * G :, :] = 1.0 / row_total(last, 0, 2 * G)
    flat = proto[...].astype(f32).T.astype(bf16)
    own = lax.axis_index("x")

    def group(half, x, rows):
        g = place(half, x)
        far = x ^ own
        slot = (far >> 1) + 2 * (far & 1)
        for v in range(2):
            w = 1 - v
            a = ab[pl.ds(v * G + g, 1), :]
            b = ab[pl.ds(2 * G + w * G + g, 1), :]
            for q in range(Q):
                at = slice(q * 128, (q + 1) * 128)
                c = wide[(w * Q + q) * 128 : (w * Q + q + 1) * 128, :]
                slopes[v, at, :] = (
                    powered[g, v, at, :].astype(f32) * a
                    - masses[g, w, at, :] * jnp.concatenate([c, c], 1) * b
                ).astype(bf16)
            slope = slopes[v]
            made = jnp.dot(flat, slope, preferred_element_type=f32)
            (give if half else keep)[slot, v] = made.astype(bf16)
            acc[...] += jnp.dot(slope, rows[x, v], preferred_element_type=f32)

    groups(group, mine, other)
    parts[...] = acc[...].astype(bf16)


def finish_kernel(embeddings, inverse, kept, got, proto, grad_embed, grad_proto):
    for v in range(2):
        grad = (kept[v].astype(f32) + got[v].astype(f32)).T
        inv = inverse[v]
        unit = embeddings[v].astype(f32) * inv
        grad_embed[v] = inv * (grad - unit * jnp.sum(unit * grad, -1, keepdims=True))
    whole = proto[...].astype(f32).reshape(NY, G, 8, 128)
    whole = jnp.concatenate([whole[:, j].reshape(NY * 8, 128) for j in range(G)], 0)
    grad_proto[...] = whole.T


def swap(x, axis, n, bit):
    return lax.ppermute(x, axis, [(i, i ^ bit) for i in range(n)])


def plus(a, b):
    return (a.astype(f32) + b.astype(f32)).astype(bf16)


def body(embeddings, prototypes):
    kept = lambda dtype: shape((G, 2, COLS, U), dtype)
    sums = shape((NY * NZ * 8, 128), bf16)
    acc = pltpu.VMEM((2 * COLS, 128), f32)

    rows, inverse, proto = call(
        prepare_kernel,
        (shape((NX, 2, U, 128), bf16), shape((2, U, 1), f32), shape((NZ, SUB, 128), bf16)),
        embeddings,
        prototypes,
        scratch=[pltpu.VMEM((512, 128), f32)],
    )
    mine = lax.all_to_all(rows, "x", 0, 0)
    other = swap(mine, "c", NC, 1)
    proto = lax.all_to_all(proto, "z", 0, 0).reshape(COLS, 128)
    powered, masses, soft, columns = call(
        scores_kernel,
        (kept(bf16), kept(f32), shape((2 * G, U), f32), sums),
        mine,
        other,
        proto,
        scratch=[acc],
    )
    first = None
    for sweep in range(ITERS):
        columns = lax.all_to_all(columns, ("y", "z"), 0, 0, tiled=True)
        more = (soft,) if sweep == 0 else ()
        mass, scale = call(
            rows_kernel,
            (shape((G, 4 * G if more else 2 * G, U), bf16), shape((8, 128), f32)),
            masses,
            columns,
            *more,
            scratch=[acc],
        )
        mass = lax.all_to_all(mass, ("x", "c"), 0, 0)
        first = mass if first is None else first
        if sweep < ITERS - 1:
            columns = call(columns_kernel, sums, masses, mass, scratch=[acc])
    half = shape((NX, 2, 128, U), bf16)
    keep, give, parts = call(
        slopes_kernel,
        (half, half, shape((COLS, 128), bf16)),
        mine,
        other,
        proto,
        powered,
        masses,
        scale,
        first,
        mass,
        scratch=[
            pltpu.VMEM((COLS, 128), f32),
            acc,
            pltpu.VMEM((4 * G, U), f32),
            pltpu.VMEM((2, COLS, U), bf16),
        ],
    )
    unit = plus(keep, swap(give, "c", NC, 1))
    near = swap(unit[2:], "x", NX, 1)
    pieces = parts.reshape(NZ, NY, SUB // NY, 128).transpose(1, 0, 2, 3)
    pieces = pieces.reshape(NY * NZ, SUB // NY, 128)
    pieces = lax.all_to_all(pieces, ("y", "z"), 0, 0)
    unit = plus(unit[:2], near)
    far = swap(unit[1], "x", NX, 2)
    piece = jnp.sum(pieces.astype(f32), 0).astype(bf16)
    everyone = jnp.broadcast_to(piece[None], (NY * G, SUB // NY, 128))
    whole = lax.all_to_all(everyone, ("y", "x", "c"), 0, 0).reshape(COLS, 128)
    return tuple(
        call(
            finish_kernel,
            (shape((2, U, 128), f32), shape((128, COLS), f32)),
            embeddings,
            inverse,
            unit[0],
            far,
            whole,
        )
    )


def solution(mesh):
    fine = Mesh(mesh.devices.reshape(NY, NX, NC, NZ), ("y", "x", "c", "z"))
    placed = (P(None, ("y", "x", "c", "z"), None), P(None, "z"))
    return jax.shard_map(
        body, mesh=fine, in_specs=placed, out_specs=placed, check_vma=False
    )
```

time: 193 us -> 174 us (0.902)
  between operations: 14.1 us -> 0.78 us
  starting transfers between devices: 13.4 us -> 23.8 us
  other arithmetic: 8.09 us -> 0.27 us
  blocking collectives: 129 us -> 122 us
  Pallas kernels: 19.9 us -> 15.8 us
    pallas_call x4 -> x0, Pallas kernels: 12.8 us -> none  [with_acc(): pl.pallas_call(kernel, out_shape=outs, in_specs=[VM] * len(args), out_spe...]
    ppermute x1 -> x4, starting transfers between devices: 8.52 us -> 17.4 us  [swap(): return lax.ppermute(x, axis, [(i, i ^ bit) for i in range(n)])]
    pallas_call x3 -> x9, Pallas kernels: 7.02 us -> 15.8 us  [call(): pl.pallas_call(kernel, out_shape=outs, in_specs=[VM] * len(args), out_spe...]
    all_to_all x3, blocking collectives: 47.3 us -> 43 us  [the longest x1 16.1 us: body(): proto = lax.all_to_all(proto, 'z', 0, 0).reshape(COLS, 128)]
    mul x1 -> x0, other arithmetic: 4.19 us -> none  [body(): unit_rows * jnp.sum(unit_rows * grad_unit, -1, keepdims=True)]
    all_to_all x3, blocking collectives: 30.7 us -> 28.4 us  [body(): mass = lax.all_to_all(mass, ('x', 'c'), 0, 0)]
  transfers between devices with their start and end apart: 3 -> 5, of which waited for: 1 -> 2; matrix products, arithmetic and copies ran while one was open for 1% -> 0% of each run, Pallas kernels for 0% -> 0%
where the time goes in v3:
time: 174 us; the launch traced here: 173 us
  blocking collectives  122 us (70%)
  starting transfers between devices  23.8 us (14%)
  Pallas kernels  15.8 us (9%)
  waiting for transfers between devices  7.72 us (4%)
  local copies, waits for them, and re-layouts  2.55 us (1%)
    all_to_all x3, blocking collectives, body(): columns = lax.all_to_all(columns, ('y', 'z'), 0, 0, tiled=True)  50.6 us
    all_to_all x3, blocking collectives, body(): mass = lax.all_to_all(mass, ('x', 'c'), 0, 0)  28.4 us
    ppermute x4, starting transfers between devices, swap(): return lax.ppermute(x, axis, [(i, i ^ bit) for i in range(n)])  17.4 us
    all_to_all x1, blocking collectives, body(): proto = lax.all_to_all(proto, 'z', 0, 0).reshape(COLS, 128)  16.1 us
    pallas_call x9, Pallas kernels, call(): pl.pallas_call(kernel, out_shape=outs, in_specs=[VM] * len(args), out_spe...  15.8 us
    all_to_all x1, blocking collectives, body(): pieces = lax.all_to_all(pieces, ('y', 'z'), 0, 0)  15.4 us
    all_to_all x1, blocking collectives, body(): mine = lax.all_to_all(rows, 'x', 0, 0)  11.6 us
    all_to_all x1, starting transfers between devices, body(): whole = lax.all_to_all(everyone, ('y', 'x', 'c'), 0, 0).reshape(COLS, 128)  6.44 us
  transfers between devices with their start and end apart: 5, of which 2 were waited for; matrix products, arithmetic and copies ran while one was open for 0% of the time, Pallas kernels for 0%

profile of v3, /device:TPU:1, one launch (start us, length us, event | category | flops | bytes accessed | tf_op | source)
XLA Modules:
  0.0 173.0 jit_solution(348851559436940877)
XLA Ops:
  2.7 11.6 %all_to_all.68.mine = bf16[4,2,256,128]{3,2,1,0:T(8,128)(2,1)S(1)} all-to-all(bf16[4,2,256,128]{3,2,1,0:T(8,128)(2,1)S(1)} %get-tuple-element.17), channel_id=1, replica_groups=mesh['y'=8,'x'=4,'c'=2,'z'=8] {'x'}, dimensions={0} | all-to-all | bytes 1048576 | tf_op jit(solution)/shard_map/all_to_all | solution.py:217
  14.2 7.7 %collective-permute-start = (bf16[4,2,256,128]{3,2,1,0:T(8,128)(2,1)S(1)}, bf16[4,2,256,128]{3,2,1,0:T(8,128)(2,1)S(1)}, u32[]{:S(2)}, u32[]{:S(2)}) collective-permute-start(bf16[4,2,256,128]{3,2,1,0:T(8,128)(2,1)S(1)} %all_to_all.68.mine), channel_id=1, source_target_pairs={{0,8},{8,0},{1,9},{9,1},{2,10},{10,2},{3,11},{11,3},{4,12},{12,4},... | collective-permute-start | bytes 1572872 | tf_op jit(solution)/shard_map/ppermute | solution.py:198
  21.9 16.1 %all_to_all.69 = bf16[8,64,128]{2,1,0:T(8,128)(2,1)S(1)} all-to-all(bf16[8,64,128]{2,1,0:T(8,128)(2,1)S(1)} %get-tuple-element.18), channel_id=1, replica_groups=mesh['y'=8,'x'=4,'c'=2,'z'=8] {'z'}, dimensions={0} | all-to-all | bytes 262144 | tf_op jit(solution)/shard_map/all_to_all | solution.py:219
  38.0 3.5 %shard_map.42 = (bf16[8,2,512,256]{3,2,1,0:T(8,128)(2,1)S(1)}, f32[8,2,512,256]{3,2,1,0:T(8,128)S(1)}, f32[16,256]{1,0:T(8,128)S(1)}, bf16[512,128]{1,0:T(8,128)(2,1)S(1)}) custom-call(bf16[4,2,256,128]{3,2,1,0:T(8,128)(2,1)S(1)} %all_to_all.68.mine, bf16[4,2,256,128]{3,2,1,0:T(8,128)(2,1)S(1)} %collective-permute-done.other, bf16[512,128]{1,0:T(8,128)(2,1)S(1)} %bitcast.16), custom_call_target="tpu_custom_call" | custom-call | tf_op jit(solution)/shard_map/pallas_call | solution.py:29
  41.5 19.8 %all_to_all.70 = bf16[64,8,128]{2,1,0:T(8,128)(2,1)S(1)} all-to-all(bf16[64,8,128]{2,1,0:T(8,128)(2,1)S(1)} %bitcast.25), channel_id=1, replica_groups=mesh['y'=8,'x'=4,'c'=2,'z'=8] {'y','z'}, dimensions={0} | all-to-all | bytes 262144 | tf_op jit(solution)/shard_map/all_to_all | solution.py:230
  61.4 1.8 %shard_map.43 = (bf16[8,32,256]{2,1,0:T(8,128)(2,1)S(1)}, f32[8,128]{1,0:T(8,128)}) custom-call(f32[8,2,512,256]{3,2,1,0:T(8,128)S(1)} %get-tuple-element.20.masses, bf16[512,128]{1,0:T(8,128)(2,1)S(1)} %bitcast.18, f32[16,256]{1,0:T(8,128)S(1)} %get-tuple-element.22.refs_0_), custom_call_target="tpu_custom_call" | custom-call | tf_op jit(solution)/shard_map/pallas_call | solution.py:29
  63.2 9.8 %all_to_all.71.rowmass.first = bf16[8,32,256]{2,1,0:T(8,128)(2,1)S(1)} all-to-all(bf16[8,32,256]{2,1,0:T(8,128)(2,1)S(1)} %get-tuple-element.23), channel_id=1, replica_groups=mesh['y'=8,'x'=4,'c'=2,'z'=8] {'x','c'}, dimensions={0} | all-to-all | bytes 262144 | tf_op jit(solution)/shard_map/all_to_all | solution.py:240
  73.0 1.1 shard_map.44
  74.1 15.4 %all_to_all.72 = bf16[64,8,128]{2,1,0:T(8,128)(2,1)S(1)} all-to-all(bf16[64,8,128]{2,1,0:T(8,128)(2,1)S(1)} %bitcast.22), channel_id=1, replica_groups=mesh['y'=8,'x'=4,'c'=2,'z'=8] {'y','z'}, dimensions={0} | all-to-all | bytes 262144 | tf_op jit(solution)/shard_map/all_to_all | solution.py:230
  89.5 1.8 %shard_map.45 = (bf16[8,16,256]{2,1,0:T(8,128)(2,1)S(1)}, f32[8,128]{1,0:T(8,128)}) custom-call(f32[8,2,512,256]{3,2,1,0:T(8,128)S(1)} %get-tuple-element.20.masses, bf16[512,128]{1,0:T(8,128)(2,1)S(1)} %bitcast.19), custom_call_target="tpu_custom_call" | custom-call | tf_op jit(solution)/shard_map/pallas_call | solution.py:29
  91.3 9.3 %all_to_all.73.rowmass = bf16[8,16,256]{2,1,0:T(8,128)(2,1)S(1)} all-to-all(bf16[8,16,256]{2,1,0:T(8,128)(2,1)S(1)} %get-tuple-element.24), channel_id=1, replica_groups=mesh['y'=8,'x'=4,'c'=2,'z'=8] {'x','c'}, dimensions={0} | all-to-all | bytes 131072 | tf_op jit(solution)/shard_map/all_to_all | solution.py:240
  100.6 1.1 shard_map.46
  101.7 15.4 %all_to_all.74 = bf16[64,8,128]{2,1,0:T(8,128)(2,1)S(1)} all-to-all(bf16[64,8,128]{2,1,0:T(8,128)(2,1)S(1)} %bitcast.21), channel_id=1, replica_groups=mesh['y'=8,'x'=4,'c'=2,'z'=8] {'y','z'}, dimensions={0} | all-to-all | bytes 262144 | tf_op jit(solution)/shard_map/all_to_all | solution.py:230
  117.1 1.2 shard_map.47
  118.3 9.3 %all_to_all.75.last = bf16[8,16,256]{2,1,0:T(8,128)(2,1)S(1)} all-to-all(bf16[8,16,256]{2,1,0:T(8,128)(2,1)S(1)} %get-tuple-element.26), channel_id=1, replica_groups=mesh['y'=8,'x'=4,'c'=2,'z'=8] {'x','c'}, dimensions={0} | all-to-all | bytes 131072 | tf_op jit(solution)/shard_map/all_to_all | solution.py:240
  127.6 3.8 %shard_map.48 = (bf16[4,2,128,256]{3,2,1,0:T(8,128)(2,1)S(1)}, bf16[4,2,128,256]{3,2,1,0:T(8,128)(2,1)S(1)}, bf16[512,128]{1,0:T(8,128)(2,1)S(1)}) custom-call(bf16[4,2,256,128]{3,2,1,0:T(8,128)(2,1)S(1)} %all_to_all.68.mine, bf16[4,2,256,128]{3,2,1,0:T(8,128)(2,1)S(1)} %collective-permute-done.other, bf16[512,128]{1,0:T(8,128)(2,1)S(1)} %bitcast.17, ...), custom_call_target="tpu_custom_call" | custom-call | tf_op jit(solution)/shard_map/pallas_call | solution.py:29
  131.4 2.7 %collective-permute-start.1 = (bf16[4,2,128,256]{3,2,1,0:T(8,128)(2,1)S(1)}, bf16[4,2,128,256]{3,2,1,0:T(8,128)(2,1)S(1)}, u32[]{:S(2)}, u32[]{:S(2)}) collective-permute-start(bf16[4,2,128,256]{3,2,1,0:T(8,128)(2,1)S(1)} %get-tuple-element.28), channel_id=1, source_target_pairs={{0,8},{8,0},{1,9},{9,1},{2,10},{10,2},{3,11},{11,3},{4,12},{12,4},... | collective-permute-start | bytes 1572872 | tf_op jit(solution)/shard_map/ppermute | solution.py:198
  134.1 1.5 collective-permute-done.1
  135.8 2.2 %collective-permute-start.2 = (bf16[2,2,128,256]{3,2,1,0:T(8,128)(2,1)S(1)}, bf16[2,2,128,256]{3,2,1,0:T(8,128)(2,1)S(1)}, u32[]{:S(2)}, u32[]{:S(2)}) collective-permute-start(bf16[2,2,128,256]{3,2,1,0:T(8,128)(2,1)S(1)} %slice.17), channel_id=1, source_target_pairs={{0,16},{16,0},{32,48},{48,32},{1,17},{17,1},{33,49},{49,33},{2,18}... | collective-permute-start | bytes 786440 | tf_op jit(solution)/shard_map/ppermute | solution.py:198
  138.0 15.4 %all_to_all.76 = bf16[64,8,128]{2,1,0:T(8,128)(2,1)S(1)} all-to-all(bf16[64,8,128]{2,1,0:T(8,128)(2,1)S(1)} %bitcast.26), channel_id=1, replica_groups=mesh['y'=8,'x'=4,'c'=2,'z'=8] {'y','z'}, dimensions={0} | all-to-all | bytes 262144 | tf_op jit(solution)/shard_map/all_to_all | solution.py:267
  154.2 6.4 %all-to-all-start.9 = ((bf16[64,8,128]{2,1,0:T(8,128)(2,1)}), bf16[64,8,128]{2,1,0:T(8,128)(2,1)S(1)}, u32[]{:S(2)}, u32[]{:S(2)}) async-start(bf16[64,8,128]{2,1,0:T(8,128)(2,1)} %broadcast_in_dim.2), calls=%async_computation.9 | async-start | bytes 262144 | tf_op jit(solution)/shard_map/all_to_all | solution.py:272
  160.7 4.8 %collective-permute-start.3 = (bf16[2,128,256]{2,1,0:T(8,128)(2,1)S(1)}, bf16[2,128,256]{2,1,0:T(8,128)(2,1)S(1)}, u32[]{:S(2)}, u32[]{:S(2)}) collective-permute-start(bf16[2,128,256]{2,1,0:T(8,128)(2,1)S(1)} %get-tuple-element.30), channel_id=1, source_target_pairs={{0,32},{16,48},{32,0},{48,16},{1,33},{17,49},{33,1},{49,17},{2,34}... | collective-permute-start | bytes 393224 | tf_op jit(solution)/shard_map/ppermute | solution.py:198
  165.5 6.2 %all-to-all-done.9 = bf16[64,8,128]{2,1,0:T(8,128)(2,1)S(1)} async-done(((bf16[64,8,128]{2,1,0:T(8,128)(2,1)}), bf16[64,8,128]{2,1,0:T(8,128)(2,1)S(1)}, u32[]{:S(2)}, u32[]{:S(2)}) %all-to-all-start.9) | async-done | bytes 131104 | tf_op jit(solution)/shard_map/all_to_all | solution.py:272
  171.7 1.3 shard_map.49
  (17 shorter events, 3.0 us)
Async XLA Ops:
  0.6 0.9 copy-start
  1.5 0.9 copy-start.2
  14.2 23.8 %collective-permute-start = (bf16[4,2,256,128]{3,2,1,0:T(8,128)(2,1)S(1)}, bf16[4,2,256,128]{3,2,1,0:T(8,128)(2,1)S(1)}, u32[]{:S(2)}, u32[]{:S(2)}) collective-permute-start(bf16[4,2,256,128]{3,2,1,0:T(8,128)(2,1)S(1)} %all_to_all.68.mine), channel_id=1, source_target_pairs={{0,8},{8,0},{1,9},{9,1},{2,10},{10,2},{3,11},{11,3},{4,12},{12,4},... | collective-permute-start | bytes 1572872 | tf_op jit(solution)/shard_map/ppermute | solution.py:198
  127.6 44.1 %copy-start.1 = (bf16[2,256,128]{2,1,0:T(8,128)(2,1)S(1)}, bf16[2,256,128]{2,1,0:T(8,128)(2,1)}, u32[]{:S(2)}) copy-start(bf16[2,256,128]{2,1,0:T(8,128)(2,1)} %embeddings.3) | copy-start | bytes 393220
  131.4 4.2 %collective-permute-start.1 = (bf16[4,2,128,256]{3,2,1,0:T(8,128)(2,1)S(1)}, bf16[4,2,128,256]{3,2,1,0:T(8,128)(2,1)S(1)}, u32[]{:S(2)}, u32[]{:S(2)}) collective-permute-start(bf16[4,2,128,256]{3,2,1,0:T(8,128)(2,1)S(1)} %get-tuple-element.28), channel_id=1, source_target_pairs={{0,8},{8,0},{1,9},{9,1},{2,10},{10,2},{3,11},{11,3},{4,12},{12,4},... | collective-permute-start | bytes 1572872 | tf_op jit(solution)/shard_map/ppermute | solution.py:198
  135.8 24.8 %collective-permute-start.2 = (bf16[2,2,128,256]{3,2,1,0:T(8,128)(2,1)S(1)}, bf16[2,2,128,256]{3,2,1,0:T(8,128)(2,1)S(1)}, u32[]{:S(2)}, u32[]{:S(2)}) collective-permute-start(bf16[2,2,128,256]{3,2,1,0:T(8,128)(2,1)S(1)} %slice.17), channel_id=1, source_target_pairs={{0,16},{16,0},{32,48},{48,32},{1,17},{17,1},{33,49},{49,33},{2,18}... | collective-permute-start | bytes 786440 | tf_op jit(solution)/shard_map/ppermute | solution.py:198
  154.2 17.6 %all-to-all-start.9 = ((bf16[64,8,128]{2,1,0:T(8,128)(2,1)}), bf16[64,8,128]{2,1,0:T(8,128)(2,1)S(1)}, u32[]{:S(2)}, u32[]{:S(2)}) async-start(bf16[64,8,128]{2,1,0:T(8,128)(2,1)} %broadcast_in_dim.2), calls=%async_computation.9 | async-start | bytes 262144 | tf_op jit(solution)/shard_map/all_to_all | solution.py:272
  160.7 11.0 %collective-permute-start.3 = (bf16[2,128,256]{2,1,0:T(8,128)(2,1)S(1)}, bf16[2,128,256]{2,1,0:T(8,128)(2,1)S(1)}, u32[]{:S(2)}, u32[]{:S(2)}) collective-permute-start(bf16[2,128,256]{2,1,0:T(8,128)(2,1)S(1)} %get-tuple-element.30), channel_id=1, source_target_pairs={{0,32},{16,48},{32,0},{48,16},{1,33},{17,49},{33,1},{49,17},{2,34}... | collective-permute-start | bytes 393224 | tf_op jit(solution)/shard_map/ppermute | solution.py:198

commit v4 on v3

--- a/solution.py
+++ b/solution.py
@@ -25,13 +25,15 @@
 shape = jax.ShapeDtypeStruct
 
 
-def call(kernel, outs, *args, scratch=()):
+def call(kernel, outs, *args, scratch=(), flops=0):
+    cost = pl.CostEstimate(flops=flops, bytes_accessed=1 << 20, transcendentals=0) if flops else None
     return pl.pallas_call(
         kernel,
         out_shape=outs,
         in_specs=[VM] * len(args),
         out_specs=jax.tree.map(lambda _: VM, outs),
         scratch_shapes=list(scratch),
+        cost_estimate=cost,
         compiler_params=pltpu.CompilerParams(vmem_limit_bytes=20 * 1024 * 1024),
     )(*args)
 
@@ -40,14 +42,15 @@
     return jnp.sum(x.reshape(-1, 8, x.shape[-1]), 0)
 
 
-def prepare_kernel(embeddings, prototypes, rows, inverse, proto, turned):
+def users_kernel(embeddings, unit, inverse):
     for v in range(2):
         e = embeddings[v].astype(f32)
         inv = lax.rsqrt(jnp.sum(e * e, -1, keepdims=True) + EPS)
         inverse[v] = inv
-        unit = (e * inv).astype(bf16)
-        for i in range(NX):
-            rows[i, v] = unit
+        unit[v] = (e * inv).astype(bf16)
+
+
+def proto_kernel(prototypes, proto, turned):
     turned[...] = prototypes[...].astype(f32).T
     j = lax.axis_index("x") * NC + lax.axis_index("c")
     own = turned[pl.ds(pl.multiple_of(j * SUB, SUB), SUB), :]
@@ -65,15 +68,15 @@
 def groups(step, mine, other):
     for half, rows in enumerate((mine, other)):
 
-        def member(x, _):
-            step(half, x, rows)
+        def member(r, _):
+            step(half, r, rows)
             return 0
 
         lax.fori_loop(0, NX, member, 0)
 
 
-def place(half, x):
-    return lax.rem(lax.axis_index("c") + half, NC) * NX + x
+def place(half, r):
+    return lax.rem(lax.axis_index("c") + half, NC) * NX + (lax.axis_index("x") ^ r)
 
 
 def scores_kernel(mine, other, proto, powered, masses, soft, columns, acc):
@@ -101,10 +104,12 @@
     send_columns(acc, columns)
 
 
-def rows_kernel(masses, columns, *refs):
-    soft, (out, scale, wide) = (refs[0], refs[1:]) if len(refs) == 4 else (None, refs)
+def rows_kernel(sweep, masses, columns, *refs):
+    soft = refs[0] if sweep == 0 else None
+    out, wide = refs[-2 if sweep < ITERS - 1 else -3], refs[-1]
     c = 1.0 / (K * fold(columns[...].astype(f32)))
-    scale[...] = c
+    if sweep == ITERS - 1:
+        refs[-2][...] = c
     turned = jnp.concatenate([c] * 16, 0).T
     for i in range(2 * Q):
         wide[i * 128 : (i + 1) * 128, :] = jnp.broadcast_to(turned[:, i : i + 1], (128, 128))
@@ -148,7 +153,7 @@
 
 
 def slopes_kernel(
-    mine, other, proto, powered, masses, scale, first, last, keep, give, parts, acc, wide, ab, slopes
+    mine, other, powered, masses, scale, first, last, slopes, parts, acc, wide, ab
 ):
     acc[...] = jnp.zeros_like(acc)
     turned = jnp.concatenate([scale[...] * (1.0 / SHARP)] * 16, 0).T
@@ -156,13 +161,9 @@
         wide[i * 128 : (i + 1) * 128, :] = jnp.broadcast_to(turned[:, i : i + 1], (128, 128))
     ab[0 : 2 * G, :] = (1.0 / SHARP) / row_total(first, 2 * G, 2 * G)
     ab[2 * G :, :] = 1.0 / row_total(last, 0, 2 * G)
-    flat = proto[...].astype(f32).T.astype(bf16)
-    own = lax.axis_index("x")
-
-    def group(half, x, rows):
-        g = place(half, x)
-        far = x ^ own
-        slot = (far >> 1) + 2 * (far & 1)
+
+    def group(half, r, rows):
+        g = place(half, r)
         for v in range(2):
             w = 1 - v
             a = ab[pl.ds(v * G + g, 1), :]
@@ -170,17 +171,34 @@
             for q in range(Q):
                 at = slice(q * 128, (q + 1) * 128)
                 c = wide[(w * Q + q) * 128 : (w * Q + q + 1) * 128, :]
-                slopes[v, at, :] = (
+                slopes[half * NX + r, v, at, :] = (
                     powered[g, v, at, :].astype(f32) * a
                     - masses[g, w, at, :] * jnp.concatenate([c, c], 1) * b
                 ).astype(bf16)
-            slope = slopes[v]
-            made = jnp.dot(flat, slope, preferred_element_type=f32)
-            (give if half else keep)[slot, v] = made.astype(bf16)
-            acc[...] += jnp.dot(slope, rows[x, v], preferred_element_type=f32)
+            acc[...] += jnp.dot(slopes[half * NX + r, v], rows[r, v], preferred_element_type=f32)
 
     groups(group, mine, other)
     parts[...] = acc[...].astype(bf16)
+
+
+def flat_kernel(proto, flat):
+    flat[...] = proto[...].astype(f32).T.astype(bf16)
+
+
+def units_kernel(flat, slopes, keep, give):
+
+    def group(half, r, out):
+        slot = lax.div(r, 2) + 2 * lax.rem(r, 2)
+        for v in range(2):
+            made = jnp.dot(flat[...], slopes[half * NX + r, v], preferred_element_type=f32)
+            out[slot, v] = made.astype(bf16)
+
+    groups(group, keep, give)
+
+
+def piece_kernel(pieces, out):
+    piece = fold(pieces[...].astype(f32))
+    out[...] = jnp.concatenate([piece] * (NY * G), 0).astype(bf16)
 
 
 def finish_kernel(embeddings, inverse, kept, got, proto, grad_embed, grad_proto):
@@ -207,16 +225,18 @@
     sums = shape((NY * NZ * 8, 128), bf16)
     acc = pltpu.VMEM((2 * COLS, 128), f32)
 
-    rows, inverse, proto = call(
-        prepare_kernel,
-        (shape((NX, 2, U, 128), bf16), shape((2, U, 1), f32), shape((NZ, SUB, 128), bf16)),
-        embeddings,
-        prototypes,
-        scratch=[pltpu.VMEM((512, 128), f32)],
-    )
-    mine = lax.all_to_all(rows, "x", 0, 0)
+    proto = call(
+        proto_kernel, shape((NZ, SUB, 128), bf16), prototypes, scratch=[pltpu.VMEM((512, 128), f32)]
+    )
+    proto = lax.all_to_all(proto, "z", 0, 0).reshape(COLS, 128)
+    unit, inverse = call(
+        users_kernel, (shape((2, U, 128), bf16), shape((2, U, 1), f32)), embeddings, flops=1 << 31
+    )
+    flat = call(flat_kernel, shape((128, COLS), bf16), proto, flops=1 << 36)
+    others = [swap(unit, "x", NX, r) for r in (1, 2, 3)]
+    others, flat = lax.optimization_barrier((others, flat))
+    mine = jnp.stack([unit] + others)
     other = swap(mine, "c", NC, 1)
-    proto = lax.all_to_all(proto, "z", 0, 0).reshape(COLS, 128)
     powered, masses, soft, columns = call(
         scores_kernel,
         (kept(bf16), kept(f32), shape((2 * G, U), f32), sums),
@@ -228,48 +248,43 @@
     first = None
     for sweep in range(ITERS):
         columns = lax.all_to_all(columns, ("y", "z"), 0, 0, tiled=True)
-        more = (soft,) if sweep == 0 else ()
-        mass, scale = call(
-            rows_kernel,
-            (shape((G, 4 * G if more else 2 * G, U), bf16), shape((8, 128), f32)),
+        lines = shape((G, 4 * G if sweep == 0 else 2 * G, U), bf16)
+        mass = call(
+            functools.partial(rows_kernel, sweep),
+            (lines, shape((8, 128), f32)) if sweep == ITERS - 1 else lines,
             masses,
             columns,
-            *more,
+            *((soft,) if sweep == 0 else ()),
             scratch=[acc],
         )
+        if sweep == ITERS - 1:
+            mass, scale = mass
         mass = lax.all_to_all(mass, ("x", "c"), 0, 0)
         first = mass if first is None else first
         if sweep < ITERS - 1:
             columns = call(columns_kernel, sums, masses, mass, scratch=[acc])
-    half = shape((NX, 2, 128, U), bf16)
-    keep, give, parts = call(
+    slopes, parts = call(
         slopes_kernel,
-        (half, half, shape((COLS, 128), bf16)),
+        (kept(bf16), shape((COLS, 128), bf16)),
         mine,
         other,
-        proto,
         powered,
         masses,
         scale,
         first,
         mass,
-        scratch=[
-            pltpu.VMEM((COLS, 128), f32),
-            acc,
-            pltpu.VMEM((4 * G, U), f32),
-            pltpu.VMEM((2, COLS, U), bf16),
-        ],
-    )
+        scratch=[pltpu.VMEM((COLS, 128), f32), acc, pltpu.VMEM((4 * G, U), f32)],
+    )
+    pieces = parts.reshape(NZ, NY, SUB // NY, 128).transpose(1, 0, 2, 3)
+    pieces = lax.all_to_all(pieces.reshape(NY * NZ * 8, 128), ("y", "z"), 0, 0, tiled=True)
+    half = shape((NX, 2, 128, U), bf16)
+    keep, give = call(units_kernel, (half, half), flat, slopes, flops=1 << 31)
     unit = plus(keep, swap(give, "c", NC, 1))
     near = swap(unit[2:], "x", NX, 1)
-    pieces = parts.reshape(NZ, NY, SUB // NY, 128).transpose(1, 0, 2, 3)
-    pieces = pieces.reshape(NY * NZ, SUB // NY, 128)
-    pieces = lax.all_to_all(pieces, ("y", "z"), 0, 0)
+    pieces = call(piece_kernel, shape((NY * G * 8, 128), bf16), pieces, flops=1 << 36)
+    whole = lax.all_to_all(pieces, ("y", "x", "c"), 0, 0, tiled=True)
     unit = plus(unit[:2], near)
     far = swap(unit[1], "x", NX, 2)
-    piece = jnp.sum(pieces.astype(f32), 0).astype(bf16)
-    everyone = jnp.broadcast_to(piece[None], (NY * G, SUB // NY, 128))
-    whole = lax.all_to_all(everyone, ("y", "x", "c"), 0, 0).reshape(COLS, 128)
     return tuple(
         call(
             finish_kernel,

time: 174 us -> 173 us (level)
  blocking collectives: 122 us -> 85.1 us
  starting transfers between devices: 23.8 us -> 44.3 us
  waiting for transfers between devices: 7.72 us -> 21.2 us
  Pallas kernels: 15.8 us -> 17.7 us
    all_to_all x3 -> x0, blocking collectives: 43 us -> none  [the longest x1 16.1 us: body(): proto = lax.all_to_all(proto, 'z', 0, 0).reshape(COLS, 128)]
    all_to_all x1 -> x3, starting transfers between devices: 6.44 us -> 21.3 us  [the longest x1 10.9 us: body(): proto = lax.all_to_all(proto, 'z', 0, 0).reshape(COLS, 128)]
    all_to_all x1 -> x3, waiting for transfers between devices: 6.2 us -> 16 us  [the longest x1 9.56 us: body(): lax.all_to_all(pieces.reshape(NY * NZ * 8, 128), ('y', 'z'), 0, 0, tiled=...]
    ppermute x4 -> x7, starting transfers between devices: 17.4 us -> 23 us  [swap(): return lax.ppermute(x, axis, [(i, i ^ bit) for i in range(n)])]
    all_to_all x3, blocking collectives: 50.6 us -> 55.3 us  [body(): columns = lax.all_to_all(columns, ('y', 'z'), 0, 0, tiled=True)]
    ppermute x4 -> x7, waiting for transfers between devices: 1.52 us -> 5.23 us  [swap(): return lax.ppermute(x, axis, [(i, i ^ bit) for i in range(n)])]
    pallas_call x9 -> x13, Pallas kernels: 15.8 us -> 17.7 us  [call(): pl.pallas_call(kernel, out_shape=outs, in_specs=[VM] * len(args), out_spe...]
  transfers between devices with their start and end apart: 5 -> 10, of which waited for: 2 -> 5; matrix products, arithmetic and copies ran while one was open for 0% -> 1% of each run, Pallas kernels for 0% -> 1%
where the time goes in v4:
time: 173 us; the launch traced here: 172 us
  blocking collectives  85.1 us (49%)
  starting transfers between devices  44.3 us (26%)
  waiting for transfers between devices  21.2 us (12%)
  Pallas kernels  17.7 us (10%)
  local copies, waits for them, and re-layouts  2.52 us (1%)
    all_to_all x3, blocking collectives, body(): columns = lax.all_to_all(columns, ('y', 'z'), 0, 0, tiled=True)  55.3 us
    all_to_all x3, blocking collectives, body(): mass = lax.all_to_all(mass, ('x', 'c'), 0, 0)  29.8 us
    ppermute x7, starting transfers between devices, swap(): return lax.ppermute(x, axis, [(i, i ^ bit) for i in range(n)])  23 us
    pallas_call x13, Pallas kernels, call(): pl.pallas_call(kernel, out_shape=outs, in_specs=[VM] * len(args), out_spe...  17.7 us
    all_to_all x1, starting transfers between devices, body(): proto = lax.all_to_all(proto, 'z', 0, 0).reshape(COLS, 128)  10.9 us
    all_to_all x1, waiting for transfers between devices, body(): lax.all_to_all(pieces.reshape(NY * NZ * 8, 128), ('y', 'z'), 0, 0, tiled=...  9.56 us
    all_to_all x1, waiting for transfers between devices, body(): whole = lax.all_to_all(pieces, ('y', 'x', 'c'), 0, 0, tiled=True)  6.41 us
    all_to_all x1, starting transfers between devices, body(): whole = lax.all_to_all(pieces, ('y', 'x', 'c'), 0, 0, tiled=True)  5.82 us
  transfers between devices with their start and end apart: 10, of which 5 were waited for; matrix products, arithmetic and copies ran while one was open for 1% of the time, Pallas kernels for 1%

profile of v4, /device:TPU:1, one launch (start us, length us, event | category | flops | bytes accessed | tf_op | source)
XLA Modules:
  0.0 171.9 jit_solution(18215619713045143113)
XLA Ops:
  2.4 10.9 %all-to-all-start = ((bf16[8,64,128]{2,1,0:T(8,128)(2,1)}), bf16[8,64,128]{2,1,0:T(8,128)(2,1)S(1)}, u32[]{:S(2)}, u32[]{:S(2)}) async-start(bf16[8,64,128]{2,1,0:T(8,128)(2,1)} %shard_map.42), calls=%async_computation | async-start | bytes 262144 | tf_op jit(solution)/shard_map/all_to_all | solution.py:231
  14.3 4.4 %collective-permute-start.2 = (bf16[2,256,128]{2,1,0:T(8,128)(2,1)S(1)}, bf16[2,256,128]{2,1,0:T(8,128)(2,1)S(1)}, u32[]{:S(2)}, u32[]{:S(2)}) collective-permute-start(bf16[2,256,128]{2,1,0:T(8,128)(2,1)S(1)} %get-tuple-element.19), channel_id=1, source_target_pairs={{0,48},{16,32},{32,16},{48,0},{1,49},{17,33},{33,17},{49,1},{2,50}... | collective-permute-start | bytes 393224 | tf_op jit(solution)/shard_map/ppermute | solution.py:216
  18.7 2.4 %collective-permute-start.1 = (bf16[2,256,128]{2,1,0:T(8,128)(2,1)S(1)}, bf16[2,256,128]{2,1,0:T(8,128)(2,1)S(1)}, u32[]{:S(2)}, u32[]{:S(2)}) collective-permute-start(bf16[2,256,128]{2,1,0:T(8,128)(2,1)S(1)} %get-tuple-element.19), channel_id=1, source_target_pairs={{0,32},{16,48},{32,0},{48,16},{1,33},{17,49},{33,1},{49,17},{2,34}... | collective-permute-start | bytes 393224 | tf_op jit(solution)/shard_map/ppermute | solution.py:216
  21.1 2.2 %collective-permute-start = (bf16[2,256,128]{2,1,0:T(8,128)(2,1)S(1)}, bf16[2,256,128]{2,1,0:T(8,128)(2,1)S(1)}, u32[]{:S(2)}, u32[]{:S(2)}) collective-permute-start(bf16[2,256,128]{2,1,0:T(8,128)(2,1)S(1)} %get-tuple-element.19), channel_id=1, source_target_pairs={{0,16},{16,0},{32,48},{48,32},{1,17},{17,1},{33,49},{49,33},{2,18}... | collective-permute-start | bytes 393224 | tf_op jit(solution)/shard_map/ppermute | solution.py:216
  23.5 2.5 %collective-permute-done.1 = bf16[2,256,128]{2,1,0:T(8,128)(2,1)S(1)} collective-permute-done((bf16[2,256,128]{2,1,0:T(8,128)(2,1)S(1)}, bf16[2,256,128]{2,1,0:T(8,128)(2,1)S(1)}, u32[]{:S(2)}, u32[]{:S(2)}) %collective-permute-start.1) | collective-permute-done | bytes 131104 | tf_op jit(solution)/shard_map/ppermute | solution.py:216
  27.2 4.3 %collective-permute-start.3 = (bf16[4,2,256,128]{3,2,1,0:T(8,128)(2,1)S(1)}, bf16[4,2,256,128]{3,2,1,0:T(8,128)(2,1)S(1)}, u32[]{:S(2)}, u32[]{:S(2)}) collective-permute-start(bf16[4,2,256,128]{3,2,1,0:T(8,128)(2,1)S(1)} %pad_maximum_fusion.mine), channel_id=1, source_target_pairs={{0,8},{8,0},{1,9},{9,1},{2,10},{10,2},{3,11},{11,3},{4,12},{12,4},... | collective-permute-start | bytes 1572872 | tf_op jit(solution)/shard_map/ppermute | solution.py:216
  31.5 1.5 collective-permute-done.3.other
  33.0 3.5 %shard_map.44 = (bf16[8,2,512,256]{3,2,1,0:T(8,128)(2,1)S(1)}, f32[8,2,512,256]{3,2,1,0:T(8,128)S(1)}, f32[16,256]{1,0:T(8,128)S(1)}, bf16[512,128]{1,0:T(8,128)(2,1)S(1)}) custom-call(bf16[4,2,256,128]{3,2,1,0:T(8,128)(2,1)S(1)} %pad_maximum_fusion.mine, bf16[4,2,256,128]{3,2,1,0:T(8,128)(2,1)S(1)} %collective-permute-done.3.other, ...), custom_call_target="tpu_custom_call" | custom-call | tf_op jit(solution)/shard_map/pallas_call | solution.py:30
  36.6 24.5 %all_to_all.75 = bf16[64,8,128]{2,1,0:T(8,128)(2,1)S(1)} all-to-all(bf16[64,8,128]{2,1,0:T(8,128)(2,1)S(1)} %bitcast.32), channel_id=1, replica_groups=mesh['y'=8,'x'=4,'c'=2,'z'=8] {'y','z'}, dimensions={0} | all-to-all | bytes 262144 | tf_op jit(solution)/shard_map/all_to_all | solution.py:250
  62.3 11.1 %all_to_all.76.rowmass.first = bf16[8,32,256]{2,1,0:T(8,128)(2,1)S(1)} all-to-all(bf16[8,32,256]{2,1,0:T(8,128)(2,1)S(1)} %shard_map.45), channel_id=1, replica_groups=mesh['y'=8,'x'=4,'c'=2,'z'=8] {'x','c'}, dimensions={0} | all-to-all | bytes 262144 | tf_op jit(solution)/shard_map/all_to_all | solution.py:262
  74.5 15.4 %all_to_all.77 = bf16[64,8,128]{2,1,0:T(8,128)(2,1)S(1)} all-to-all(bf16[64,8,128]{2,1,0:T(8,128)(2,1)S(1)} %bitcast.26), channel_id=1, replica_groups=mesh['y'=8,'x'=4,'c'=2,'z'=8] {'y','z'}, dimensions={0} | all-to-all | bytes 262144 | tf_op jit(solution)/shard_map/all_to_all | solution.py:250
  91.2 9.3 %all_to_all.78.rowmass = bf16[8,16,256]{2,1,0:T(8,128)(2,1)S(1)} all-to-all(bf16[8,16,256]{2,1,0:T(8,128)(2,1)S(1)} %shard_map.47), channel_id=1, replica_groups=mesh['y'=8,'x'=4,'c'=2,'z'=8] {'x','c'}, dimensions={0} | all-to-all | bytes 131072 | tf_op jit(solution)/shard_map/all_to_all | solution.py:262
  101.6 15.4 %all_to_all.79 = bf16[64,8,128]{2,1,0:T(8,128)(2,1)S(1)} all-to-all(bf16[64,8,128]{2,1,0:T(8,128)(2,1)S(1)} %bitcast.25), channel_id=1, replica_groups=mesh['y'=8,'x'=4,'c'=2,'z'=8] {'y','z'}, dimensions={0} | all-to-all | bytes 262144 | tf_op jit(solution)/shard_map/all_to_all | solution.py:250
  118.2 9.3 %all_to_all.80.last = bf16[8,16,256]{2,1,0:T(8,128)(2,1)S(1)} all-to-all(bf16[8,16,256]{2,1,0:T(8,128)(2,1)S(1)} %get-tuple-element.29), channel_id=1, replica_groups=mesh['y'=8,'x'=4,'c'=2,'z'=8] {'x','c'}, dimensions={0} | all-to-all | bytes 131072 | tf_op jit(solution)/shard_map/all_to_all | solution.py:262
  127.5 3.4 %shard_map.50 = (bf16[8,2,512,256]{3,2,1,0:T(8,128)(2,1)S(1)}, bf16[512,128]{1,0:T(8,128)(2,1)S(1)}) custom-call(bf16[4,2,256,128]{3,2,1,0:T(8,128)(2,1)S(1)} %pad_maximum_fusion.mine, bf16[4,2,256,128]{3,2,1,0:T(8,128)(2,1)S(1)} %collective-permute-done.3.other, bf16[8,2,512,256]{3,2,1,0:T(8,128)(2,1)S(1)} %get-tuple-element.24.powered, ...), custom_call_target="tpu_custom_call" | custom-call | tf_op jit(solution)/shard_map/pallas_call | solution.py:30
  130.9 1.9 %shard_map.51 = (bf16[4,2,128,256]{3,2,1,0:T(8,128)(2,1)S(1)}, bf16[4,2,128,256]{3,2,1,0:T(8,128)(2,1)S(1)}) custom-call(bf16[128,512]{1,0:T(8,128)(2,1)S(1)} %shard_map.43.flat, bf16[8,2,512,256]{3,2,1,0:T(8,128)(2,1)S(1)} %get-tuple-element.30.slopes), custom_call_target="tpu_custom_call" | custom-call | flops 2147483648 | bytes 1048576 | tf_op jit(solution)/shard_map/pallas_call | solution.py:30
  132.8 2.7 %collective-permute-start.4 = (bf16[4,2,128,256]{3,2,1,0:T(8,128)(2,1)S(1)}, bf16[4,2,128,256]{3,2,1,0:T(8,128)(2,1)S(1)}, u32[]{:S(2)}, u32[]{:S(2)}) collective-permute-start(bf16[4,2,128,256]{3,2,1,0:T(8,128)(2,1)S(1)} %get-tuple-element.32), channel_id=1, source_target_pairs={{0,8},{8,0},{1,9},{9,1},{2,10},{10,2},{3,11},{11,3},{4,12},{12,4},... | collective-permute-start | bytes 1572872 | tf_op jit(solution)/shard_map/ppermute | solution.py:216
  136.2 4.6 %all-to-all-start.7 = ((bf16[64,8,128]{2,1,0:T(8,128)(2,1)}), bf16[64,8,128]{2,1,0:T(8,128)(2,1)S(1)}, u32[]{:S(2)}, u32[]{:S(2)}) async-start(bf16[64,8,128]{2,1,0:T(8,128)(2,1)} %bitcast.15), calls=%async_computation.7 | async-start | bytes 262144 | tf_op jit(solution)/shard_map/all_to_all | solution.py:279
  141.0 2.2 %collective-permute-start.5 = (bf16[2,2,128,256]{3,2,1,0:T(8,128)(2,1)S(1)}, bf16[2,2,128,256]{3,2,1,0:T(8,128)(2,1)S(1)}, u32[]{:S(2)}, u32[]{:S(2)}) collective-permute-start(bf16[2,2,128,256]{3,2,1,0:T(8,128)(2,1)S(1)} %slice.17), channel_id=1, source_target_pairs={{0,16},{16,0},{32,48},{48,32},{1,17},{17,1},{33,49},{49,33},{2,18}... | collective-permute-start | bytes 786440 | tf_op jit(solution)/shard_map/ppermute | solution.py:216
  143.2 9.6 %all-to-all-done.7 = bf16[64,8,128]{2,1,0:T(8,128)(2,1)S(1)} async-done(((bf16[64,8,128]{2,1,0:T(8,128)(2,1)}), bf16[64,8,128]{2,1,0:T(8,128)(2,1)S(1)}, u32[]{:S(2)}, u32[]{:S(2)}) %all-to-all-start.7) | async-done | bytes 131104 | tf_op jit(solution)/shard_map/all_to_all | solution.py:279
  153.5 5.8 %all-to-all-start.8 = ((bf16[64,8,128]{2,1,0:T(8,128)(2,1)}), bf16[64,8,128]{2,1,0:T(8,128)(2,1)S(1)}, u32[]{:S(2)}, u32[]{:S(2)}) async-start(bf16[64,8,128]{2,1,0:T(8,128)(2,1)} %bitcast.17), calls=%async_computation.8 | async-start | bytes 262144 | tf_op jit(solution)/shard_map/all_to_all | solution.py:285
  159.4 4.8 %collective-permute-start.6 = (bf16[2,128,256]{2,1,0:T(8,128)(2,1)S(1)}, bf16[2,128,256]{2,1,0:T(8,128)(2,1)S(1)}, u32[]{:S(2)}, u32[]{:S(2)}) collective-permute-start(bf16[2,128,256]{2,1,0:T(8,128)(2,1)S(1)} %get-tuple-element.34), channel_id=1, source_target_pairs={{0,32},{16,48},{32,0},{48,16},{1,33},{17,49},{33,1},{49,17},{2,34}... | collective-permute-start | bytes 393224 | tf_op jit(solution)/shard_map/ppermute | solution.py:216
  164.2 6.4 %all-to-all-done.8 = bf16[64,8,128]{2,1,0:T(8,128)(2,1)S(1)} async-done(((bf16[64,8,128]{2,1,0:T(8,128)(2,1)}), bf16[64,8,128]{2,1,0:T(8,128)(2,1)S(1)}, u32[]{:S(2)}, u32[]{:S(2)}) %all-to-all-start.8) | async-done | bytes 131104 | tf_op jit(solution)/shard_map/all_to_all | solution.py:285
  170.7 1.3 shard_map.53
  (27 shorter events, 11.7 us)
Async XLA Ops:
  0.6 0.9 copy-start
  2.4 20.9 %all-to-all-start = ((bf16[8,64,128]{2,1,0:T(8,128)(2,1)}), bf16[8,64,128]{2,1,0:T(8,128)(2,1)S(1)}, u32[]{:S(2)}, u32[]{:S(2)}) async-start(bf16[8,64,128]{2,1,0:T(8,128)(2,1)} %shard_map.42), calls=%async_computation | async-start | bytes 262144 | tf_op jit(solution)/shard_map/all_to_all | solution.py:231
  13.3 0.9 copy-start.1
  14.3 9.1 %collective-permute-start.2 = (bf16[2,256,128]{2,1,0:T(8,128)(2,1)S(1)}, bf16[2,256,128]{2,1,0:T(8,128)(2,1)S(1)}, u32[]{:S(2)}, u32[]{:S(2)}) collective-permute-start(bf16[2,256,128]{2,1,0:T(8,128)(2,1)S(1)} %get-tuple-element.19), channel_id=1, source_target_pairs={{0,48},{16,32},{32,16},{48,0},{1,49},{17,33},{33,17},{49,1},{2,50}... | collective-permute-start | bytes 393224 | tf_op jit(solution)/shard_map/ppermute | solution.py:216
  18.7 7.2 %collective-permute-start.1 = (bf16[2,256,128]{2,1,0:T(8,128)(2,1)S(1)}, bf16[2,256,128]{2,1,0:T(8,128)(2,1)S(1)}, u32[]{:S(2)}, u32[]{:S(2)}) collective-permute-start(bf16[2,256,128]{2,1,0:T(8,128)(2,1)S(1)} %get-tuple-element.19), channel_id=1, source_target_pairs={{0,32},{16,48},{32,0},{48,16},{1,33},{17,49},{33,1},{49,17},{2,34}... | collective-permute-start | bytes 393224 | tf_op jit(solution)/shard_map/ppermute | solution.py:216
  21.1 6.0 %collective-permute-start = (bf16[2,256,128]{2,1,0:T(8,128)(2,1)S(1)}, bf16[2,256,128]{2,1,0:T(8,128)(2,1)S(1)}, u32[]{:S(2)}, u32[]{:S(2)}) collective-permute-start(bf16[2,256,128]{2,1,0:T(8,128)(2,1)S(1)} %get-tuple-element.19), channel_id=1, source_target_pairs={{0,16},{16,0},{32,48},{48,32},{1,17},{17,1},{33,49},{49,33},{2,18}... | collective-permute-start | bytes 393224 | tf_op jit(solution)/shard_map/ppermute | solution.py:216
  27.2 5.8 %collective-permute-start.3 = (bf16[4,2,256,128]{3,2,1,0:T(8,128)(2,1)S(1)}, bf16[4,2,256,128]{3,2,1,0:T(8,128)(2,1)S(1)}, u32[]{:S(2)}, u32[]{:S(2)}) collective-permute-start(bf16[4,2,256,128]{3,2,1,0:T(8,128)(2,1)S(1)} %pad_maximum_fusion.mine), channel_id=1, source_target_pairs={{0,8},{8,0},{1,9},{9,1},{2,10},{10,2},{3,11},{11,3},{4,12},{12,4},... | collective-permute-start | bytes 1572872 | tf_op jit(solution)/shard_map/ppermute | solution.py:216
  132.8 8.0 %collective-permute-start.4 = (bf16[4,2,128,256]{3,2,1,0:T(8,128)(2,1)S(1)}, bf16[4,2,128,256]{3,2,1,0:T(8,128)(2,1)S(1)}, u32[]{:S(2)}, u32[]{:S(2)}) collective-permute-start(bf16[4,2,128,256]{3,2,1,0:T(8,128)(2,1)S(1)} %get-tuple-element.32), channel_id=1, source_target_pairs={{0,8},{8,0},{1,9},{9,1},{2,10},{10,2},{3,11},{11,3},{4,12},{12,4},... | collective-permute-start | bytes 1572872 | tf_op jit(solution)/shard_map/ppermute | solution.py:216
  136.2 16.6 %all-to-all-start.7 = ((bf16[64,8,128]{2,1,0:T(8,128)(2,1)}), bf16[64,8,128]{2,1,0:T(8,128)(2,1)S(1)}, u32[]{:S(2)}, u32[]{:S(2)}) async-start(bf16[64,8,128]{2,1,0:T(8,128)(2,1)} %bitcast.15), calls=%async_computation.7 | async-start | bytes 262144 | tf_op jit(solution)/shard_map/all_to_all | solution.py:279
  141.0 18.3 %collective-permute-start.5 = (bf16[2,2,128,256]{3,2,1,0:T(8,128)(2,1)S(1)}, bf16[2,2,128,256]{3,2,1,0:T(8,128)(2,1)S(1)}, u32[]{:S(2)}, u32[]{:S(2)}) collective-permute-start(bf16[2,2,128,256]{3,2,1,0:T(8,128)(2,1)S(1)} %slice.17), channel_id=1, source_target_pairs={{0,16},{16,0},{32,48},{48,32},{1,17},{17,1},{33,49},{49,33},{2,18}... | collective-permute-start | bytes 786440 | tf_op jit(solution)/shard_map/ppermute | solution.py:216
  152.7 17.9 %copy-start.2 = (bf16[2,256,128]{2,1,0:T(8,128)(2,1)S(1)}, bf16[2,256,128]{2,1,0:T(8,128)(2,1)}, u32[]{:S(2)}) copy-start(bf16[2,256,128]{2,1,0:T(8,128)(2,1)} %embeddings.3) | copy-start | bytes 393220
  153.5 17.2 %all-to-all-start.8 = ((bf16[64,8,128]{2,1,0:T(8,128)(2,1)}), bf16[64,8,128]{2,1,0:T(8,128)(2,1)S(1)}, u32[]{:S(2)}, u32[]{:S(2)}) async-start(bf16[64,8,128]{2,1,0:T(8,128)(2,1)} %bitcast.17), calls=%async_computation.8 | async-start | bytes 262144 | tf_op jit(solution)/shard_map/all_to_all | solution.py:285
  159.4 11.2 %collective-permute-start.6 = (bf16[2,128,256]{2,1,0:T(8,128)(2,1)S(1)}, bf16[2,128,256]{2,1,0:T(8,128)(2,1)S(1)}, u32[]{:S(2)}, u32[]{:S(2)}) collective-permute-start(bf16[2,128,256]{2,1,0:T(8,128)(2,1)S(1)} %get-tuple-element.34), channel_id=1, source_target_pairs={{0,32},{16,48},{32,0},{48,16},{1,33},{17,49},{33,1},{49,17},{2,34}... | collective-permute-start | bytes 393224 | tf_op jit(solution)/shard_map/ppermute | solution.py:216

commit v5 on v3

--- a/solution.py
+++ b/solution.py
@@ -25,13 +25,15 @@
 shape = jax.ShapeDtypeStruct
 
 
-def call(kernel, outs, *args, scratch=()):
+def call(kernel, outs, *args, scratch=(), flops=0):
+    cost = pl.CostEstimate(flops=flops, bytes_accessed=1 << 20, transcendentals=0) if flops else None
     return pl.pallas_call(
         kernel,
         out_shape=outs,
         in_specs=[VM] * len(args),
         out_specs=jax.tree.map(lambda _: VM, outs),
         scratch_shapes=list(scratch),
+        cost_estimate=cost,
         compiler_params=pltpu.CompilerParams(vmem_limit_bytes=20 * 1024 * 1024),
     )(*args)
 
@@ -40,15 +42,23 @@
     return jnp.sum(x.reshape(-1, 8, x.shape[-1]), 0)
 
 
-def prepare_kernel(embeddings, prototypes, rows, inverse, proto, turned):
-    for v in range(2):
-        e = embeddings[v].astype(f32)
+def prepare_kernel(embeddings, prototypes, rows, inverse, proto, users, columns, turned, sems):
+    fetch = [
+        pltpu.make_async_copy(src, dst, sems.at[i])
+        for i, (src, dst) in enumerate(((embeddings, users), (prototypes, columns)))
+    ]
+    for copy in fetch:
+        copy.start()
+    fetch[0].wait()
+    for v in range(2):
+        e = users[v].astype(f32)
         inv = lax.rsqrt(jnp.sum(e * e, -1, keepdims=True) + EPS)
         inverse[v] = inv
         unit = (e * inv).astype(bf16)
         for i in range(NX):
             rows[i, v] = unit
-    turned[...] = prototypes[...].astype(f32).T
+    fetch[1].wait()
+    turned[...] = columns[...].astype(f32).T
     j = lax.axis_index("x") * NC + lax.axis_index("c")
     own = turned[pl.ds(pl.multiple_of(j * SUB, SUB), SUB), :]
     own = (own * lax.rsqrt(jnp.sum(own * own, -1, keepdims=True) + EPS)).astype(bf16)
@@ -101,10 +111,12 @@
     send_columns(acc, columns)
 
 
-def rows_kernel(masses, columns, *refs):
-    soft, (out, scale, wide) = (refs[0], refs[1:]) if len(refs) == 4 else (None, refs)
+def rows_kernel(sweep, masses, columns, *refs):
+    soft = refs[0] if sweep == 0 else None
+    out, wide = refs[-2 if sweep < ITERS - 1 else -3], refs[-1]
     c = 1.0 / (K * fold(columns[...].astype(f32)))
-    scale[...] = c
+    if sweep == ITERS - 1:
+        refs[-2][...] = c
     turned = jnp.concatenate([c] * 16, 0).T
     for i in range(2 * Q):
         wide[i * 128 : (i + 1) * 128, :] = jnp.broadcast_to(turned[:, i : i + 1], (128, 128))
@@ -147,8 +159,27 @@
     send_columns(acc, columns)
 
 
+def flat_kernel(proto, flat):
+    flat[...] = proto[...].astype(f32).T.astype(bf16)
+
+
 def slopes_kernel(
-    mine, other, proto, powered, masses, scale, first, last, keep, give, parts, acc, wide, ab, slopes
+    mine,
+    other,
+    flat,
+    powered,
+    masses,
+    scale,
+    first,
+    last,
+    keep,
+    give0,
+    give1,
+    parts,
+    acc,
+    wide,
+    ab,
+    slopes,
 ):
     acc[...] = jnp.zeros_like(acc)
     turned = jnp.concatenate([scale[...] * (1.0 / SHARP)] * 16, 0).T
@@ -156,13 +187,11 @@
         wide[i * 128 : (i + 1) * 128, :] = jnp.broadcast_to(turned[:, i : i + 1], (128, 128))
     ab[0 : 2 * G, :] = (1.0 / SHARP) / row_total(first, 2 * G, 2 * G)
     ab[2 * G :, :] = 1.0 / row_total(last, 0, 2 * G)
-    flat = proto[...].astype(f32).T.astype(bf16)
-    own = lax.axis_index("x")
 
     def group(half, x, rows):
         g = place(half, x)
-        far = x ^ own
-        slot = (far >> 1) + 2 * (far & 1)
+        far = x ^ lax.axis_index("x")
+        slot = lax.div(far, 2) + 2 * lax.rem(far, 2)
         for v in range(2):
             w = 1 - v
             a = ab[pl.ds(v * G + g, 1), :]
@@ -174,32 +203,51 @@
                     powered[g, v, at, :].astype(f32) * a
                     - masses[g, w, at, :] * jnp.concatenate([c, c], 1) * b
                 ).astype(bf16)
-            slope = slopes[v]
-            made = jnp.dot(flat, slope, preferred_element_type=f32)
-            (give if half else keep)[slot, v] = made.astype(bf16)
-            acc[...] += jnp.dot(slope, rows[x, v], preferred_element_type=f32)
+            made = jnp.dot(flat[...], slopes[v], preferred_element_type=f32)
+            if half:
+                (give0, give1)[v][slot] = made.astype(bf16)
+            else:
+                keep[v, slot] = made.astype(bf16)
+            acc[...] += jnp.dot(slopes[v], rows[x, v], preferred_element_type=f32)
 
     groups(group, mine, other)
-    parts[...] = acc[...].astype(bf16)
+    for y in range(NY):
+        for z in range(NZ):
+            at = z * SUB + y * 8
+            parts[(y * NZ + z) * 8 : (y * NZ + z + 1) * 8, :] = acc[at : at + 8, :]
+
+
+def piece_kernel(pieces, out):
+    out[...] = jnp.concatenate([fold(pieces[...])] * (NY * NX), 0).astype(bf16)
+
+
+def cores_kernel(keep, got0, got1, stay, near):
+    for v, got in enumerate((got0, got1)):
+        for i in range(2):
+            stay[v, i] = (keep[v, i].astype(f32) + got[i].astype(f32)).astype(bf16)
+            near[v, i] = (keep[v, 2 + i].astype(f32) + got[2 + i].astype(f32)).astype(bf16)
+
+
+def near_kernel(stay, got, unit, far):
+    for v in range(2):
+        unit[v] = stay[v, 0].astype(f32) + got[v, 0].astype(f32)
+        far[v] = (stay[v, 1].astype(f32) + got[v, 1].astype(f32)).astype(bf16)
 
 
 def finish_kernel(embeddings, inverse, kept, got, proto, grad_embed, grad_proto):
     for v in range(2):
-        grad = (kept[v].astype(f32) + got[v].astype(f32)).T
+        grad = (kept[v] + got[v].astype(f32)).T
         inv = inverse[v]
         unit = embeddings[v].astype(f32) * inv
         grad_embed[v] = inv * (grad - unit * jnp.sum(unit * grad, -1, keepdims=True))
-    whole = proto[...].astype(f32).reshape(NY, G, 8, 128)
-    whole = jnp.concatenate([whole[:, j].reshape(NY * 8, 128) for j in range(G)], 0)
-    grad_proto[...] = whole.T
+    for x in range(NX):
+        blocks = [proto[c].astype(f32).reshape(NY, NX, 8, 128)[:, x] for c in range(NC)]
+        whole = jnp.concatenate([b.reshape(SUB, 128) for b in blocks], 0)
+        grad_proto[:, x * NC * SUB : (x + 1) * NC * SUB] = whole.T
 
 
 def swap(x, axis, n, bit):
     return lax.ppermute(x, axis, [(i, i ^ bit) for i in range(n)])
-
-
-def plus(a, b):
-    return (a.astype(f32) + b.astype(f32)).astype(bf16)
 
 
 def body(embeddings, prototypes):
@@ -207,16 +255,28 @@
     sums = shape((NY * NZ * 8, 128), bf16)
     acc = pltpu.VMEM((2 * COLS, 128), f32)
 
-    rows, inverse, proto = call(
+    rows, inverse, proto = pl.pallas_call(
         prepare_kernel,
-        (shape((NX, 2, U, 128), bf16), shape((2, U, 1), f32), shape((NZ, SUB, 128), bf16)),
-        embeddings,
-        prototypes,
-        scratch=[pltpu.VMEM((512, 128), f32)],
-    )
+        out_shape=(
+            shape((NX, 2, U, 128), bf16),
+            shape((2, U, 1), f32),
+            shape((NZ, SUB, 128), bf16),
+        ),
+        in_specs=[pl.BlockSpec(memory_space=pltpu.HBM)] * 2,
+        out_specs=(VM,) * 3,
+        scratch_shapes=[
+            pltpu.VMEM((2, U, 128), bf16),
+            pltpu.VMEM((128, 512), bf16),
+            pltpu.VMEM((512, 128), f32),
+            pltpu.SemaphoreType.DMA((2,)),
+        ],
+        compiler_params=pltpu.CompilerParams(vmem_limit_bytes=20 * 1024 * 1024),
+    )(*(pltpu.with_memory_space_constraint(a, pltpu.HBM) for a in (embeddings, prototypes)))
     mine = lax.all_to_all(rows, "x", 0, 0)
+    proto = lax.all_to_all(proto, "z", 0, 0).reshape(COLS, 128)
     other = swap(mine, "c", NC, 1)
-    proto = lax.all_to_all(proto, "z", 0, 0).reshape(COLS, 128)
+    flat = call(flat_kernel, shape((128, COLS), bf16), proto, flops=1 << 36)
+    proto, flat = lax.optimization_barrier((proto, flat))
     powered, masses, soft, columns = call(
         scores_kernel,
         (kept(bf16), kept(f32), shape((2 * G, U), f32), sums),
@@ -228,26 +288,28 @@
     first = None
     for sweep in range(ITERS):
         columns = lax.all_to_all(columns, ("y", "z"), 0, 0, tiled=True)
-        more = (soft,) if sweep == 0 else ()
-        mass, scale = call(
-            rows_kernel,
-            (shape((G, 4 * G if more else 2 * G, U), bf16), shape((8, 128), f32)),
+        lines = shape((G, 4 * G if sweep == 0 else 2 * G, U), bf16)
+        mass = call(
+            functools.partial(rows_kernel, sweep),
+            (lines, shape((8, 128), f32)) if sweep == ITERS - 1 else lines,
             masses,
             columns,
-            *more,
+            *((soft,) if sweep == 0 else ()),
             scratch=[acc],
         )
+        if sweep == ITERS - 1:
+            mass, scale = mass
         mass = lax.all_to_all(mass, ("x", "c"), 0, 0)
         first = mass if first is None else first
         if sweep < ITERS - 1:
             columns = call(columns_kernel, sums, masses, mass, scratch=[acc])
-    half = shape((NX, 2, 128, U), bf16)
-    keep, give, parts = call(
+    half, part = shape((2, NX, 128, U), bf16), shape((NX, 128, U), bf16)
+    keep, give0, give1, parts = call(
         slopes_kernel,
-        (half, half, shape((COLS, 128), bf16)),
+        (half, part, part, shape((COLS, 128), f32)),
         mine,
         other,
-        proto,
+        flat,
         powered,
         masses,
         scale,
@@ -260,23 +322,24 @@
             pltpu.VMEM((2, COLS, U), bf16),
         ],
     )
-    unit = plus(keep, swap(give, "c", NC, 1))
-    near = swap(unit[2:], "x", NX, 1)
-    pieces = parts.reshape(NZ, NY, SUB // NY, 128).transpose(1, 0, 2, 3)
-    pieces = pieces.reshape(NY * NZ, SUB // NY, 128)
-    pieces = lax.all_to_all(pieces, ("y", "z"), 0, 0)
-    unit = plus(unit[:2], near)
-    far = swap(unit[1], "x", NX, 2)
-    piece = jnp.sum(pieces.astype(f32), 0).astype(bf16)
-    everyone = jnp.broadcast_to(piece[None], (NY * G, SUB // NY, 128))
-    whole = lax.all_to_all(everyone, ("y", "x", "c"), 0, 0).reshape(COLS, 128)
+    pieces = lax.all_to_all(parts, ("y", "z"), 0, 0, tiled=True)
+    half = shape((2, 2, 128, U), bf16)
+    stay, near = call(cores_kernel, (half, half), keep, *(swap(g, "c", NC, 1) for g in (give0, give1)))
+    near = swap(near, "x", NX, 1)
+    pieces = call(piece_kernel, shape((NY * NX * 8, 128), bf16), pieces, flops=1 << 36)
+    whole = lax.all_to_all(pieces, ("y", "x"), 0, 0, tiled=True)
+    whole = lax.all_gather(whole, "c", axis=0)
+    unit, far = call(
+        near_kernel, (shape((2, 128, U), f32), shape((2, 128, U), bf16)), stay, near
+    )
+    far = swap(far, "x", NX, 2)
     return tuple(
         call(
             finish_kernel,
             (shape((2, U, 128), f32), shape((128, COLS), f32)),
             embeddings,
             inverse,
-            unit[0],
+            unit,
             far,
             whole,
         )

time: 174 us -> 168 us (0.966)
  blocking collectives: 122 us -> 96.8 us
  starting transfers between devices: 23.8 us -> 37.2 us
  waiting for transfers between devices: 7.72 us -> 14.2 us
  local copies, waits for them, and re-layouts: 2.55 us -> 0.01 us
  Pallas kernels: 15.8 us -> 18.1 us
    all_to_all x2 -> x0, blocking collectives: 31.5 us -> none  [the longest x1 16.1 us: body(): proto = lax.all_to_all(proto, 'z', 0, 0).reshape(COLS, 128)]
    all_to_all x1 -> x3, starting transfers between devices: 6.44 us -> 21.7 us  [the longest x1 11.7 us: body(): proto = lax.all_to_all(proto, 'z', 0, 0).reshape(COLS, 128)]
    all_to_all x1 -> x3, waiting for transfers between devices: 6.2 us -> 12.7 us  [the longest x1 4.55 us: body(): pieces = lax.all_to_all(parts, ('y', 'z'), 0, 0, tiled=True)]
    all_gather x0 -> x1, blocking collectives: none -> 4.16 us  [body(): whole = lax.all_gather(whole, 'c', axis=0)]
    all_to_all x3, blocking collectives: 50.6 us -> 52.7 us  [body(): columns = lax.all_to_all(columns, ('y', 'z'), 0, 0, tiled=True)]
    pallas_call x0 -> x1, Pallas kernels: none -> 1.94 us  [body(): pl.pallas_call(prepare_kernel, out_shape=(shape((NX, 2, U, 128), bf16), s...]
    ppermute x4 -> x5, starting transfers between devices: 17.4 us -> 15.5 us  [swap(): return lax.ppermute(x, axis, [(i, i ^ bit) for i in range(n)])]
    unnamed x6 -> x2, local copies, waits for them, and re-layouts: 1.81 us -> 0.01 us
  transfers between devices with their start and end apart: 5 -> 8, of which waited for: 2 -> 4; matrix products, arithmetic and copies ran while one was open for 0% -> 0% of each run, Pallas kernels for 0% -> 1%
where the time goes in v5:
time: 168 us; the launch traced here: 167 us
  blocking collectives  96.8 us (58%)
  starting transfers between devices  37.2 us (22%)
  Pallas kernels  18.1 us (11%)
  waiting for transfers between devices  14.2 us (8%)
    all_to_all x3, blocking collectives, body(): columns = lax.all_to_all(columns, ('y', 'z'), 0, 0, tiled=True)  52.7 us
    all_to_all x3, blocking collectives, body(): mass = lax.all_to_all(mass, ('x', 'c'), 0, 0)  28.4 us
    pallas_call x12, Pallas kernels, call(): pl.pallas_call(kernel, out_shape=outs, in_specs=[VM] * len(args), out_spe...  16.2 us
    ppermute x5, starting transfers between devices, swap(): return lax.ppermute(x, axis, [(i, i ^ bit) for i in range(n)])  15.5 us
    all_to_all x1, starting transfers between devices, body(): proto = lax.all_to_all(proto, 'z', 0, 0).reshape(COLS, 128)  11.7 us
    all_to_all x1, blocking collectives, body(): mine = lax.all_to_all(rows, 'x', 0, 0)  11.6 us
    all_to_all x1, starting transfers between devices, body(): whole = lax.all_to_all(pieces, ('y', 'x'), 0, 0, tiled=True)  5.36 us
    all_to_all x1, starting transfers between devices, body(): pieces = lax.all_to_all(parts, ('y', 'z'), 0, 0, tiled=True)  4.62 us
  transfers between devices with their start and end apart: 8, of which 4 were waited for; matrix products, arithmetic and copies ran while one was open for 0% of the time, Pallas kernels for 1%

profile of v5, /device:TPU:1, one launch (start us, length us, event | category | flops | bytes accessed | tf_op | source)
XLA Modules:
  0.0 167.1 jit_solution(17465747639331004330)
XLA Ops:
  0.6 1.9 %shard_map.41 = (bf16[4,2,256,128]{3,2,1,0:T(8,128)(2,1)S(1)}, f32[2,256,1]{2,1,0:T(8,128)S(1)}, bf16[8,64,128]{2,1,0:T(8,128)(2,1)}) custom-call(bf16[2,256,128]{2,1,0:T(8,128)(2,1)} %embeddings.3, bf16[128,512]{1,0:T(8,128)(2,1)} %prototypes.1), custom_call_target="tpu_custom_call" | custom-call | tf_op jit(solution)/shard_map/pallas_call | solution.py:258
  2.6 11.6 %all_to_all.78.mine = bf16[4,2,256,128]{3,2,1,0:T(8,128)(2,1)S(1)} all-to-all(bf16[4,2,256,128]{3,2,1,0:T(8,128)(2,1)S(1)} %get-tuple-element.22), channel_id=1, replica_groups=mesh['y'=8,'x'=4,'c'=2,'z'=8] {'x'}, dimensions={0} | all-to-all | bytes 1048576 | tf_op jit(solution)/shard_map/all_to_all | solution.py:275
  14.1 11.7 %all-to-all-start.1 = ((bf16[8,64,128]{2,1,0:T(8,128)(2,1)}), bf16[8,64,128]{2,1,0:T(8,128)(2,1)S(1)}, u32[]{:S(2)}, u32[]{:S(2)}) async-start(bf16[8,64,128]{2,1,0:T(8,128)(2,1)} %get-tuple-element.23), calls=%async_computation.1 | async-start | bytes 262144 | tf_op jit(solution)/shard_map/all_to_all | solution.py:276
  25.8 4.0 %collective-permute-start = (bf16[4,2,256,128]{3,2,1,0:T(8,128)(2,1)S(1)}, bf16[4,2,256,128]{3,2,1,0:T(8,128)(2,1)S(1)}, u32[]{:S(2)}, u32[]{:S(2)}) collective-permute-start(bf16[4,2,256,128]{3,2,1,0:T(8,128)(2,1)S(1)} %all_to_all.78.mine), channel_id=1, source_target_pairs={{0,8},{8,0},{1,9},{9,1},{2,10},{10,2},{3,11},{11,3},{4,12},{12,4},... | collective-permute-start | bytes 1572872 | tf_op jit(solution)/shard_map/ppermute | solution.py:250
  29.9 4.0 %all-to-all-done.1 = bf16[8,64,128]{2,1,0:T(8,128)(2,1)S(1)} async-done(((bf16[8,64,128]{2,1,0:T(8,128)(2,1)}), bf16[8,64,128]{2,1,0:T(8,128)(2,1)S(1)}, u32[]{:S(2)}, u32[]{:S(2)}) %all-to-all-start.1) | async-done | bytes 131104 | tf_op jit(solution)/shard_map/all_to_all | solution.py:276
  34.0 3.5 %shard_map.43 = (bf16[8,2,512,256]{3,2,1,0:T(8,128)(2,1)S(1)}, f32[8,2,512,256]{3,2,1,0:T(8,128)S(1)}, f32[16,256]{1,0:T(8,128)S(1)}, bf16[512,128]{1,0:T(8,128)(2,1)S(1)}) custom-call(bf16[4,2,256,128]{3,2,1,0:T(8,128)(2,1)S(1)} %all_to_all.78.mine, bf16[4,2,256,128]{3,2,1,0:T(8,128)(2,1)S(1)} %collective-permute-done.other, bf16[512,128]{1,0:T(8,128)(2,1)S(1)} %bitcast.17), custom_call_target="tpu_custom_call" | custom-call | tf_op jit(solution)/shard_map/pallas_call | solution.py:30
  37.5 21.9 %all_to_all.79 = bf16[64,8,128]{2,1,0:T(8,128)(2,1)S(1)} all-to-all(bf16[64,8,128]{2,1,0:T(8,128)(2,1)S(1)} %bitcast.19), channel_id=1, replica_groups=mesh['y'=8,'x'=4,'c'=2,'z'=8] {'y','z'}, dimensions={0} | all-to-all | bytes 262144 | tf_op jit(solution)/shard_map/all_to_all | solution.py:290
  60.7 9.7 %all_to_all.80.rowmass.first = bf16[8,32,256]{2,1,0:T(8,128)(2,1)S(1)} all-to-all(bf16[8,32,256]{2,1,0:T(8,128)(2,1)S(1)} %shard_map.44), channel_id=1, replica_groups=mesh['y'=8,'x'=4,'c'=2,'z'=8] {'x','c'}, dimensions={0} | all-to-all | bytes 262144 | tf_op jit(solution)/shard_map/all_to_all | solution.py:302
  71.5 15.4 %all_to_all.81 = bf16[64,8,128]{2,1,0:T(8,128)(2,1)S(1)} all-to-all(bf16[64,8,128]{2,1,0:T(8,128)(2,1)S(1)} %bitcast.15), channel_id=1, replica_groups=mesh['y'=8,'x'=4,'c'=2,'z'=8] {'y','z'}, dimensions={0} | all-to-all | bytes 262144 | tf_op jit(solution)/shard_map/all_to_all | solution.py:290
  88.1 9.3 %all_to_all.82.rowmass = bf16[8,16,256]{2,1,0:T(8,128)(2,1)S(1)} all-to-all(bf16[8,16,256]{2,1,0:T(8,128)(2,1)S(1)} %shard_map.46), channel_id=1, replica_groups=mesh['y'=8,'x'=4,'c'=2,'z'=8] {'x','c'}, dimensions={0} | all-to-all | bytes 131072 | tf_op jit(solution)/shard_map/all_to_all | solution.py:302
  98.5 15.4 %all_to_all.83 = bf16[64,8,128]{2,1,0:T(8,128)(2,1)S(1)} all-to-all(bf16[64,8,128]{2,1,0:T(8,128)(2,1)S(1)} %bitcast.14), channel_id=1, replica_groups=mesh['y'=8,'x'=4,'c'=2,'z'=8] {'y','z'}, dimensions={0} | all-to-all | bytes 262144 | tf_op jit(solution)/shard_map/all_to_all | solution.py:290
  115.2 9.3 %all_to_all.84.last = bf16[8,16,256]{2,1,0:T(8,128)(2,1)S(1)} all-to-all(bf16[8,16,256]{2,1,0:T(8,128)(2,1)S(1)} %get-tuple-element.31), channel_id=1, replica_groups=mesh['y'=8,'x'=4,'c'=2,'z'=8] {'x','c'}, dimensions={0} | all-to-all | bytes 131072 | tf_op jit(solution)/shard_map/all_to_all | solution.py:302
  124.5 4.6 %shard_map.49 = (bf16[2,4,128,256]{3,2,1,0:T(8,128)(2,1)S(1)}, bf16[4,128,256]{2,1,0:T(8,128)(2,1)S(1)}, bf16[4,128,256]{2,1,0:T(8,128)(2,1)S(1)}, f32[512,128]{1,0:T(8,128)}) custom-call(bf16[4,2,256,128]{3,2,1,0:T(8,128)(2,1)S(1)} %all_to_all.78.mine, bf16[4,2,256,128]{3,2,1,0:T(8,128)(2,1)S(1)} %collective-permute-done.other, ...), custom_call_target="tpu_custom_call" | custom-call | tf_op jit(solution)/shard_map/pallas_call | solution.py:30
  129.1 4.6 %all-to-all-start.8 = ((f32[64,8,128]{2,1,0:T(8,128)}), f32[64,8,128]{2,1,0:T(8,128)S(1)}, u32[]{:S(2)}, u32[]{:S(2)}) async-start(f32[64,8,128]{2,1,0:T(8,128)} %bitcast.7), calls=%async_computation.8 | async-start | bytes 524288 | tf_op jit(solution)/shard_map/all_to_all | solution.py:325
  133.7 2.7 %collective-permute-start.1 = (bf16[4,128,256]{2,1,0:T(8,128)(2,1)S(1)}, bf16[4,128,256]{2,1,0:T(8,128)(2,1)S(1)}, u32[]{:S(2)}, u32[]{:S(2)}) collective-permute-start(bf16[4,128,256]{2,1,0:T(8,128)(2,1)S(1)} %get-tuple-element.33), channel_id=1, source_target_pairs={{0,8},{8,0},{1,9},{9,1},{2,10},{10,2},{3,11},{11,3},{4,12},{12,4},... | collective-permute-start | bytes 786440 | tf_op jit(solution)/shard_map/ppermute | solution.py:250
  136.4 1.9 %collective-permute-start.2 = (bf16[4,128,256]{2,1,0:T(8,128)(2,1)S(1)}, bf16[4,128,256]{2,1,0:T(8,128)(2,1)S(1)}, u32[]{:S(2)}, u32[]{:S(2)}) collective-permute-start(bf16[4,128,256]{2,1,0:T(8,128)(2,1)S(1)} %get-tuple-element.34), channel_id=1, source_target_pairs={{0,8},{8,0},{1,9},{9,1},{2,10},{10,2},{3,11},{11,3},{4,12},{12,4},... | collective-permute-start | bytes 786440 | tf_op jit(solution)/shard_map/ppermute | solution.py:250
  138.3 1.5 collective-permute-done.2.got1
  139.9 2.2 %collective-permute-start.3 = (bf16[2,2,128,256]{3,2,1,0:T(8,128)(2,1)S(1)}, bf16[2,2,128,256]{3,2,1,0:T(8,128)(2,1)S(1)}, u32[]{:S(2)}, u32[]{:S(2)}) collective-permute-start(bf16[2,2,128,256]{3,2,1,0:T(8,128)(2,1)S(1)} %get-tuple-element.36), channel_id=1, source_target_pairs={{0,16},{16,0},{32,48},{48,32},{1,17},{17,1},{33,49},{49,33},{2,18}... | collective-permute-start | bytes 786440 | tf_op jit(solution)/shard_map/ppermute | solution.py:250
  142.2 4.5 %all-to-all-done.8 = f32[64,8,128]{2,1,0:T(8,128)S(1)} async-done(((f32[64,8,128]{2,1,0:T(8,128)}), f32[64,8,128]{2,1,0:T(8,128)S(1)}, u32[]{:S(2)}, u32[]{:S(2)}) %all-to-all-start.8) | async-done | bytes 262176 | tf_op jit(solution)/shard_map/all_to_all | solution.py:325
  147.4 5.4 %all-to-all-start.9 = ((bf16[32,8,128]{2,1,0:T(8,128)(2,1)}), bf16[32,8,128]{2,1,0:T(8,128)(2,1)S(1)}, u32[]{:S(2)}, u32[]{:S(2)}) async-start(bf16[32,8,128]{2,1,0:T(8,128)(2,1)} %bitcast.9), calls=%async_computation.9 | async-start | bytes 131072 | tf_op jit(solution)/shard_map/all_to_all | solution.py:330
  152.9 4.6 %collective-permute-start.4 = (bf16[2,128,256]{2,1,0:T(8,128)(2,1)S(1)}, bf16[2,128,256]{2,1,0:T(8,128)(2,1)S(1)}, u32[]{:S(2)}, u32[]{:S(2)}) collective-permute-start(bf16[2,128,256]{2,1,0:T(8,128)(2,1)S(1)} %get-tuple-element.38), channel_id=1, source_target_pairs={{0,32},{16,48},{32,0},{48,16},{1,33},{17,49},{33,1},{49,17},{2,34}... | collective-permute-start | bytes 393224 | tf_op jit(solution)/shard_map/ppermute | solution.py:250
  157.5 4.1 %all-to-all-done.9 = bf16[32,8,128]{2,1,0:T(8,128)(2,1)S(1)} async-done(((bf16[32,8,128]{2,1,0:T(8,128)(2,1)}), bf16[32,8,128]{2,1,0:T(8,128)(2,1)S(1)}, u32[]{:S(2)}, u32[]{:S(2)}) %all-to-all-start.9) | async-done | bytes 65568 | tf_op jit(solution)/shard_map/all_to_all | solution.py:330
  161.7 4.2 %all_gather.7.proto = bf16[2,256,128]{2,1,0:T(8,128)(2,1)S(1)} all-gather(bf16[1,256,128]{2,1,0:T(8,128)(2,1)S(1)} %bitcast.20), channel_id=1, replica_groups=mesh['y'=8,'x'=4,'c'=2,'z'=8] {'c'}, dimensions={0}, use_global_device_ids=true | all-gather | bytes 196608 | tf_op jit(solution)/shard_map/all_gather | solution.py:331
  165.8 1.3 shard_map.53
  (15 shorter events, 6.8 us)
Async XLA Ops:
  14.1 19.7 %all-to-all-start.1 = ((bf16[8,64,128]{2,1,0:T(8,128)(2,1)}), bf16[8,64,128]{2,1,0:T(8,128)(2,1)S(1)}, u32[]{:S(2)}, u32[]{:S(2)}) async-start(bf16[8,64,128]{2,1,0:T(8,128)(2,1)} %get-tuple-element.23), calls=%async_computation.1 | async-start | bytes 262144 | tf_op jit(solution)/shard_map/all_to_all | solution.py:276
  25.8 8.1 %collective-permute-start = (bf16[4,2,256,128]{3,2,1,0:T(8,128)(2,1)S(1)}, bf16[4,2,256,128]{3,2,1,0:T(8,128)(2,1)S(1)}, u32[]{:S(2)}, u32[]{:S(2)}) collective-permute-start(bf16[4,2,256,128]{3,2,1,0:T(8,128)(2,1)S(1)} %all_to_all.78.mine), channel_id=1, source_target_pairs={{0,8},{8,0},{1,9},{9,1},{2,10},{10,2},{3,11},{11,3},{4,12},{12,4},... | collective-permute-start | bytes 1572872 | tf_op jit(solution)/shard_map/ppermute | solution.py:250
  129.1 17.6 %all-to-all-start.8 = ((f32[64,8,128]{2,1,0:T(8,128)}), f32[64,8,128]{2,1,0:T(8,128)S(1)}, u32[]{:S(2)}, u32[]{:S(2)}) async-start(f32[64,8,128]{2,1,0:T(8,128)} %bitcast.7), calls=%async_computation.8 | async-start | bytes 524288 | tf_op jit(solution)/shard_map/all_to_all | solution.py:325
  133.7 4.6 %collective-permute-start.1 = (bf16[4,128,256]{2,1,0:T(8,128)(2,1)S(1)}, bf16[4,128,256]{2,1,0:T(8,128)(2,1)S(1)}, u32[]{:S(2)}, u32[]{:S(2)}) collective-permute-start(bf16[4,128,256]{2,1,0:T(8,128)(2,1)S(1)} %get-tuple-element.33), channel_id=1, source_target_pairs={{0,8},{8,0},{1,9},{9,1},{2,10},{10,2},{3,11},{11,3},{4,12},{12,4},... | collective-permute-start | bytes 786440 | tf_op jit(solution)/shard_map/ppermute | solution.py:250
  136.4 3.4 %collective-permute-start.2 = (bf16[4,128,256]{2,1,0:T(8,128)(2,1)S(1)}, bf16[4,128,256]{2,1,0:T(8,128)(2,1)S(1)}, u32[]{:S(2)}, u32[]{:S(2)}) collective-permute-start(bf16[4,128,256]{2,1,0:T(8,128)(2,1)S(1)} %get-tuple-element.34), channel_id=1, source_target_pairs={{0,8},{8,0},{1,9},{9,1},{2,10},{10,2},{3,11},{11,3},{4,12},{12,4},... | collective-permute-start | bytes 786440 | tf_op jit(solution)/shard_map/ppermute | solution.py:250
  139.9 12.8 %collective-permute-start.3 = (bf16[2,2,128,256]{3,2,1,0:T(8,128)(2,1)S(1)}, bf16[2,2,128,256]{3,2,1,0:T(8,128)(2,1)S(1)}, u32[]{:S(2)}, u32[]{:S(2)}) collective-permute-start(bf16[2,2,128,256]{3,2,1,0:T(8,128)(2,1)S(1)} %get-tuple-element.36), channel_id=1, source_target_pairs={{0,16},{16,0},{32,48},{48,32},{1,17},{17,1},{33,49},{49,33},{2,18}... | collective-permute-start | bytes 786440 | tf_op jit(solution)/shard_map/ppermute | solution.py:250
  146.7 19.1 %copy-start = (bf16[2,256,128]{2,1,0:T(8,128)(2,1)S(1)}, bf16[2,256,128]{2,1,0:T(8,128)(2,1)}, u32[]{:S(2)}) copy-start(bf16[2,256,128]{2,1,0:T(8,128)(2,1)} %embeddings.3) | copy-start | bytes 393220
  147.4 14.2 %all-to-all-start.9 = ((bf16[32,8,128]{2,1,0:T(8,128)(2,1)}), bf16[32,8,128]{2,1,0:T(8,128)(2,1)S(1)}, u32[]{:S(2)}, u32[]{:S(2)}) async-start(bf16[32,8,128]{2,1,0:T(8,128)(2,1)} %bitcast.9), calls=%async_computation.9 | async-start | bytes 131072 | tf_op jit(solution)/shard_map/all_to_all | solution.py:330
  152.9 13.0 %collective-permute-start.4 = (bf16[2,128,256]{2,1,0:T(8,128)(2,1)S(1)}, bf16[2,128,256]{2,1,0:T(8,128)(2,1)S(1)}, u32[]{:S(2)}, u32[]{:S(2)}) collective-permute-start(bf16[2,128,256]{2,1,0:T(8,128)(2,1)S(1)} %get-tuple-element.38), channel_id=1, source_target_pairs={{0,32},{16,48},{32,0},{48,16},{1,33},{17,49},{33,1},{49,17},{2,34}... | collective-permute-start | bytes 393224 | tf_op jit(solution)/shard_map/ppermute | solution.py:250

commit v6 on v5

--- a/solution.py
+++ b/solution.py
@@ -42,14 +42,25 @@
     return jnp.sum(x.reshape(-1, 8, x.shape[-1]), 0)
 
 
-def prepare_kernel(embeddings, prototypes, rows, inverse, proto, users, columns, turned, sems):
+def prepare_kernel(
+    embeddings, prototypes, rows, inverse, proto, users, columns, turned, copies, sems
+):
     fetch = [
         pltpu.make_async_copy(src, dst, sems.at[i])
-        for i, (src, dst) in enumerate(((embeddings, users), (prototypes, columns)))
+        for i, (src, dst) in enumerate(((prototypes, columns), (embeddings, users)))
     ]
     for copy in fetch:
         copy.start()
     fetch[0].wait()
+    turned[...] = columns[...].astype(f32).T
+    j = lax.axis_index("x") * NC + lax.axis_index("c")
+    own = turned[pl.ds(pl.multiple_of(j * SUB, SUB), SUB), :]
+    own = (own * lax.rsqrt(jnp.sum(own * own, -1, keepdims=True) + EPS)).astype(bf16)
+    for i in range(NZ):
+        copies[i] = own
+    leave = pltpu.make_async_copy(copies, proto, sems.at[2])
+    leave.start()
+    fetch[1].wait()
     for v in range(2):
         e = users[v].astype(f32)
         inv = lax.rsqrt(jnp.sum(e * e, -1, keepdims=True) + EPS)
@@ -57,13 +68,7 @@
         unit = (e * inv).astype(bf16)
         for i in range(NX):
             rows[i, v] = unit
-    fetch[1].wait()
-    turned[...] = columns[...].astype(f32).T
-    j = lax.axis_index("x") * NC + lax.axis_index("c")
-    own = turned[pl.ds(pl.multiple_of(j * SUB, SUB), SUB), :]
-    own = (own * lax.rsqrt(jnp.sum(own * own, -1, keepdims=True) + EPS)).astype(bf16)
-    for i in range(NZ):
-        proto[i] = own
+    leave.wait()
 
 
 def send_columns(acc, out):
@@ -79,7 +84,7 @@
             step(half, x, rows)
             return 0
 
-        lax.fori_loop(0, NX, member, 0)
+        lax.fori_loop(0, NX, member, 0, unroll=True)
 
 
 def place(half, x):
@@ -93,8 +98,8 @@
         g = place(half, x)
         for v in range(2):
             rowsum = jnp.zeros((8, U), f32)
-            for q in range(Q):
-                at = slice(q * 128, (q + 1) * 128)
+            for q in range(COLS // 256):
+                at = slice(q * 256, (q + 1) * 256)
                 s = lax.dot_general(
                     proto[at, :], rows[x, v], (((1,), (1,)), ((), ())), preferred_element_type=f32
                 )
@@ -103,8 +108,7 @@
                 powered[g, v, at, :] = e.astype(bf16)
                 masses[g, v, at, :] = k
                 rowsum += fold(e)
-                i = v * Q + q
-                acc[i * 128 : (i + 1) * 128, :] += k[:, :128] + k[:, 128:]
+                acc[v * COLS + q * 256 : v * COLS + (q + 1) * 256, :] += k[:, :128] + k[:, 128:]
             soft[pl.ds(v * G + g, 1), :] = jnp.sum(rowsum, 0, keepdims=True)
 
     groups(group, mine, other)
@@ -129,7 +133,7 @@
             cc = jnp.concatenate([cc, cc], 1)
             return tuple(acc[g] + masses[g, v, pl.ds(at, 8), :] * cc for g in range(G))
 
-        acc = lax.fori_loop(0, COLS // 8, eight, (jnp.zeros((8, U), f32),) * G, unroll=4)
+        acc = lax.fori_loop(0, COLS // 8, eight, (jnp.zeros((8, U), f32),) * G, unroll=16)
         lines += [jnp.sum(a, 0, keepdims=True) for a in acc]
     if soft is not None:
         lines.append(soft[...])
@@ -155,7 +159,7 @@
             acc[pl.ds(v * COLS + at, 8), :] = total[:, :128] + total[:, 128:]
             return 0
 
-        lax.fori_loop(0, COLS // 8, eight, 0, unroll=4)
+        lax.fori_loop(0, COLS // 8, eight, 0, unroll=16)
     send_columns(acc, columns)
 
 
@@ -192,6 +196,7 @@
         g = place(half, x)
         far = x ^ lax.axis_index("x")
         slot = lax.div(far, 2) + 2 * lax.rem(far, 2)
+        slope = slopes.at[x % 2]
         for v in range(2):
             w = 1 - v
             a = ab[pl.ds(v * G + g, 1), :]
@@ -199,16 +204,17 @@
             for q in range(Q):
                 at = slice(q * 128, (q + 1) * 128)
                 c = wide[(w * Q + q) * 128 : (w * Q + q + 1) * 128, :]
-                slopes[v, at, :] = (
+                slope[at, v * U : (v + 1) * U] = (
                     powered[g, v, at, :].astype(f32) * a
                     - masses[g, w, at, :] * jnp.concatenate([c, c], 1) * b
                 ).astype(bf16)
-            made = jnp.dot(flat[...], slopes[v], preferred_element_type=f32)
+        made = jnp.dot(flat[...], slope[...], preferred_element_type=f32).astype(bf16)
+        for v in range(2):
             if half:
-                (give0, give1)[v][slot] = made.astype(bf16)
+                (give0, give1)[v][slot] = made[:, v * U : (v + 1) * U]
             else:
-                keep[v, slot] = made.astype(bf16)
-            acc[...] += jnp.dot(slopes[v], rows[x, v], preferred_element_type=f32)
+                keep[v, slot] = made[:, v * U : (v + 1) * U]
+        acc[...] += jnp.dot(slope[...], rows[x].reshape(2 * U, 128), preferred_element_type=f32)
 
     groups(group, mine, other)
     for y in range(NY):
@@ -263,12 +269,13 @@
             shape((NZ, SUB, 128), bf16),
         ),
         in_specs=[pl.BlockSpec(memory_space=pltpu.HBM)] * 2,
-        out_specs=(VM,) * 3,
+        out_specs=(VM, VM, pl.BlockSpec(memory_space=pl.ANY)),
         scratch_shapes=[
             pltpu.VMEM((2, U, 128), bf16),
             pltpu.VMEM((128, 512), bf16),
             pltpu.VMEM((512, 128), f32),
-            pltpu.SemaphoreType.DMA((2,)),
+            pltpu.VMEM((NZ, SUB, 128), bf16),
+            pltpu.SemaphoreType.DMA((3,)),
         ],
         compiler_params=pltpu.CompilerParams(vmem_limit_bytes=20 * 1024 * 1024),
     )(*(pltpu.with_memory_space_constraint(a, pltpu.HBM) for a in (embeddings, prototypes)))
@@ -319,7 +326,7 @@
             pltpu.VMEM((COLS, 128), f32),
             acc,
             pltpu.VMEM((4 * G, U), f32),
-            pltpu.VMEM((2, COLS, U), bf16),
+            pltpu.VMEM((2, COLS, 2 * U), bf16),
         ],
     )
     pieces = lax.all_to_all(parts, ("y", "z"), 0, 0, tiled=True)

time: 168 us -> 164 us (0.976)
  Pallas kernels: 18.1 us -> 14.3 us
    pallas_call x12, Pallas kernels: 16.2 us -> 12.5 us  [call(): pl.pallas_call(kernel, out_shape=outs, in_specs=[VM] * len(args), out_spe...]
where the time goes in v6:
time: 164 us; the launch traced here: 163 us
  blocking collectives  96.8 us (59%)
  starting transfers between devices  37.1 us (23%)
  Pallas kernels  14.3 us (9%)
  waiting for transfers between devices  14.2 us (9%)
    all_to_all x3, blocking collectives, body(): columns = lax.all_to_all(columns, ('y', 'z'), 0, 0, tiled=True)  52.7 us
    all_to_all x3, blocking collectives, body(): mass = lax.all_to_all(mass, ('x', 'c'), 0, 0)  28.4 us
    ppermute x5, starting transfers between devices, swap(): return lax.ppermute(x, axis, [(i, i ^ bit) for i in range(n)])  15.5 us
    pallas_call x12, Pallas kernels, call(): pl.pallas_call(kernel, out_shape=outs, in_specs=[VM] * len(args), out_spe...  12.5 us
    all_to_all x1, starting transfers between devices, body(): proto = lax.all_to_all(proto, 'z', 0, 0).reshape(COLS, 128)  11.7 us
    all_to_all x1, blocking collectives, body(): mine = lax.all_to_all(rows, 'x', 0, 0)  11.6 us
    all_to_all x1, starting transfers between devices, body(): whole = lax.all_to_all(pieces, ('y', 'x'), 0, 0, tiled=True)  5.36 us
    all_to_all x1, starting transfers between devices, body(): pieces = lax.all_to_all(parts, ('y', 'z'), 0, 0, tiled=True)  4.62 us
  transfers between devices with their start and end apart: 8, of which 4 were waited for; matrix products, arithmetic and copies ran while one was open for 0% of the time, Pallas kernels for 1%

profile of v6, /device:TPU:1, one launch (start us, length us, event | category | flops | bytes accessed | tf_op | source)
XLA Modules:
  0.0 163.3 jit_solution(1640569806640892204)
XLA Ops:
  0.6 1.8 %shard_map.41 = (bf16[4,2,256,128]{3,2,1,0:T(8,128)(2,1)S(1)}, f32[2,256,1]{2,1,0:T(8,128)S(1)}, bf16[8,64,128]{2,1,0:T(8,128)(2,1)}) custom-call(bf16[2,256,128]{2,1,0:T(8,128)(2,1)} %embeddings.3, bf16[128,512]{1,0:T(8,128)(2,1)} %prototypes.1), custom_call_target="tpu_custom_call" | custom-call | tf_op jit(solution)/shard_map/pallas_call | solution.py:264
  2.4 11.6 %all_to_all.78.mine = bf16[4,2,256,128]{3,2,1,0:T(8,128)(2,1)S(1)} all-to-all(bf16[4,2,256,128]{3,2,1,0:T(8,128)(2,1)S(1)} %get-tuple-element.22), channel_id=1, replica_groups=mesh['y'=8,'x'=4,'c'=2,'z'=8] {'x'}, dimensions={0} | all-to-all | bytes 1048576 | tf_op jit(solution)/shard_map/all_to_all | solution.py:282
  14.0 11.7 %all-to-all-start.1 = ((bf16[8,64,128]{2,1,0:T(8,128)(2,1)}), bf16[8,64,128]{2,1,0:T(8,128)(2,1)S(1)}, u32[]{:S(2)}, u32[]{:S(2)}) async-start(bf16[8,64,128]{2,1,0:T(8,128)(2,1)} %get-tuple-element.23), calls=%async_computation.1 | async-start | bytes 262144 | tf_op jit(solution)/shard_map/all_to_all | solution.py:283
  25.7 4.0 %collective-permute-start = (bf16[4,2,256,128]{3,2,1,0:T(8,128)(2,1)S(1)}, bf16[4,2,256,128]{3,2,1,0:T(8,128)(2,1)S(1)}, u32[]{:S(2)}, u32[]{:S(2)}) collective-permute-start(bf16[4,2,256,128]{3,2,1,0:T(8,128)(2,1)S(1)} %all_to_all.78.mine), channel_id=1, source_target_pairs={{0,8},{8,0},{1,9},{9,1},{2,10},{10,2},{3,11},{11,3},{4,12},{12,4},... | collective-permute-start | bytes 1572872 | tf_op jit(solution)/shard_map/ppermute | solution.py:256
  29.7 4.0 %all-to-all-done.1 = bf16[8,64,128]{2,1,0:T(8,128)(2,1)S(1)} async-done(((bf16[8,64,128]{2,1,0:T(8,128)(2,1)}), bf16[8,64,128]{2,1,0:T(8,128)(2,1)S(1)}, u32[]{:S(2)}, u32[]{:S(2)}) %all-to-all-start.1) | async-done | bytes 131104 | tf_op jit(solution)/shard_map/all_to_all | solution.py:283
  33.8 2.2 %shard_map.43 = (bf16[8,2,512,256]{3,2,1,0:T(8,128)(2,1)S(1)}, f32[8,2,512,256]{3,2,1,0:T(8,128)S(1)}, f32[16,256]{1,0:T(8,128)S(1)}, bf16[512,128]{1,0:T(8,128)(2,1)S(1)}) custom-call(bf16[4,2,256,128]{3,2,1,0:T(8,128)(2,1)S(1)} %all_to_all.78.mine, bf16[4,2,256,128]{3,2,1,0:T(8,128)(2,1)S(1)} %collective-permute-done.other, bf16[512,128]{1,0:T(8,128)(2,1)S(1)} %bitcast.17), custom_call_target="tpu_custom_call" | custom-call | tf_op jit(solution)/shard_map/pallas_call | solution.py:30
  36.1 21.9 %all_to_all.79 = bf16[64,8,128]{2,1,0:T(8,128)(2,1)S(1)} all-to-all(bf16[64,8,128]{2,1,0:T(8,128)(2,1)S(1)} %bitcast.19), channel_id=1, replica_groups=mesh['y'=8,'x'=4,'c'=2,'z'=8] {'y','z'}, dimensions={0} | all-to-all | bytes 262144 | tf_op jit(solution)/shard_map/all_to_all | solution.py:297
  59.0 9.7 %all_to_all.80.rowmass.first = bf16[8,32,256]{2,1,0:T(8,128)(2,1)S(1)} all-to-all(bf16[8,32,256]{2,1,0:T(8,128)(2,1)S(1)} %shard_map.44), channel_id=1, replica_groups=mesh['y'=8,'x'=4,'c'=2,'z'=8] {'x','c'}, dimensions={0} | all-to-all | bytes 262144 | tf_op jit(solution)/shard_map/all_to_all | solution.py:309
  69.6 15.4 %all_to_all.81 = bf16[64,8,128]{2,1,0:T(8,128)(2,1)S(1)} all-to-all(bf16[64,8,128]{2,1,0:T(8,128)(2,1)S(1)} %bitcast.15), channel_id=1, replica_groups=mesh['y'=8,'x'=4,'c'=2,'z'=8] {'y','z'}, dimensions={0} | all-to-all | bytes 262144 | tf_op jit(solution)/shard_map/all_to_all | solution.py:297
  86.1 9.3 %all_to_all.82.rowmass = bf16[8,16,256]{2,1,0:T(8,128)(2,1)S(1)} all-to-all(bf16[8,16,256]{2,1,0:T(8,128)(2,1)S(1)} %shard_map.46), channel_id=1, replica_groups=mesh['y'=8,'x'=4,'c'=2,'z'=8] {'x','c'}, dimensions={0} | all-to-all | bytes 131072 | tf_op jit(solution)/shard_map/all_to_all | solution.py:309
  96.3 15.4 %all_to_all.83 = bf16[64,8,128]{2,1,0:T(8,128)(2,1)S(1)} all-to-all(bf16[64,8,128]{2,1,0:T(8,128)(2,1)S(1)} %bitcast.14), channel_id=1, replica_groups=mesh['y'=8,'x'=4,'c'=2,'z'=8] {'y','z'}, dimensions={0} | all-to-all | bytes 262144 | tf_op jit(solution)/shard_map/all_to_all | solution.py:297
  112.7 9.3 %all_to_all.84.last = bf16[8,16,256]{2,1,0:T(8,128)(2,1)S(1)} all-to-all(bf16[8,16,256]{2,1,0:T(8,128)(2,1)S(1)} %get-tuple-element.31), channel_id=1, replica_groups=mesh['y'=8,'x'=4,'c'=2,'z'=8] {'x','c'}, dimensions={0} | all-to-all | bytes 131072 | tf_op jit(solution)/shard_map/all_to_all | solution.py:309
  122.0 3.2 %shard_map.49 = (bf16[2,4,128,256]{3,2,1,0:T(8,128)(2,1)S(1)}, bf16[4,128,256]{2,1,0:T(8,128)(2,1)S(1)}, bf16[4,128,256]{2,1,0:T(8,128)(2,1)S(1)}, f32[512,128]{1,0:T(8,128)}) custom-call(bf16[4,2,256,128]{3,2,1,0:T(8,128)(2,1)S(1)} %all_to_all.78.mine, bf16[4,2,256,128]{3,2,1,0:T(8,128)(2,1)S(1)} %collective-permute-done.other, ...), custom_call_target="tpu_custom_call" | custom-call | tf_op jit(solution)/shard_map/pallas_call | solution.py:30
  125.2 4.6 %all-to-all-start.8 = ((f32[64,8,128]{2,1,0:T(8,128)}), f32[64,8,128]{2,1,0:T(8,128)S(1)}, u32[]{:S(2)}, u32[]{:S(2)}) async-start(f32[64,8,128]{2,1,0:T(8,128)} %bitcast.7), calls=%async_computation.8 | async-start | bytes 524288 | tf_op jit(solution)/shard_map/all_to_all | solution.py:332
  129.9 2.7 %collective-permute-start.1 = (bf16[4,128,256]{2,1,0:T(8,128)(2,1)S(1)}, bf16[4,128,256]{2,1,0:T(8,128)(2,1)S(1)}, u32[]{:S(2)}, u32[]{:S(2)}) collective-permute-start(bf16[4,128,256]{2,1,0:T(8,128)(2,1)S(1)} %get-tuple-element.33), channel_id=1, source_target_pairs={{0,8},{8,0},{1,9},{9,1},{2,10},{10,2},{3,11},{11,3},{4,12},{12,4},... | collective-permute-start | bytes 786440 | tf_op jit(solution)/shard_map/ppermute | solution.py:256
  132.6 1.9 %collective-permute-start.2 = (bf16[4,128,256]{2,1,0:T(8,128)(2,1)S(1)}, bf16[4,128,256]{2,1,0:T(8,128)(2,1)S(1)}, u32[]{:S(2)}, u32[]{:S(2)}) collective-permute-start(bf16[4,128,256]{2,1,0:T(8,128)(2,1)S(1)} %get-tuple-element.34), channel_id=1, source_target_pairs={{0,8},{8,0},{1,9},{9,1},{2,10},{10,2},{3,11},{11,3},{4,12},{12,4},... | collective-permute-start | bytes 786440 | tf_op jit(solution)/shard_map/ppermute | solution.py:256
  134.5 1.5 collective-permute-done.2.got1
  136.1 2.2 %collective-permute-start.3 = (bf16[2,2,128,256]{3,2,1,0:T(8,128)(2,1)S(1)}, bf16[2,2,128,256]{3,2,1,0:T(8,128)(2,1)S(1)}, u32[]{:S(2)}, u32[]{:S(2)}) collective-permute-start(bf16[2,2,128,256]{3,2,1,0:T(8,128)(2,1)S(1)} %get-tuple-element.36), channel_id=1, source_target_pairs={{0,16},{16,0},{32,48},{48,32},{1,17},{17,1},{33,49},{49,33},{2,18}... | collective-permute-start | bytes 786440 | tf_op jit(solution)/shard_map/ppermute | solution.py:256
  138.3 4.6 %all-to-all-done.8 = f32[64,8,128]{2,1,0:T(8,128)S(1)} async-done(((f32[64,8,128]{2,1,0:T(8,128)}), f32[64,8,128]{2,1,0:T(8,128)S(1)}, u32[]{:S(2)}, u32[]{:S(2)}) %all-to-all-start.8) | async-done | bytes 262176 | tf_op jit(solution)/shard_map/all_to_all | solution.py:332
  143.6 5.4 %all-to-all-start.9 = ((bf16[32,8,128]{2,1,0:T(8,128)(2,1)}), bf16[32,8,128]{2,1,0:T(8,128)(2,1)S(1)}, u32[]{:S(2)}, u32[]{:S(2)}) async-start(bf16[32,8,128]{2,1,0:T(8,128)(2,1)} %bitcast.9), calls=%async_computation.9 | async-start | bytes 131072 | tf_op jit(solution)/shard_map/all_to_all | solution.py:337
  149.0 4.6 %collective-permute-start.4 = (bf16[2,128,256]{2,1,0:T(8,128)(2,1)S(1)}, bf16[2,128,256]{2,1,0:T(8,128)(2,1)S(1)}, u32[]{:S(2)}, u32[]{:S(2)}) collective-permute-start(bf16[2,128,256]{2,1,0:T(8,128)(2,1)S(1)} %get-tuple-element.38), channel_id=1, source_target_pairs={{0,32},{16,48},{32,0},{48,16},{1,33},{17,49},{33,1},{49,17},{2,34}... | collective-permute-start | bytes 393224 | tf_op jit(solution)/shard_map/ppermute | solution.py:256
  153.7 4.1 %all-to-all-done.9 = bf16[32,8,128]{2,1,0:T(8,128)(2,1)S(1)} async-done(((bf16[32,8,128]{2,1,0:T(8,128)(2,1)}), bf16[32,8,128]{2,1,0:T(8,128)(2,1)S(1)}, u32[]{:S(2)}, u32[]{:S(2)}) %all-to-all-start.9) | async-done | bytes 65568 | tf_op jit(solution)/shard_map/all_to_all | solution.py:337
  157.8 4.2 %all_gather.7.proto = bf16[2,256,128]{2,1,0:T(8,128)(2,1)S(1)} all-gather(bf16[1,256,128]{2,1,0:T(8,128)(2,1)S(1)} %bitcast.20), channel_id=1, replica_groups=mesh['y'=8,'x'=4,'c'=2,'z'=8] {'c'}, dimensions={0}, use_global_device_ids=true | all-gather | bytes 196608 | tf_op jit(solution)/shard_map/all_gather | solution.py:338
  162.0 1.3 shard_map.53
  (15 shorter events, 5.9 us)
Async XLA Ops:
  14.0 19.7 %all-to-all-start.1 = ((bf16[8,64,128]{2,1,0:T(8,128)(2,1)}), bf16[8,64,128]{2,1,0:T(8,128)(2,1)S(1)}, u32[]{:S(2)}, u32[]{:S(2)}) async-start(bf16[8,64,128]{2,1,0:T(8,128)(2,1)} %get-tuple-element.23), calls=%async_computation.1 | async-start | bytes 262144 | tf_op jit(solution)/shard_map/all_to_all | solution.py:283
  25.7 8.1 %collective-permute-start = (bf16[4,2,256,128]{3,2,1,0:T(8,128)(2,1)S(1)}, bf16[4,2,256,128]{3,2,1,0:T(8,128)(2,1)S(1)}, u32[]{:S(2)}, u32[]{:S(2)}) collective-permute-start(bf16[4,2,256,128]{3,2,1,0:T(8,128)(2,1)S(1)} %all_to_all.78.mine), channel_id=1, source_target_pairs={{0,8},{8,0},{1,9},{9,1},{2,10},{10,2},{3,11},{11,3},{4,12},{12,4},... | collective-permute-start | bytes 1572872 | tf_op jit(solution)/shard_map/ppermute | solution.py:256
  125.2 17.7 %all-to-all-start.8 = ((f32[64,8,128]{2,1,0:T(8,128)}), f32[64,8,128]{2,1,0:T(8,128)S(1)}, u32[]{:S(2)}, u32[]{:S(2)}) async-start(f32[64,8,128]{2,1,0:T(8,128)} %bitcast.7), calls=%async_computation.8 | async-start | bytes 524288 | tf_op jit(solution)/shard_map/all_to_all | solution.py:332
  129.9 4.6 %collective-permute-start.1 = (bf16[4,128,256]{2,1,0:T(8,128)(2,1)S(1)}, bf16[4,128,256]{2,1,0:T(8,128)(2,1)S(1)}, u32[]{:S(2)}, u32[]{:S(2)}) collective-permute-start(bf16[4,128,256]{2,1,0:T(8,128)(2,1)S(1)} %get-tuple-element.33), channel_id=1, source_target_pairs={{0,8},{8,0},{1,9},{9,1},{2,10},{10,2},{3,11},{11,3},{4,12},{12,4},... | collective-permute-start | bytes 786440 | tf_op jit(solution)/shard_map/ppermute | solution.py:256
  132.6 3.4 %collective-permute-start.2 = (bf16[4,128,256]{2,1,0:T(8,128)(2,1)S(1)}, bf16[4,128,256]{2,1,0:T(8,128)(2,1)S(1)}, u32[]{:S(2)}, u32[]{:S(2)}) collective-permute-start(bf16[4,128,256]{2,1,0:T(8,128)(2,1)S(1)} %get-tuple-element.34), channel_id=1, source_target_pairs={{0,8},{8,0},{1,9},{9,1},{2,10},{10,2},{3,11},{11,3},{4,12},{12,4},... | collective-permute-start | bytes 786440 | tf_op jit(solution)/shard_map/ppermute | solution.py:256
  136.1 12.8 %collective-permute-start.3 = (bf16[2,2,128,256]{3,2,1,0:T(8,128)(2,1)S(1)}, bf16[2,2,128,256]{3,2,1,0:T(8,128)(2,1)S(1)}, u32[]{:S(2)}, u32[]{:S(2)}) collective-permute-start(bf16[2,2,128,256]{3,2,1,0:T(8,128)(2,1)S(1)} %get-tuple-element.36), channel_id=1, source_target_pairs={{0,16},{16,0},{32,48},{48,32},{1,17},{17,1},{33,49},{49,33},{2,18}... | collective-permute-start | bytes 786440 | tf_op jit(solution)/shard_map/ppermute | solution.py:256
  142.9 19.1 %copy-start = (bf16[2,256,128]{2,1,0:T(8,128)(2,1)S(1)}, bf16[2,256,128]{2,1,0:T(8,128)(2,1)}, u32[]{:S(2)}) copy-start(bf16[2,256,128]{2,1,0:T(8,128)(2,1)} %embeddings.3) | copy-start | bytes 393220
  143.6 14.2 %all-to-all-start.9 = ((bf16[32,8,128]{2,1,0:T(8,128)(2,1)}), bf16[32,8,128]{2,1,0:T(8,128)(2,1)S(1)}, u32[]{:S(2)}, u32[]{:S(2)}) async-start(bf16[32,8,128]{2,1,0:T(8,128)(2,1)} %bitcast.9), calls=%async_computation.9 | async-start | bytes 131072 | tf_op jit(solution)/shard_map/all_to_all | solution.py:337
  149.0 13.0 %collective-permute-start.4 = (bf16[2,128,256]{2,1,0:T(8,128)(2,1)S(1)}, bf16[2,128,256]{2,1,0:T(8,128)(2,1)S(1)}, u32[]{:S(2)}, u32[]{:S(2)}) collective-permute-start(bf16[2,128,256]{2,1,0:T(8,128)(2,1)S(1)} %get-tuple-element.38), channel_id=1, source_target_pairs={{0,32},{16,48},{32,0},{48,16},{1,33},{17,49},{33,1},{49,17},{2,34}... | collective-permute-start | bytes 393224 | tf_op jit(solution)/shard_map/ppermute | solution.py:256

commit v7 on v6

--- a/solution.py
+++ b/solution.py
@@ -25,7 +25,7 @@
 shape = jax.ShapeDtypeStruct
 
 
-def call(kernel, outs, *args, scratch=(), flops=0):
+def call(kernel, outs, *args, scratch=(), flops=0, aliases={}):
     cost = pl.CostEstimate(flops=flops, bytes_accessed=1 << 20, transcendentals=0) if flops else None
     return pl.pallas_call(
         kernel,
@@ -34,6 +34,7 @@
         out_specs=jax.tree.map(lambda _: VM, outs),
         scratch_shapes=list(scratch),
         cost_estimate=cost,
+        input_output_aliases=aliases,
         compiler_params=pltpu.CompilerParams(vmem_limit_bytes=20 * 1024 * 1024),
     )(*args)
 
@@ -43,7 +44,7 @@
 
 
 def prepare_kernel(
-    embeddings, prototypes, rows, inverse, proto, users, columns, turned, copies, sems
+    embeddings, prototypes, unit, inverse, proto, users, columns, turned, copies, sems
 ):
     fetch = [
         pltpu.make_async_copy(src, dst, sems.at[i])
@@ -65,9 +66,7 @@
         e = users[v].astype(f32)
         inv = lax.rsqrt(jnp.sum(e * e, -1, keepdims=True) + EPS)
         inverse[v] = inv
-        unit = (e * inv).astype(bf16)
-        for i in range(NX):
-            rows[i, v] = unit
+        unit[v] = (e * inv).astype(bf16)
     leave.wait()
 
 
@@ -77,31 +76,31 @@
     out[...] = jnp.concatenate([part] * (NY * NZ), 0).astype(out.dtype)
 
 
-def groups(step, mine, other):
-    for half, rows in enumerate((mine, other)):
-
-        def member(x, _):
-            step(half, x, rows)
-            return 0
-
-        lax.fori_loop(0, NX, member, 0, unroll=True)
-
-
-def place(half, x):
-    return lax.rem(lax.axis_index("c") + half, NC) * NX + x
-
-
-def scores_kernel(mine, other, proto, powered, masses, soft, columns, acc):
-    acc[...] = jnp.zeros_like(acc)
-
-    def group(half, x, rows):
-        g = place(half, x)
+def members(step):
+    def member(r, _):
+        step(r)
+        return 0
+
+    lax.fori_loop(0, NX, member, 0, unroll=True)
+
+
+def place(half, r):
+    return lax.rem(lax.axis_index("c") + half, NC) * NX + (lax.axis_index("x") ^ r)
+
+
+def scores_kernel(half, rows, proto, *refs):
+    powered, masses, soft, acc = refs if half == 0 else refs[4:8]
+    if half == 0:
+        acc[...] = jnp.zeros_like(acc)
+
+    def group(r):
+        g = place(half, r)
         for v in range(2):
             rowsum = jnp.zeros((8, U), f32)
             for q in range(COLS // 256):
                 at = slice(q * 256, (q + 1) * 256)
                 s = lax.dot_general(
-                    proto[at, :], rows[x, v], (((1,), (1,)), ((), ())), preferred_element_type=f32
+                    proto[at, :], rows[r, v], (((1,), (1,)), ((), ())), preferred_element_type=f32
                 )
                 e = jnp.exp(s * (1.0 / SHARP))
                 k = e * e
@@ -111,8 +110,9 @@
                 acc[v * COLS + q * 256 : v * COLS + (q + 1) * 256, :] += k[:, :128] + k[:, 128:]
             soft[pl.ds(v * G + g, 1), :] = jnp.sum(rowsum, 0, keepdims=True)
 
-    groups(group, mine, other)
-    send_columns(acc, columns)
+    members(group)
+    if half:
+        send_columns(acc, refs[-1])
 
 
 def rows_kernel(sweep, masses, columns, *refs):
@@ -192,11 +192,10 @@
     ab[0 : 2 * G, :] = (1.0 / SHARP) / row_total(first, 2 * G, 2 * G)
     ab[2 * G :, :] = 1.0 / row_total(last, 0, 2 * G)
 
-    def group(half, x, rows):
-        g = place(half, x)
-        far = x ^ lax.axis_index("x")
-        slot = lax.div(far, 2) + 2 * lax.rem(far, 2)
-        slope = slopes.at[x % 2]
+    def group(half, r, rows):
+        g = place(half, r)
+        slot = ((r << 1) & 3) ^ ((r >> 1) * 3)
+        slope = slopes.at[r % 2]
         for v in range(2):
             w = 1 - v
             a = ab[pl.ds(v * G + g, 1), :]
@@ -214,9 +213,10 @@
                 (give0, give1)[v][slot] = made[:, v * U : (v + 1) * U]
             else:
                 keep[v, slot] = made[:, v * U : (v + 1) * U]
-        acc[...] += jnp.dot(slope[...], rows[x].reshape(2 * U, 128), preferred_element_type=f32)
-
-    groups(group, mine, other)
+        acc[...] += jnp.dot(slope[...], rows[r].reshape(2 * U, 128), preferred_element_type=f32)
+
+    for half, rows in enumerate((mine, other)):
+        members(lambda r, half=half, rows=rows: group(half, r, rows))
     for y in range(NY):
         for z in range(NZ):
             at = z * SUB + y * 8
@@ -261,10 +261,10 @@
     sums = shape((NY * NZ * 8, 128), bf16)
     acc = pltpu.VMEM((2 * COLS, 128), f32)
 
-    rows, inverse, proto = pl.pallas_call(
+    unit, inverse, proto = pl.pallas_call(
         prepare_kernel,
         out_shape=(
-            shape((NX, 2, U, 128), bf16),
+            shape((2, U, 128), bf16),
             shape((2, U, 1), f32),
             shape((NZ, SUB, 128), bf16),
         ),
@@ -279,18 +279,28 @@
         ],
         compiler_params=pltpu.CompilerParams(vmem_limit_bytes=20 * 1024 * 1024),
     )(*(pltpu.with_memory_space_constraint(a, pltpu.HBM) for a in (embeddings, prototypes)))
-    mine = lax.all_to_all(rows, "x", 0, 0)
     proto = lax.all_to_all(proto, "z", 0, 0).reshape(COLS, 128)
+    others = [swap(unit, "x", NX, r) for r in range(1, NX)]
+    flat = call(flat_kernel, shape((128, COLS), bf16), proto, flops=1 << 36)
+    others, proto, flat = lax.optimization_barrier((others, proto, flat))
+    mine = jnp.stack([unit] + others)
     other = swap(mine, "c", NC, 1)
-    flat = call(flat_kernel, shape((128, COLS), bf16), proto, flops=1 << 36)
-    proto, flat = lax.optimization_barrier((proto, flat))
-    powered, masses, soft, columns = call(
-        scores_kernel,
-        (kept(bf16), kept(f32), shape((2 * G, U), f32), sums),
+    part = shape((2 * COLS, 128), f32)
+    grid = (kept(bf16), kept(f32), shape((2 * G, U), f32))
+    half = call(
+        functools.partial(scores_kernel, 0),
+        (*grid, part),
         mine,
+        proto,
+        flops=1 << 31,
+    )
+    powered, masses, soft, _, columns = call(
+        functools.partial(scores_kernel, 1),
+        (*grid, part, sums),
         other,
         proto,
-        scratch=[acc],
+        *half,
+        aliases={2: 0, 3: 1, 4: 2, 5: 3},
     )
     first = None
     for sweep in range(ITERS):
@@ -339,7 +349,7 @@
     unit, far = call(
         near_kernel, (shape((2, 128, U), f32), shape((2, 128, U), bf16)), stay, near
     )
-    far = swap(far, "x", NX, 2)
+    far = swap(far, "x", NX, 3)
     return tuple(
         call(
             finish_kernel,

time: 164 us -> 165 us (level)
  starting transfers between devices: 37.1 us -> 45.3 us
  blocking collectives: 96.8 us -> 89.3 us
    all_to_all x1 -> x0, blocking collectives: 11.6 us -> none  [body(): mine = lax.all_to_all(rows, 'x', 0, 0)]
    ppermute x5 -> x8, starting transfers between devices: 15.5 us -> 24.4 us  [swap(): return lax.ppermute(x, axis, [(i, i ^ bit) for i in range(n)])]
    ppermute x5 -> x8, waiting for transfers between devices: 1.5 us -> 5.61 us  [swap(): return lax.ppermute(x, axis, [(i, i ^ bit) for i in range(n)])]
    all_to_all x1, waiting for transfers between devices: 3.99 us -> 0.01 us  [body(): proto = lax.all_to_all(proto, 'z', 0, 0).reshape(COLS, 128)]
    all_to_all x3, blocking collectives: 52.7 us -> 55.3 us  [body(): columns = lax.all_to_all(columns, ('y', 'z'), 0, 0, tiled=True)]
    pallas_call x12 -> x13, Pallas kernels: 12.5 us -> 12.7 us  [call(): pl.pallas_call(kernel, out_shape=outs, in_specs=[VM] * len(args), out_spe...]
  transfers between devices with their start and end apart: 8 -> 11, of which waited for: 4 -> 6; matrix products, arithmetic and copies ran while one was open for 0% -> 0% of each run, Pallas kernels for 1% -> 1%
where the time goes in v7:
time: 165 us; the launch traced here: 164 us
  blocking collectives  89.3 us (54%)
  starting transfers between devices  45.3 us (27%)
  waiting for transfers between devices  14.6 us (9%)
  Pallas kernels  14.4 us (9%)
    all_to_all x3, blocking collectives, body(): columns = lax.all_to_all(columns, ('y', 'z'), 0, 0, tiled=True)  55.3 us
    all_to_all x3, blocking collectives, body(): mass = lax.all_to_all(mass, ('x', 'c'), 0, 0)  29.8 us
    ppermute x8, starting transfers between devices, swap(): return lax.ppermute(x, axis, [(i, i ^ bit) for i in range(n)])  24.4 us
    pallas_call x13, Pallas kernels, call(): pl.pallas_call(kernel, out_shape=outs, in_specs=[VM] * len(args), out_spe...  12.7 us
    all_to_all x1, starting transfers between devices, body(): proto = lax.all_to_all(proto, 'z', 0, 0).reshape(COLS, 128)  10.9 us
    ppermute x8, waiting for transfers between devices, swap(): return lax.ppermute(x, axis, [(i, i ^ bit) for i in range(n)])  5.61 us
    all_to_all x1, starting transfers between devices, body(): whole = lax.all_to_all(pieces, ('y', 'x'), 0, 0, tiled=True)  5.37 us
    all_to_all x1, starting transfers between devices, body(): pieces = lax.all_to_all(parts, ('y', 'z'), 0, 0, tiled=True)  4.62 us
  transfers between devices with their start and end apart: 11, of which 6 were waited for; matrix products, arithmetic and copies ran while one was open for 0% of the time, Pallas kernels for 1%

profile of v7, /device:TPU:1, one launch (start us, length us, event | category | flops | bytes accessed | tf_op | source)
XLA Modules:
  0.0 164.4 jit_solution(10248011769147173497)
XLA Ops:
  0.6 1.8 %shard_map.41 = (bf16[2,256,128]{2,1,0:T(8,128)(2,1)S(1)}, f32[2,256,1]{2,1,0:T(8,128)S(1)}, bf16[8,64,128]{2,1,0:T(8,128)(2,1)}) custom-call(bf16[2,256,128]{2,1,0:T(8,128)(2,1)} %embeddings.3, bf16[128,512]{1,0:T(8,128)(2,1)} %prototypes.1), custom_call_target="tpu_custom_call" | custom-call | tf_op jit(solution)/shard_map/pallas_call | solution.py:264
  2.4 10.9 %all-to-all-start = ((bf16[8,64,128]{2,1,0:T(8,128)(2,1)}), bf16[8,64,128]{2,1,0:T(8,128)(2,1)S(1)}, u32[]{:S(2)}, u32[]{:S(2)}) async-start(bf16[8,64,128]{2,1,0:T(8,128)(2,1)} %get-tuple-element.30), calls=%async_computation | async-start | bytes 262144 | tf_op jit(solution)/shard_map/all_to_all | solution.py:282
  13.3 4.4 %collective-permute-start.2 = (bf16[2,256,128]{2,1,0:T(8,128)(2,1)S(1)}, bf16[2,256,128]{2,1,0:T(8,128)(2,1)S(1)}, u32[]{:S(2)}, u32[]{:S(2)}) collective-permute-start(bf16[2,256,128]{2,1,0:T(8,128)(2,1)S(1)} %get-tuple-element.29), channel_id=1, source_target_pairs={{0,48},{16,32},{32,16},{48,0},{1,49},{17,33},{33,17},{49,1},{2,50}... | collective-permute-start | bytes 393224 | tf_op jit(solution)/shard_map/ppermute | solution.py:256
  17.7 2.4 %collective-permute-start.1 = (bf16[2,256,128]{2,1,0:T(8,128)(2,1)S(1)}, bf16[2,256,128]{2,1,0:T(8,128)(2,1)S(1)}, u32[]{:S(2)}, u32[]{:S(2)}) collective-permute-start(bf16[2,256,128]{2,1,0:T(8,128)(2,1)S(1)} %get-tuple-element.29), channel_id=1, source_target_pairs={{0,32},{16,48},{32,0},{48,16},{1,33},{17,49},{33,1},{49,17},{2,34}... | collective-permute-start | bytes 393224 | tf_op jit(solution)/shard_map/ppermute | solution.py:256
  20.1 2.2 %collective-permute-start = (bf16[2,256,128]{2,1,0:T(8,128)(2,1)S(1)}, bf16[2,256,128]{2,1,0:T(8,128)(2,1)S(1)}, u32[]{:S(2)}, u32[]{:S(2)}) collective-permute-start(bf16[2,256,128]{2,1,0:T(8,128)(2,1)S(1)} %get-tuple-element.29), channel_id=1, source_target_pairs={{0,16},{16,0},{32,48},{48,32},{1,17},{17,1},{33,49},{49,33},{2,18}... | collective-permute-start | bytes 393224 | tf_op jit(solution)/shard_map/ppermute | solution.py:256
  22.4 2.5 %collective-permute-done.1 = bf16[2,256,128]{2,1,0:T(8,128)(2,1)S(1)} collective-permute-done((bf16[2,256,128]{2,1,0:T(8,128)(2,1)S(1)}, bf16[2,256,128]{2,1,0:T(8,128)(2,1)S(1)}, u32[]{:S(2)}, u32[]{:S(2)}) %collective-permute-start.1) | collective-permute-done | bytes 131104 | tf_op jit(solution)/shard_map/ppermute | solution.py:256
  26.2 4.3 %collective-permute-start.3 = (bf16[4,2,256,128]{3,2,1,0:T(8,128)(2,1)S(1)}, bf16[4,2,256,128]{3,2,1,0:T(8,128)(2,1)S(1)}, u32[]{:S(2)}, u32[]{:S(2)}) collective-permute-start(bf16[4,2,256,128]{3,2,1,0:T(8,128)(2,1)S(1)} %pad_maximum_fusion.rows.mine), channel_id=1, source_target_pairs={{0,8},{8,0},{1,9},{9,1},{2,10},{10,2},{3,11},{11,3},{4,12},{12,4},... | collective-permute-start | bytes 1572872 | tf_op jit(solution)/shard_map/ppermute | solution.py:256
  33.2 24.5 %all_to_all.73 = bf16[64,8,128]{2,1,0:T(8,128)(2,1)S(1)} all-to-all(bf16[64,8,128]{2,1,0:T(8,128)(2,1)S(1)} %bitcast.24), channel_id=1, replica_groups=mesh['y'=8,'x'=4,'c'=2,'z'=8] {'y','z'}, dimensions={0} | all-to-all | bytes 262144 | tf_op jit(solution)/shard_map/all_to_all | solution.py:307
  58.8 11.1 %all_to_all.74.rowmass.first = bf16[8,32,256]{2,1,0:T(8,128)(2,1)S(1)} all-to-all(bf16[8,32,256]{2,1,0:T(8,128)(2,1)S(1)} %shard_map.45), channel_id=1, replica_groups=mesh['y'=8,'x'=4,'c'=2,'z'=8] {'x','c'}, dimensions={0} | all-to-all | bytes 262144 | tf_op jit(solution)/shard_map/all_to_all | solution.py:319
  70.8 15.4 %all_to_all.75 = bf16[64,8,128]{2,1,0:T(8,128)(2,1)S(1)} all-to-all(bf16[64,8,128]{2,1,0:T(8,128)(2,1)S(1)} %bitcast.22), channel_id=1, replica_groups=mesh['y'=8,'x'=4,'c'=2,'z'=8] {'y','z'}, dimensions={0} | all-to-all | bytes 262144 | tf_op jit(solution)/shard_map/all_to_all | solution.py:307
  87.3 9.3 %all_to_all.76.rowmass = bf16[8,16,256]{2,1,0:T(8,128)(2,1)S(1)} all-to-all(bf16[8,16,256]{2,1,0:T(8,128)(2,1)S(1)} %shard_map.47), channel_id=1, replica_groups=mesh['y'=8,'x'=4,'c'=2,'z'=8] {'x','c'}, dimensions={0} | all-to-all | bytes 131072 | tf_op jit(solution)/shard_map/all_to_all | solution.py:319
  97.4 15.4 %all_to_all.77 = bf16[64,8,128]{2,1,0:T(8,128)(2,1)S(1)} all-to-all(bf16[64,8,128]{2,1,0:T(8,128)(2,1)S(1)} %bitcast.21), channel_id=1, replica_groups=mesh['y'=8,'x'=4,'c'=2,'z'=8] {'y','z'}, dimensions={0} | all-to-all | bytes 262144 | tf_op jit(solution)/shard_map/all_to_all | solution.py:307
  113.9 9.3 %all_to_all.78.last = bf16[8,16,256]{2,1,0:T(8,128)(2,1)S(1)} all-to-all(bf16[8,16,256]{2,1,0:T(8,128)(2,1)S(1)} %get-tuple-element.45), channel_id=1, replica_groups=mesh['y'=8,'x'=4,'c'=2,'z'=8] {'x','c'}, dimensions={0} | all-to-all | bytes 131072 | tf_op jit(solution)/shard_map/all_to_all | solution.py:319
  123.2 3.2 %shard_map.50 = (bf16[2,4,128,256]{3,2,1,0:T(8,128)(2,1)S(1)}, bf16[4,128,256]{2,1,0:T(8,128)(2,1)S(1)}, bf16[4,128,256]{2,1,0:T(8,128)(2,1)S(1)}, f32[512,128]{1,0:T(8,128)}) custom-call(bf16[4,2,256,128]{3,2,1,0:T(8,128)(2,1)S(1)} %pad_maximum_fusion.rows.mine, bf16[4,2,256,128]{3,2,1,0:T(8,128)(2,1)S(1)} %collective-permute-done.3.rows.other, ...), custom_call_target="tpu_custom_call" | custom-call | tf_op jit(solution)/shard_map/pallas_call | solution.py:30
  126.4 4.6 %all-to-all-start.7 = ((f32[64,8,128]{2,1,0:T(8,128)}), f32[64,8,128]{2,1,0:T(8,128)S(1)}, u32[]{:S(2)}, u32[]{:S(2)}) async-start(f32[64,8,128]{2,1,0:T(8,128)} %bitcast.11), calls=%async_computation.7 | async-start | bytes 524288 | tf_op jit(solution)/shard_map/all_to_all | solution.py:342
  131.1 2.7 %collective-permute-start.4 = (bf16[4,128,256]{2,1,0:T(8,128)(2,1)S(1)}, bf16[4,128,256]{2,1,0:T(8,128)(2,1)S(1)}, u32[]{:S(2)}, u32[]{:S(2)}) collective-permute-start(bf16[4,128,256]{2,1,0:T(8,128)(2,1)S(1)} %get-tuple-element.47), channel_id=1, source_target_pairs={{0,8},{8,0},{1,9},{9,1},{2,10},{10,2},{3,11},{11,3},{4,12},{12,4},... | collective-permute-start | bytes 786440 | tf_op jit(solution)/shard_map/ppermute | solution.py:256
  133.8 1.9 %collective-permute-start.5 = (bf16[4,128,256]{2,1,0:T(8,128)(2,1)S(1)}, bf16[4,128,256]{2,1,0:T(8,128)(2,1)S(1)}, u32[]{:S(2)}, u32[]{:S(2)}) collective-permute-start(bf16[4,128,256]{2,1,0:T(8,128)(2,1)S(1)} %get-tuple-element.48), channel_id=1, source_target_pairs={{0,8},{8,0},{1,9},{9,1},{2,10},{10,2},{3,11},{11,3},{4,12},{12,4},... | collective-permute-start | bytes 786440 | tf_op jit(solution)/shard_map/ppermute | solution.py:256
  135.7 1.5 collective-permute-done.5.got1
  137.3 2.2 %collective-permute-start.6 = (bf16[2,2,128,256]{3,2,1,0:T(8,128)(2,1)S(1)}, bf16[2,2,128,256]{3,2,1,0:T(8,128)(2,1)S(1)}, u32[]{:S(2)}, u32[]{:S(2)}) collective-permute-start(bf16[2,2,128,256]{3,2,1,0:T(8,128)(2,1)S(1)} %get-tuple-element.50), channel_id=1, source_target_pairs={{0,16},{16,0},{32,48},{48,32},{1,17},{17,1},{33,49},{49,33},{2,18}... | collective-permute-start | bytes 786440 | tf_op jit(solution)/shard_map/ppermute | solution.py:256
  139.5 4.6 %all-to-all-done.7 = f32[64,8,128]{2,1,0:T(8,128)S(1)} async-done(((f32[64,8,128]{2,1,0:T(8,128)}), f32[64,8,128]{2,1,0:T(8,128)S(1)}, u32[]{:S(2)}, u32[]{:S(2)}) %all-to-all-start.7) | async-done | bytes 262176 | tf_op jit(solution)/shard_map/all_to_all | solution.py:342
  144.8 5.4 %all-to-all-start.8 = ((bf16[32,8,128]{2,1,0:T(8,128)(2,1)}), bf16[32,8,128]{2,1,0:T(8,128)(2,1)S(1)}, u32[]{:S(2)}, u32[]{:S(2)}) async-start(bf16[32,8,128]{2,1,0:T(8,128)(2,1)} %bitcast.13), calls=%async_computation.8 | async-start | bytes 131072 | tf_op jit(solution)/shard_map/all_to_all | solution.py:347
  150.2 4.3 %collective-permute-start.7 = (bf16[2,128,256]{2,1,0:T(8,128)(2,1)S(1)}, bf16[2,128,256]{2,1,0:T(8,128)(2,1)S(1)}, u32[]{:S(2)}, u32[]{:S(2)}) collective-permute-start(bf16[2,128,256]{2,1,0:T(8,128)(2,1)S(1)} %get-tuple-element.52), channel_id=1, source_target_pairs={{0,48},{16,32},{32,16},{48,0},{1,49},{17,33},{33,17},{49,1},{2,50}... | collective-permute-start | bytes 393224 | tf_op jit(solution)/shard_map/ppermute | solution.py:256
  154.6 4.4 %all-to-all-done.8 = bf16[32,8,128]{2,1,0:T(8,128)(2,1)S(1)} async-done(((bf16[32,8,128]{2,1,0:T(8,128)(2,1)}), bf16[32,8,128]{2,1,0:T(8,128)(2,1)S(1)}, u32[]{:S(2)}, u32[]{:S(2)}) %all-to-all-start.8) | async-done | bytes 65568 | tf_op jit(solution)/shard_map/all_to_all | solution.py:347
  159.0 4.2 %all_gather.7.proto = bf16[2,256,128]{2,1,0:T(8,128)(2,1)S(1)} all-gather(bf16[1,256,128]{2,1,0:T(8,128)(2,1)S(1)} %bitcast.26), channel_id=1, replica_groups=mesh['y'=8,'x'=4,'c'=2,'z'=8] {'c'}, dimensions={0}, use_global_device_ids=true | all-gather | bytes 196608 | tf_op jit(solution)/shard_map/all_gather | solution.py:348
  (22 shorter events, 11.2 us)
Async XLA Ops:
  2.4 19.9 %all-to-all-start = ((bf16[8,64,128]{2,1,0:T(8,128)(2,1)}), bf16[8,64,128]{2,1,0:T(8,128)(2,1)S(1)}, u32[]{:S(2)}, u32[]{:S(2)}) async-start(bf16[8,64,128]{2,1,0:T(8,128)(2,1)} %get-tuple-element.30), calls=%async_computation | async-start | bytes 262144 | tf_op jit(solution)/shard_map/all_to_all | solution.py:282
  13.3 9.1 %collective-permute-start.2 = (bf16[2,256,128]{2,1,0:T(8,128)(2,1)S(1)}, bf16[2,256,128]{2,1,0:T(8,128)(2,1)S(1)}, u32[]{:S(2)}, u32[]{:S(2)}) collective-permute-start(bf16[2,256,128]{2,1,0:T(8,128)(2,1)S(1)} %get-tuple-element.29), channel_id=1, source_target_pairs={{0,48},{16,32},{32,16},{48,0},{1,49},{17,33},{33,17},{49,1},{2,50}... | collective-permute-start | bytes 393224 | tf_op jit(solution)/shard_map/ppermute | solution.py:256
  17.7 7.2 %collective-permute-start.1 = (bf16[2,256,128]{2,1,0:T(8,128)(2,1)S(1)}, bf16[2,256,128]{2,1,0:T(8,128)(2,1)S(1)}, u32[]{:S(2)}, u32[]{:S(2)}) collective-permute-start(bf16[2,256,128]{2,1,0:T(8,128)(2,1)S(1)} %get-tuple-element.29), channel_id=1, source_target_pairs={{0,32},{16,48},{32,0},{48,16},{1,33},{17,49},{33,1},{49,17},{2,34}... | collective-permute-start | bytes 393224 | tf_op jit(solution)/shard_map/ppermute | solution.py:256
  20.1 6.0 %collective-permute-start = (bf16[2,256,128]{2,1,0:T(8,128)(2,1)S(1)}, bf16[2,256,128]{2,1,0:T(8,128)(2,1)S(1)}, u32[]{:S(2)}, u32[]{:S(2)}) collective-permute-start(bf16[2,256,128]{2,1,0:T(8,128)(2,1)S(1)} %get-tuple-element.29), channel_id=1, source_target_pairs={{0,16},{16,0},{32,48},{48,32},{1,17},{17,1},{33,49},{49,33},{2,18}... | collective-permute-start | bytes 393224 | tf_op jit(solution)/shard_map/ppermute | solution.py:256
  26.2 5.8 %collective-permute-start.3 = (bf16[4,2,256,128]{3,2,1,0:T(8,128)(2,1)S(1)}, bf16[4,2,256,128]{3,2,1,0:T(8,128)(2,1)S(1)}, u32[]{:S(2)}, u32[]{:S(2)}) collective-permute-start(bf16[4,2,256,128]{3,2,1,0:T(8,128)(2,1)S(1)} %pad_maximum_fusion.rows.mine), channel_id=1, source_target_pairs={{0,8},{8,0},{1,9},{9,1},{2,10},{10,2},{3,11},{11,3},{4,12},{12,4},... | collective-permute-start | bytes 1572872 | tf_op jit(solution)/shard_map/ppermute | solution.py:256
  126.4 17.6 %all-to-all-start.7 = ((f32[64,8,128]{2,1,0:T(8,128)}), f32[64,8,128]{2,1,0:T(8,128)S(1)}, u32[]{:S(2)}, u32[]{:S(2)}) async-start(f32[64,8,128]{2,1,0:T(8,128)} %bitcast.11), calls=%async_computation.7 | async-start | bytes 524288 | tf_op jit(solution)/shard_map/all_to_all | solution.py:342
  131.1 4.6 %collective-permute-start.4 = (bf16[4,128,256]{2,1,0:T(8,128)(2,1)S(1)}, bf16[4,128,256]{2,1,0:T(8,128)(2,1)S(1)}, u32[]{:S(2)}, u32[]{:S(2)}) collective-permute-start(bf16[4,128,256]{2,1,0:T(8,128)(2,1)S(1)} %get-tuple-element.47), channel_id=1, source_target_pairs={{0,8},{8,0},{1,9},{9,1},{2,10},{10,2},{3,11},{11,3},{4,12},{12,4},... | collective-permute-start | bytes 786440 | tf_op jit(solution)/shard_map/ppermute | solution.py:256
  133.8 3.4 %collective-permute-start.5 = (bf16[4,128,256]{2,1,0:T(8,128)(2,1)S(1)}, bf16[4,128,256]{2,1,0:T(8,128)(2,1)S(1)}, u32[]{:S(2)}, u32[]{:S(2)}) collective-permute-start(bf16[4,128,256]{2,1,0:T(8,128)(2,1)S(1)} %get-tuple-element.48), channel_id=1, source_target_pairs={{0,8},{8,0},{1,9},{9,1},{2,10},{10,2},{3,11},{11,3},{4,12},{12,4},... | collective-permute-start | bytes 786440 | tf_op jit(solution)/shard_map/ppermute | solution.py:256
  137.3 12.8 %collective-permute-start.6 = (bf16[2,2,128,256]{3,2,1,0:T(8,128)(2,1)S(1)}, bf16[2,2,128,256]{3,2,1,0:T(8,128)(2,1)S(1)}, u32[]{:S(2)}, u32[]{:S(2)}) collective-permute-start(bf16[2,2,128,256]{3,2,1,0:T(8,128)(2,1)S(1)} %get-tuple-element.50), channel_id=1, source_target_pairs={{0,16},{16,0},{32,48},{48,32},{1,17},{17,1},{33,49},{49,33},{2,18}... | collective-permute-start | bytes 786440 | tf_op jit(solution)/shard_map/ppermute | solution.py:256
  144.1 19.1 %copy-start = (bf16[2,256,128]{2,1,0:T(8,128)(2,1)S(1)}, bf16[2,256,128]{2,1,0:T(8,128)(2,1)}, u32[]{:S(2)}) copy-start(bf16[2,256,128]{2,1,0:T(8,128)(2,1)} %embeddings.3) | copy-start | bytes 393220
  144.8 14.2 %all-to-all-start.8 = ((bf16[32,8,128]{2,1,0:T(8,128)(2,1)}), bf16[32,8,128]{2,1,0:T(8,128)(2,1)S(1)}, u32[]{:S(2)}, u32[]{:S(2)}) async-start(bf16[32,8,128]{2,1,0:T(8,128)(2,1)} %bitcast.13), calls=%async_computation.8 | async-start | bytes 131072 | tf_op jit(solution)/shard_map/all_to_all | solution.py:347
  150.2 13.0 %collective-permute-start.7 = (bf16[2,128,256]{2,1,0:T(8,128)(2,1)S(1)}, bf16[2,128,256]{2,1,0:T(8,128)(2,1)S(1)}, u32[]{:S(2)}, u32[]{:S(2)}) collective-permute-start(bf16[2,128,256]{2,1,0:T(8,128)(2,1)S(1)} %get-tuple-element.52), channel_id=1, source_target_pairs={{0,48},{16,32},{32,16},{48,0},{1,49},{17,33},{33,17},{49,1},{2,50}... | collective-permute-start | bytes 393224 | tf_op jit(solution)/shard_map/ppermute | solution.py:256

commit v8 on v6

--- a/solution.py
+++ b/solution.py
@@ -23,6 +23,28 @@
 f32, bf16 = jnp.float32, jnp.bfloat16
 VM = pl.BlockSpec(memory_space=pltpu.VMEM)
 shape = jax.ShapeDtypeStruct
+
+
+SIZES = dict(y=NY, x=NX, c=NC, z=NZ)
+FIRST = dict(y=4, x=2, c=0, z=4)
+
+
+def order(axes):
+    places = [[]]
+    for a in axes:
+        places = [p + [(i + FIRST[a]) % SIZES[a]] for p in places for i in range(SIZES[a])]
+    return places
+
+
+def exchange(x, axes):
+    members = []
+    for place_ in order(axes):
+        at = 0
+        for a, i in zip(axes, place_):
+            at = at * SIZES[a] + i
+        members.append(at)
+    axis = axes if len(axes) > 1 else axes[0]
+    return lax.all_to_all(x, axis, 0, 0, tiled=True, axis_index_groups=[members])
 
 
 def call(kernel, outs, *args, scratch=(), flops=0):
@@ -176,14 +198,16 @@
     scale,
     first,
     last,
-    keep,
-    give0,
-    give1,
+    stay,
+    near,
+    give_stay,
+    give_near,
     parts,
     acc,
     wide,
     ab,
     slopes,
+    units,
 ):
     acc[...] = jnp.zeros_like(acc)
     turned = jnp.concatenate([scale[...] * (1.0 / SHARP)] * 16, 0).T
@@ -194,8 +218,8 @@
 
     def group(half, x, rows):
         g = place(half, x)
-        far = x ^ lax.axis_index("x")
-        slot = lax.div(far, 2) + 2 * lax.rem(far, 2)
+        far = lax.rem(x + FIRST["x"], NX) ^ lax.axis_index("x")
+        slot = ((far << 1) & 3) ^ ((far >> 1) * 3)
         slope = slopes.at[x % 2]
         for v in range(2):
             w = 1 - v
@@ -210,34 +234,32 @@
                 ).astype(bf16)
         made = jnp.dot(flat[...], slope[...], preferred_element_type=f32).astype(bf16)
         for v in range(2):
-            if half:
-                (give0, give1)[v][slot] = made[:, v * U : (v + 1) * U]
-            else:
-                keep[v, slot] = made[:, v * U : (v + 1) * U]
+            units[half, slot, v] = made[:, v * U : (v + 1) * U]
         acc[...] += jnp.dot(slope[...], rows[x].reshape(2 * U, 128), preferred_element_type=f32)
 
     groups(group, mine, other)
-    for y in range(NY):
-        for z in range(NZ):
-            at = z * SUB + y * 8
-            parts[(y * NZ + z) * 8 : (y * NZ + z + 1) * 8, :] = acc[at : at + 8, :]
+    for i in range(2):
+        for v in range(2):
+            stay[v, i], near[v, i] = units[0, i, v], units[0, 2 + i, v]
+            give_stay[v, i], give_near[v, i] = units[1, i, v], units[1, 2 + i, v]
+    for i, (y, z) in enumerate(order(("y", "z"))):
+        at = (z - FIRST["z"]) % NZ * SUB + y * 8
+        parts[i * 8 : (i + 1) * 8, :] = acc[at : at + 8, :]
 
 
 def piece_kernel(pieces, out):
     out[...] = jnp.concatenate([fold(pieces[...])] * (NY * NX), 0).astype(bf16)
 
 
-def cores_kernel(keep, got0, got1, stay, near):
-    for v, got in enumerate((got0, got1)):
-        for i in range(2):
-            stay[v, i] = (keep[v, i].astype(f32) + got[i].astype(f32)).astype(bf16)
-            near[v, i] = (keep[v, 2 + i].astype(f32) + got[2 + i].astype(f32)).astype(bf16)
-
-
-def near_kernel(stay, got, unit, far):
-    for v in range(2):
-        unit[v] = stay[v, 0].astype(f32) + got[v, 0].astype(f32)
-        far[v] = (stay[v, 1].astype(f32) + got[v, 1].astype(f32)).astype(bf16)
+def add_kernel(mine, got, out):
+    out[...] = (mine[...].astype(f32) + got[...].astype(f32)).astype(bf16)
+
+
+def near_kernel(stay, other, got, unit, far):
+    for v in range(2):
+        unit[v] = stay[v, 0].astype(f32) + other[v, 0].astype(f32) + got[v, 0].astype(f32)
+        last = stay[v, 1].astype(f32) + other[v, 1].astype(f32) + got[v, 1].astype(f32)
+        far[v] = last.astype(bf16)
 
 
 def finish_kernel(embeddings, inverse, kept, got, proto, grad_embed, grad_proto):
@@ -247,8 +269,11 @@
         unit = embeddings[v].astype(f32) * inv
         grad_embed[v] = inv * (grad - unit * jnp.sum(unit * grad, -1, keepdims=True))
     for x in range(NX):
-        blocks = [proto[c].astype(f32).reshape(NY, NX, 8, 128)[:, x] for c in range(NC)]
-        whole = jnp.concatenate([b.reshape(SUB, 128) for b in blocks], 0)
+        blocks = []
+        for c in range(NC):
+            b = proto[c].astype(f32).reshape(NY, NX, 8, 128)[:, (x - FIRST["x"]) % NX]
+            blocks += [b[(y - FIRST["y"]) % NY] for y in range(NY)]
+        whole = jnp.concatenate(blocks, 0)
         grad_proto[:, x * NC * SUB : (x + 1) * NC * SUB] = whole.T
 
 
@@ -279,8 +304,8 @@
         ],
         compiler_params=pltpu.CompilerParams(vmem_limit_bytes=20 * 1024 * 1024),
     )(*(pltpu.with_memory_space_constraint(a, pltpu.HBM) for a in (embeddings, prototypes)))
-    mine = lax.all_to_all(rows, "x", 0, 0)
-    proto = lax.all_to_all(proto, "z", 0, 0).reshape(COLS, 128)
+    mine = exchange(rows, ("x",))
+    proto = exchange(proto, ("z",)).reshape(COLS, 128)
     other = swap(mine, "c", NC, 1)
     flat = call(flat_kernel, shape((128, COLS), bf16), proto, flops=1 << 36)
     proto, flat = lax.optimization_barrier((proto, flat))
@@ -294,7 +319,7 @@
     )
     first = None
     for sweep in range(ITERS):
-        columns = lax.all_to_all(columns, ("y", "z"), 0, 0, tiled=True)
+        columns = exchange(columns, ("y", "z"))
         lines = shape((G, 4 * G if sweep == 0 else 2 * G, U), bf16)
         mass = call(
             functools.partial(rows_kernel, sweep),
@@ -306,14 +331,14 @@
         )
         if sweep == ITERS - 1:
             mass, scale = mass
-        mass = lax.all_to_all(mass, ("x", "c"), 0, 0)
+        mass = exchange(mass, ("x", "c"))
         first = mass if first is None else first
         if sweep < ITERS - 1:
             columns = call(columns_kernel, sums, masses, mass, scratch=[acc])
-    half, part = shape((2, NX, 128, U), bf16), shape((NX, 128, U), bf16)
-    keep, give0, give1, parts = call(
+    half = shape((2, 2, 128, U), bf16)
+    stay, near, give_stay, give_near, parts = call(
         slopes_kernel,
-        (half, part, part, shape((COLS, 128), f32)),
+        (half, half, half, half, shape((COLS, 128), f32)),
         mine,
         other,
         flat,
@@ -327,19 +352,20 @@
             acc,
             pltpu.VMEM((4 * G, U), f32),
             pltpu.VMEM((2, COLS, 2 * U), bf16),
+            pltpu.VMEM((NC, NX, 2, 128, U), bf16),
         ],
     )
-    pieces = lax.all_to_all(parts, ("y", "z"), 0, 0, tiled=True)
-    half = shape((2, 2, 128, U), bf16)
-    stay, near = call(cores_kernel, (half, half), keep, *(swap(g, "c", NC, 1) for g in (give0, give1)))
+    pieces = exchange(parts, ("y", "z"))
+    near = call(add_kernel, half, near, swap(give_near, "c", NC, 1))
+    other = swap(give_stay, "c", NC, 1)
     near = swap(near, "x", NX, 1)
     pieces = call(piece_kernel, shape((NY * NX * 8, 128), bf16), pieces, flops=1 << 36)
-    whole = lax.all_to_all(pieces, ("y", "x"), 0, 0, tiled=True)
+    whole = exchange(pieces, ("y", "x"))
     whole = lax.all_gather(whole, "c", axis=0)
     unit, far = call(
-        near_kernel, (shape((2, 128, U), f32), shape((2, 128, U), bf16)), stay, near
-    )
-    far = swap(far, "x", NX, 2)
+        near_kernel, (shape((2, 128, U), f32), shape((2, 128, U), bf16)), stay, other, near
+    )
+    far = swap(far, "x", NX, 3)
     return tuple(
         call(
             finish_kernel,

time: 164 us -> 159 us (0.970)
  starting transfers between devices: 37.1 us -> 52.1 us
  waiting for transfers between devices: 14.2 us -> 2.67 us
  blocking collectives: 96.8 us -> 88.6 us
    all_to_all x3, starting transfers between devices: 21.7 us -> 38.1 us  [exchange(): lax.all_to_all(x, axis, 0, 0, tiled=True, axis_index_groups=[members])]
    all_to_all x3, waiting for transfers between devices: 12.7 us -> 0.01 us  [exchange(): lax.all_to_all(x, axis, 0, 0, tiled=True, axis_index_groups=[members])]
    all_to_all x7, blocking collectives: 92.7 us -> 85.2 us  [exchange(): lax.all_to_all(x, axis, 0, 0, tiled=True, axis_index_groups=[members])]
  transfers between devices with their start and end apart: 8 -> 8, of which waited for: 4 -> 2; matrix products, arithmetic and copies ran while one was open for 0% -> 0% of each run, Pallas kernels for 1% -> 1%
where the time goes in v8:
time: 159 us
  blocking collectives  88.6 us (56%)
  starting transfers between devices  52.1 us (33%)
  Pallas kernels  14.3 us (9%)
  waiting for transfers between devices  2.67 us (2%)
    all_to_all x7, blocking collectives, exchange(): lax.all_to_all(x, axis, 0, 0, tiled=True, axis_index_groups=[members])  85.2 us
    all_to_all x3, starting transfers between devices, exchange(): lax.all_to_all(x, axis, 0, 0, tiled=True, axis_index_groups=[members])  38.1 us
    ppermute x5, starting transfers between devices, swap(): return lax.ppermute(x, axis, [(i, i ^ bit) for i in range(n)])  14 us
    pallas_call x12, Pallas kernels, call(): pl.pallas_call(kernel, out_shape=outs, in_specs=[VM] * len(args), out_spe...  12.5 us
    all_gather x1, blocking collectives, body(): whole = lax.all_gather(whole, 'c', axis=0)  3.45 us
  transfers between devices with their start and end apart: 8, of which 2 were waited for; matrix products, arithmetic and copies ran while one was open for 0% of the time, Pallas kernels for 1%

profile of v8, /device:TPU:1, one launch (start us, length us, event | category | flops | bytes accessed | tf_op | source)
XLA Modules:
  0.0 158.5 jit_solution(2404484949541439339)
XLA Ops:
  0.6 1.8 %shard_map.41 = (bf16[4,2,256,128]{3,2,1,0:T(8,128)(2,1)S(1)}, f32[2,256,1]{2,1,0:T(8,128)S(1)}, bf16[8,64,128]{2,1,0:T(8,128)(2,1)}) custom-call(bf16[2,256,128]{2,1,0:T(8,128)(2,1)} %embeddings.3, bf16[128,512]{1,0:T(8,128)(2,1)} %prototypes.1), custom_call_target="tpu_custom_call" | custom-call | tf_op jit(solution)/shard_map/pallas_call | solution.py:289
  2.4 10.2 %all_to_all.78.mine = bf16[4,2,256,128]{3,2,1,0:T(8,128)(2,1)S(1)} all-to-all(bf16[4,2,256,128]{3,2,1,0:T(8,128)(2,1)S(1)} %get-tuple-element.21), channel_id=1, replica_groups={{32,48,0,16},{33,49,1,17},{34,50,2,18},{35,51,3,19},{36,52,4,20},{37,53..., dimensions={0} | all-to-all | bytes 1048576 | tf_op jit(solution)/shard_map/all_to_all | solution.py:47
  12.6 15.0 %all-to-all-start.1 = ((bf16[8,64,128]{2,1,0:T(8,128)(2,1)}), bf16[8,64,128]{2,1,0:T(8,128)(2,1)S(1)}, u32[]{:S(2)}, u32[]{:S(2)}) async-start(bf16[8,64,128]{2,1,0:T(8,128)(2,1)} %get-tuple-element.22), calls=%async_computation.1 | async-start | bytes 262144 | tf_op jit(solution)/shard_map/all_to_all | solution.py:47
  27.7 3.9 %collective-permute-start = (bf16[4,2,256,128]{3,2,1,0:T(8,128)(2,1)S(1)}, bf16[4,2,256,128]{3,2,1,0:T(8,128)(2,1)S(1)}, u32[]{:S(2)}, u32[]{:S(2)}) collective-permute-start(bf16[4,2,256,128]{3,2,1,0:T(8,128)(2,1)S(1)} %all_to_all.78.mine), channel_id=1, source_target_pairs={{0,8},{8,0},{1,9},{9,1},{2,10},{10,2},{3,11},{11,3},{4,12},{12,4},... | collective-permute-start | bytes 1572872 | tf_op jit(solution)/shard_map/ppermute | solution.py:281
  31.7 1.4 collective-permute-done.other
  33.1 2.2 %shard_map.43 = (bf16[8,2,512,256]{3,2,1,0:T(8,128)(2,1)S(1)}, f32[8,2,512,256]{3,2,1,0:T(8,128)S(1)}, f32[16,256]{1,0:T(8,128)S(1)}, bf16[512,128]{1,0:T(8,128)(2,1)S(1)}) custom-call(bf16[4,2,256,128]{3,2,1,0:T(8,128)(2,1)S(1)} %all_to_all.78.mine, bf16[4,2,256,128]{3,2,1,0:T(8,128)(2,1)S(1)} %collective-permute-done.other, bf16[512,128]{1,0:T(8,128)(2,1)S(1)} %bitcast.17), custom_call_target="tpu_custom_call" | custom-call | tf_op jit(solution)/shard_map/pallas_call | solution.py:52
  35.4 15.5 %all_to_all.79 = bf16[64,8,128]{2,1,0:T(8,128)(2,1)S(1)} all-to-all(bf16[64,8,128]{2,1,0:T(8,128)(2,1)S(1)} %bitcast.19), channel_id=1, replica_groups={{260,261,262,263,256,257,258,259,324,325,326,327,320,321,322,323,388,38..., dimensions={0} | all-to-all | bytes 262144 | tf_op jit(solution)/shard_map/all_to_all | solution.py:47
  50.9 1.1 shard_map.44
  51.9 9.9 %all_to_all.80.rowmass.first = bf16[8,32,256]{2,1,0:T(8,128)(2,1)S(1)} all-to-all(bf16[8,32,256]{2,1,0:T(8,128)(2,1)S(1)} %shard_map.44), channel_id=1, replica_groups={{32,40,48,56,0,8,16,24},{33,41,49,57,1,9,17,25},{34,42,50,58,2,10,18,26..., dimensions={0} | all-to-all | bytes 262144 | tf_op jit(solution)/shard_map/all_to_all | solution.py:47
  62.7 15.7 %all_to_all.81 = bf16[64,8,128]{2,1,0:T(8,128)(2,1)S(1)} all-to-all(bf16[64,8,128]{2,1,0:T(8,128)(2,1)S(1)} %bitcast.15), channel_id=1, replica_groups={{260,261,262,263,256,257,258,259,324,325,326,327,320,321,322,323,388,38..., dimensions={0} | all-to-all | bytes 262144 | tf_op jit(solution)/shard_map/all_to_all | solution.py:47
  78.4 1.1 shard_map.46
  79.5 9.1 %all_to_all.82.rowmass = bf16[8,16,256]{2,1,0:T(8,128)(2,1)S(1)} all-to-all(bf16[8,16,256]{2,1,0:T(8,128)(2,1)S(1)} %shard_map.46), channel_id=1, replica_groups={{32,40,48,56,0,8,16,24},{33,41,49,57,1,9,17,25},{34,42,50,58,2,10,18,26..., dimensions={0} | all-to-all | bytes 131072 | tf_op jit(solution)/shard_map/all_to_all | solution.py:47
  89.4 16.4 %all_to_all.83 = bf16[64,8,128]{2,1,0:T(8,128)(2,1)S(1)} all-to-all(bf16[64,8,128]{2,1,0:T(8,128)(2,1)S(1)} %bitcast.14), channel_id=1, replica_groups={{260,261,262,263,256,257,258,259,324,325,326,327,320,321,322,323,388,38..., dimensions={0} | all-to-all | bytes 262144 | tf_op jit(solution)/shard_map/all_to_all | solution.py:47
  106.9 8.3 %all_to_all.84.last = bf16[8,16,256]{2,1,0:T(8,128)(2,1)S(1)} all-to-all(bf16[8,16,256]{2,1,0:T(8,128)(2,1)S(1)} %get-tuple-element.30), channel_id=1, replica_groups={{32,40,48,56,0,8,16,24},{33,41,49,57,1,9,17,25},{34,42,50,58,2,10,18,26..., dimensions={0} | all-to-all | bytes 131072 | tf_op jit(solution)/shard_map/all_to_all | solution.py:47
  115.2 3.2 %shard_map.49 = (bf16[2,2,128,256]{3,2,1,0:T(8,128)(2,1)S(1)}, bf16[2,2,128,256]{3,2,1,0:T(8,128)(2,1)S(1)}, bf16[2,2,128,256]{3,2,1,0:T(8,128)(2,1)S(1)}, bf16[...) custom-call(bf16[4,2,256,128]{3,2,1,0:T(8,128)(2,1)S(1)} %all_to_all.78.mine, ...), custom_call_target="tpu_custom_call" | custom-call | tf_op jit(solution)/shard_map/pallas_call | solution.py:52
  118.4 13.7 %all-to-all-start.8 = ((f32[64,8,128]{2,1,0:T(8,128)}), f32[64,8,128]{2,1,0:T(8,128)S(1)}, u32[]{:S(2)}, u32[]{:S(2)}) async-start(f32[64,8,128]{2,1,0:T(8,128)} %bitcast.7), calls=%async_computation.8 | async-start | bytes 524288 | tf_op jit(solution)/shard_map/all_to_all | solution.py:47
  132.2 2.8 %collective-permute-start.2 = (bf16[2,2,128,256]{3,2,1,0:T(8,128)(2,1)S(1)}, bf16[2,2,128,256]{3,2,1,0:T(8,128)(2,1)S(1)}, u32[]{:S(2)}, u32[]{:S(2)}) collective-permute-start(bf16[2,2,128,256]{3,2,1,0:T(8,128)(2,1)S(1)} %get-tuple-element.34), channel_id=1, source_target_pairs={{0,8},{8,0},{1,9},{9,1},{2,10},{10,2},{3,11},{11,3},{4,12},{12,4},... | collective-permute-start | bytes 786440 | tf_op jit(solution)/shard_map/ppermute | solution.py:281
  135.0 1.9 %collective-permute-start.1 = (bf16[2,2,128,256]{3,2,1,0:T(8,128)(2,1)S(1)}, bf16[2,2,128,256]{3,2,1,0:T(8,128)(2,1)S(1)}, u32[]{:S(2)}, u32[]{:S(2)}) collective-permute-start(bf16[2,2,128,256]{3,2,1,0:T(8,128)(2,1)S(1)} %get-tuple-element.32), channel_id=1, source_target_pairs={{0,8},{8,0},{1,9},{9,1},{2,10},{10,2},{3,11},{11,3},{4,12},{12,4},... | collective-permute-start | bytes 786440 | tf_op jit(solution)/shard_map/ppermute | solution.py:281
  137.0 3.1 %collective-permute-start.3 = (bf16[2,2,128,256]{3,2,1,0:T(8,128)(2,1)S(1)}, bf16[2,2,128,256]{3,2,1,0:T(8,128)(2,1)S(1)}, u32[]{:S(2)}, u32[]{:S(2)}) collective-permute-start(bf16[2,2,128,256]{3,2,1,0:T(8,128)(2,1)S(1)} %shard_map.50), channel_id=1, source_target_pairs={{0,16},{16,0},{32,48},{48,32},{1,17},{17,1},{33,49},{49,33},{2,18}... | collective-permute-start | bytes 786440 | tf_op jit(solution)/shard_map/ppermute | solution.py:281
  140.8 9.4 %all-to-all-start.9 = ((bf16[32,8,128]{2,1,0:T(8,128)(2,1)}), bf16[32,8,128]{2,1,0:T(8,128)(2,1)S(1)}, u32[]{:S(2)}, u32[]{:S(2)}) async-start(bf16[32,8,128]{2,1,0:T(8,128)(2,1)} %bitcast.9), calls=%async_computation.9 | async-start | bytes 131072 | tf_op jit(solution)/shard_map/all_to_all | solution.py:47
  150.3 2.2 %collective-permute-start.4 = (bf16[2,128,256]{2,1,0:T(8,128)(2,1)S(1)}, bf16[2,128,256]{2,1,0:T(8,128)(2,1)S(1)}, u32[]{:S(2)}, u32[]{:S(2)}) collective-permute-start(bf16[2,128,256]{2,1,0:T(8,128)(2,1)S(1)} %get-tuple-element.36), channel_id=1, source_target_pairs={{0,48},{16,32},{32,16},{48,0},{1,49},{17,33},{33,17},{49,1},{2,50}... | collective-permute-start | bytes 393224 | tf_op jit(solution)/shard_map/ppermute | solution.py:281
  152.5 3.4 %all_gather.7.proto = bf16[2,256,128]{2,1,0:T(8,128)(2,1)S(1)} all-gather(bf16[1,256,128]{2,1,0:T(8,128)(2,1)S(1)} %bitcast.20), channel_id=1, replica_groups=mesh['y'=8,'x'=4,'c'=2,'z'=8] {'c'}, dimensions={0}, use_global_device_ids=true | all-gather | bytes 196608 | tf_op jit(solution)/shard_map/all_gather | solution.py:364
  156.0 1.3 collective-permute-done.4.got
  157.2 1.3 shard_map.53
  (15 shorter events, 3.7 us)
Async XLA Ops:
  12.6 19.0 %all-to-all-start.1 = ((bf16[8,64,128]{2,1,0:T(8,128)(2,1)}), bf16[8,64,128]{2,1,0:T(8,128)(2,1)S(1)}, u32[]{:S(2)}, u32[]{:S(2)}) async-start(bf16[8,64,128]{2,1,0:T(8,128)(2,1)} %get-tuple-element.22), calls=%async_computation.1 | async-start | bytes 262144 | tf_op jit(solution)/shard_map/all_to_all | solution.py:47
  27.7 5.5 %collective-permute-start = (bf16[4,2,256,128]{3,2,1,0:T(8,128)(2,1)S(1)}, bf16[4,2,256,128]{3,2,1,0:T(8,128)(2,1)S(1)}, u32[]{:S(2)}, u32[]{:S(2)}) collective-permute-start(bf16[4,2,256,128]{3,2,1,0:T(8,128)(2,1)S(1)} %all_to_all.78.mine), channel_id=1, source_target_pairs={{0,8},{8,0},{1,9},{9,1},{2,10},{10,2},{3,11},{11,3},{4,12},{12,4},... | collective-permute-start | bytes 1572872 | tf_op jit(solution)/shard_map/ppermute | solution.py:281
  118.4 21.7 %all-to-all-start.8 = ((f32[64,8,128]{2,1,0:T(8,128)}), f32[64,8,128]{2,1,0:T(8,128)S(1)}, u32[]{:S(2)}, u32[]{:S(2)}) async-start(f32[64,8,128]{2,1,0:T(8,128)} %bitcast.7), calls=%async_computation.8 | async-start | bytes 524288 | tf_op jit(solution)/shard_map/all_to_all | solution.py:47
  132.2 4.7 %collective-permute-start.2 = (bf16[2,2,128,256]{3,2,1,0:T(8,128)(2,1)S(1)}, bf16[2,2,128,256]{3,2,1,0:T(8,128)(2,1)S(1)}, u32[]{:S(2)}, u32[]{:S(2)}) collective-permute-start(bf16[2,2,128,256]{3,2,1,0:T(8,128)(2,1)S(1)} %get-tuple-element.34), channel_id=1, source_target_pairs={{0,8},{8,0},{1,9},{9,1},{2,10},{10,2},{3,11},{11,3},{4,12},{12,4},... | collective-permute-start | bytes 786440 | tf_op jit(solution)/shard_map/ppermute | solution.py:281
  135.0 15.2 %collective-permute-start.1 = (bf16[2,2,128,256]{3,2,1,0:T(8,128)(2,1)S(1)}, bf16[2,2,128,256]{3,2,1,0:T(8,128)(2,1)S(1)}, u32[]{:S(2)}, u32[]{:S(2)}) collective-permute-start(bf16[2,2,128,256]{3,2,1,0:T(8,128)(2,1)S(1)} %get-tuple-element.32), channel_id=1, source_target_pairs={{0,8},{8,0},{1,9},{9,1},{2,10},{10,2},{3,11},{11,3},{4,12},{12,4},... | collective-permute-start | bytes 786440 | tf_op jit(solution)/shard_map/ppermute | solution.py:281
  137.0 13.2 %collective-permute-start.3 = (bf16[2,2,128,256]{3,2,1,0:T(8,128)(2,1)S(1)}, bf16[2,2,128,256]{3,2,1,0:T(8,128)(2,1)S(1)}, u32[]{:S(2)}, u32[]{:S(2)}) collective-permute-start(bf16[2,2,128,256]{3,2,1,0:T(8,128)(2,1)S(1)} %shard_map.50), channel_id=1, source_target_pairs={{0,16},{16,0},{32,48},{48,32},{1,17},{17,1},{33,49},{49,33},{2,18}... | collective-permute-start | bytes 786440 | tf_op jit(solution)/shard_map/ppermute | solution.py:281
  140.1 17.2 %copy-start = (bf16[2,256,128]{2,1,0:T(8,128)(2,1)S(1)}, bf16[2,256,128]{2,1,0:T(8,128)(2,1)}, u32[]{:S(2)}) copy-start(bf16[2,256,128]{2,1,0:T(8,128)(2,1)} %embeddings.3) | copy-start | bytes 393220
  140.8 11.7 %all-to-all-start.9 = ((bf16[32,8,128]{2,1,0:T(8,128)(2,1)}), bf16[32,8,128]{2,1,0:T(8,128)(2,1)S(1)}, u32[]{:S(2)}, u32[]{:S(2)}) async-start(bf16[32,8,128]{2,1,0:T(8,128)(2,1)} %bitcast.9), calls=%async_computation.9 | async-start | bytes 131072 | tf_op jit(solution)/shard_map/all_to_all | solution.py:47
  150.3 6.9 %collective-permute-start.4 = (bf16[2,128,256]{2,1,0:T(8,128)(2,1)S(1)}, bf16[2,128,256]{2,1,0:T(8,128)(2,1)S(1)}, u32[]{:S(2)}, u32[]{:S(2)}) collective-permute-start(bf16[2,128,256]{2,1,0:T(8,128)(2,1)S(1)} %get-tuple-element.36), channel_id=1, source_target_pairs={{0,48},{16,32},{32,16},{48,0},{1,49},{17,33},{33,17},{49,1},{2,50}... | collective-permute-start | bytes 393224 | tf_op jit(solution)/shard_map/ppermute | solution.py:281

commit v9 on v7

--- a/solution.py
+++ b/solution.py
@@ -23,6 +23,29 @@
 f32, bf16 = jnp.float32, jnp.bfloat16
 VM = pl.BlockSpec(memory_space=pltpu.VMEM)
 shape = jax.ShapeDtypeStruct
+
+
+SIZES = dict(y=NY, x=NX, c=NC, z=NZ)
+FIRST = dict(y=4, x=2, c=1, z=4)
+GATHER_FIRST = dict(z=0)
+
+
+def order(axes, first=FIRST):
+    places = [[]]
+    for a in axes:
+        places = [p + [(i + first[a]) % SIZES[a]] for p in places for i in range(SIZES[a])]
+    return places
+
+
+def exchange(x, axes, first=FIRST):
+    members = []
+    for place_ in order(axes, first):
+        at = 0
+        for a, i in zip(axes, place_):
+            at = at * SIZES[a] + i
+        members.append(at)
+    axis = axes if len(axes) > 1 else axes[0]
+    return lax.all_to_all(x, axis, 0, 0, tiled=True, axis_index_groups=[members])
 
 
 def call(kernel, outs, *args, scratch=(), flops=0, aliases={}):
@@ -176,14 +199,16 @@
     scale,
     first,
     last,
-    keep,
-    give0,
-    give1,
+    stay,
+    near,
+    give_stay,
+    give_near,
     parts,
     acc,
     wide,
     ab,
     slopes,
+    units,
 ):
     acc[...] = jnp.zeros_like(acc)
     turned = jnp.concatenate([scale[...] * (1.0 / SHARP)] * 16, 0).T
@@ -209,35 +234,33 @@
                 ).astype(bf16)
         made = jnp.dot(flat[...], slope[...], preferred_element_type=f32).astype(bf16)
         for v in range(2):
-            if half:
-                (give0, give1)[v][slot] = made[:, v * U : (v + 1) * U]
-            else:
-                keep[v, slot] = made[:, v * U : (v + 1) * U]
+            units[half, slot, v] = made[:, v * U : (v + 1) * U]
         acc[...] += jnp.dot(slope[...], rows[r].reshape(2 * U, 128), preferred_element_type=f32)
 
     for half, rows in enumerate((mine, other)):
         members(lambda r, half=half, rows=rows: group(half, r, rows))
-    for y in range(NY):
-        for z in range(NZ):
-            at = z * SUB + y * 8
-            parts[(y * NZ + z) * 8 : (y * NZ + z + 1) * 8, :] = acc[at : at + 8, :]
+    for i in range(2):
+        for v in range(2):
+            stay[v, i], near[v, i] = units[0, i, v], units[0, 2 + i, v]
+            give_stay[v, i], give_near[v, i] = units[1, i, v], units[1, 2 + i, v]
+    for i, (y, z) in enumerate(order(("y", "z"))):
+        at = (z - GATHER_FIRST["z"]) % NZ * SUB + y * 8
+        parts[i * 8 : (i + 1) * 8, :] = acc[at : at + 8, :]
 
 
 def piece_kernel(pieces, out):
     out[...] = jnp.concatenate([fold(pieces[...])] * (NY * NX), 0).astype(bf16)
 
 
-def cores_kernel(keep, got0, got1, stay, near):
-    for v, got in enumerate((got0, got1)):
-        for i in range(2):
-            stay[v, i] = (keep[v, i].astype(f32) + got[i].astype(f32)).astype(bf16)
-            near[v, i] = (keep[v, 2 + i].astype(f32) + got[2 + i].astype(f32)).astype(bf16)
-
-
-def near_kernel(stay, got, unit, far):
-    for v in range(2):
-        unit[v] = stay[v, 0].astype(f32) + got[v, 0].astype(f32)
-        far[v] = (stay[v, 1].astype(f32) + got[v, 1].astype(f32)).astype(bf16)
+def add_kernel(mine, got, out):
+    out[...] = (mine[...].astype(f32) + got[...].astype(f32)).astype(bf16)
+
+
+def near_kernel(stay, other, got, unit, far):
+    for v in range(2):
+        unit[v] = stay[v, 0].astype(f32) + other[v, 0].astype(f32) + got[v, 0].astype(f32)
+        last = stay[v, 1].astype(f32) + other[v, 1].astype(f32) + got[v, 1].astype(f32)
+        far[v] = last.astype(bf16)
 
 
 def finish_kernel(embeddings, inverse, kept, got, proto, grad_embed, grad_proto):
@@ -247,8 +270,11 @@
         unit = embeddings[v].astype(f32) * inv
         grad_embed[v] = inv * (grad - unit * jnp.sum(unit * grad, -1, keepdims=True))
     for x in range(NX):
-        blocks = [proto[c].astype(f32).reshape(NY, NX, 8, 128)[:, x] for c in range(NC)]
-        whole = jnp.concatenate([b.reshape(SUB, 128) for b in blocks], 0)
+        blocks = []
+        for c in range(NC):
+            b = proto[c].astype(f32).reshape(NY, NX, 8, 128)[:, (x - FIRST["x"]) % NX]
+            blocks += [b[(y - FIRST["y"]) % NY] for y in range(NY)]
+        whole = jnp.concatenate(blocks, 0)
         grad_proto[:, x * NC * SUB : (x + 1) * NC * SUB] = whole.T
 
 
@@ -279,7 +305,7 @@
         ],
         compiler_params=pltpu.CompilerParams(vmem_limit_bytes=20 * 1024 * 1024),
     )(*(pltpu.with_memory_space_constraint(a, pltpu.HBM) for a in (embeddings, prototypes)))
-    proto = lax.all_to_all(proto, "z", 0, 0).reshape(COLS, 128)
+    proto = exchange(proto, ("z",), GATHER_FIRST).reshape(COLS, 128)
     others = [swap(unit, "x", NX, r) for r in range(1, NX)]
     flat = call(flat_kernel, shape((128, COLS), bf16), proto, flops=1 << 36)
     others, proto, flat = lax.optimization_barrier((others, proto, flat))
@@ -304,7 +330,7 @@
     )
     first = None
     for sweep in range(ITERS):
-        columns = lax.all_to_all(columns, ("y", "z"), 0, 0, tiled=True)
+        columns = exchange(columns, ("y", "z"))
         lines = shape((G, 4 * G if sweep == 0 else 2 * G, U), bf16)
         mass = call(
             functools.partial(rows_kernel, sweep),
@@ -316,14 +342,14 @@
         )
         if sweep == ITERS - 1:
             mass, scale = mass
-        mass = lax.all_to_all(mass, ("x", "c"), 0, 0)
+        mass = exchange(mass, ("x", "c"))
         first = mass if first is None else first
         if sweep < ITERS - 1:
             columns = call(columns_kernel, sums, masses, mass, scratch=[acc])
-    half, part = shape((2, NX, 128, U), bf16), shape((NX, 128, U), bf16)
-    keep, give0, give1, parts = call(
+    half = shape((2, 2, 128, U), bf16)
+    stay, near, give_stay, give_near, parts = call(
         slopes_kernel,
-        (half, part, part, shape((COLS, 128), f32)),
+        (half, half, half, half, shape((COLS, 128), f32)),
         mine,
         other,
         flat,
@@ -337,17 +363,18 @@
             acc,
             pltpu.VMEM((4 * G, U), f32),
             pltpu.VMEM((2, COLS, 2 * U), bf16),
+            pltpu.VMEM((NC, NX, 2, 128, U), bf16),
         ],
     )
-    pieces = lax.all_to_all(parts, ("y", "z"), 0, 0, tiled=True)
-    half = shape((2, 2, 128, U), bf16)
-    stay, near = call(cores_kernel, (half, half), keep, *(swap(g, "c", NC, 1) for g in (give0, give1)))
+    pieces = exchange(parts, ("y", "z"))
+    near = call(add_kernel, half, near, swap(give_near, "c", NC, 1))
+    other = swap(give_stay, "c", NC, 1)
     near = swap(near, "x", NX, 1)
     pieces = call(piece_kernel, shape((NY * NX * 8, 128), bf16), pieces, flops=1 << 36)
-    whole = lax.all_to_all(pieces, ("y", "x"), 0, 0, tiled=True)
+    whole = exchange(pieces, ("y", "x"))
     whole = lax.all_gather(whole, "c", axis=0)
     unit, far = call(
-        near_kernel, (shape((2, 128, U), f32), shape((2, 128, U), bf16)), stay, near
+        near_kernel, (shape((2, 128, U), f32), shape((2, 128, U), bf16)), stay, other, near
     )
     far = swap(far, "x", NX, 3)
     return tuple(

time: 165 us -> 157 us (0.952)
  starting transfers between devices: 45.3 us -> 57 us
  blocking collectives: 89.3 us -> 78.1 us
  waiting for transfers between devices: 14.6 us -> 5.45 us
    all_to_all x3, starting transfers between devices: 20.9 us -> 34 us  [exchange(): lax.all_to_all(x, axis, 0, 0, tiled=True, axis_index_groups=[members])]
    all_to_all x6, blocking collectives: 85.1 us -> 74.7 us  [exchange(): lax.all_to_all(x, axis, 0, 0, tiled=True, axis_index_groups=[members])]
    all_to_all x3, waiting for transfers between devices: 8.95 us -> 0.01 us  [exchange(): lax.all_to_all(x, axis, 0, 0, tiled=True, axis_index_groups=[members])]
  transfers between devices with their start and end apart: 11 -> 11, of which waited for: 6 -> 4; matrix products, arithmetic and copies ran while one was open for 0% -> 0% of each run, Pallas kernels for 1% -> 1%
where the time goes in v9:
time: 157 us; the launch traced here: 156 us
  blocking collectives  78.1 us (50%)
  starting transfers between devices  57 us (36%)
  Pallas kernels  14.4 us (9%)
  waiting for transfers between devices  5.45 us (3%)
    all_to_all x6, blocking collectives, exchange(): lax.all_to_all(x, axis, 0, 0, tiled=True, axis_index_groups=[members])  74.7 us
    all_to_all x3, starting transfers between devices, exchange(): lax.all_to_all(x, axis, 0, 0, tiled=True, axis_index_groups=[members])  34 us
    ppermute x8, starting transfers between devices, swap(): return lax.ppermute(x, axis, [(i, i ^ bit) for i in range(n)])  23 us
    pallas_call x13, Pallas kernels, call(): pl.pallas_call(kernel, out_shape=outs, in_specs=[VM] * len(args), out_spe...  12.6 us
    ppermute x8, waiting for transfers between devices, swap(): return lax.ppermute(x, axis, [(i, i ^ bit) for i in range(n)])  5.44 us
    all_gather x1, blocking collectives, body(): whole = lax.all_gather(whole, 'c', axis=0)  3.39 us
  transfers between devices with their start and end apart: 11, of which 4 were waited for; matrix products, arithmetic and copies ran while one was open for 0% of the time, Pallas kernels for 1%

profile of v9, /device:TPU:1, one launch (start us, length us, event | category | flops | bytes accessed | tf_op | source)
XLA Modules:
  0.0 155.9 jit_solution(17706330103834248339)
XLA Ops:
  0.6 1.8 %shard_map.41 = (bf16[2,256,128]{2,1,0:T(8,128)(2,1)S(1)}, f32[2,256,1]{2,1,0:T(8,128)S(1)}, bf16[8,64,128]{2,1,0:T(8,128)(2,1)}) custom-call(bf16[2,256,128]{2,1,0:T(8,128)(2,1)} %embeddings.3, bf16[128,512]{1,0:T(8,128)(2,1)} %prototypes.1), custom_call_target="tpu_custom_call" | custom-call | tf_op jit(solution)/shard_map/pallas_call | solution.py:290
  2.4 10.9 %all-to-all-start = ((bf16[8,64,128]{2,1,0:T(8,128)(2,1)}), bf16[8,64,128]{2,1,0:T(8,128)(2,1)S(1)}, u32[]{:S(2)}, u32[]{:S(2)}) async-start(bf16[8,64,128]{2,1,0:T(8,128)(2,1)} %get-tuple-element.29), calls=%async_computation | async-start | bytes 262144 | tf_op jit(solution)/shard_map/all_to_all | solution.py:48
  13.3 4.4 %collective-permute-start.2 = (bf16[2,256,128]{2,1,0:T(8,128)(2,1)S(1)}, bf16[2,256,128]{2,1,0:T(8,128)(2,1)S(1)}, u32[]{:S(2)}, u32[]{:S(2)}) collective-permute-start(bf16[2,256,128]{2,1,0:T(8,128)(2,1)S(1)} %get-tuple-element.28), channel_id=1, source_target_pairs={{0,48},{16,32},{32,16},{48,0},{1,49},{17,33},{33,17},{49,1},{2,50}... | collective-permute-start | bytes 393224 | tf_op jit(solution)/shard_map/ppermute | solution.py:282
  17.7 2.4 %collective-permute-start.1 = (bf16[2,256,128]{2,1,0:T(8,128)(2,1)S(1)}, bf16[2,256,128]{2,1,0:T(8,128)(2,1)S(1)}, u32[]{:S(2)}, u32[]{:S(2)}) collective-permute-start(bf16[2,256,128]{2,1,0:T(8,128)(2,1)S(1)} %get-tuple-element.28), channel_id=1, source_target_pairs={{0,32},{16,48},{32,0},{48,16},{1,33},{17,49},{33,1},{49,17},{2,34}... | collective-permute-start | bytes 393224 | tf_op jit(solution)/shard_map/ppermute | solution.py:282
  20.1 2.2 %collective-permute-start = (bf16[2,256,128]{2,1,0:T(8,128)(2,1)S(1)}, bf16[2,256,128]{2,1,0:T(8,128)(2,1)S(1)}, u32[]{:S(2)}, u32[]{:S(2)}) collective-permute-start(bf16[2,256,128]{2,1,0:T(8,128)(2,1)S(1)} %get-tuple-element.28), channel_id=1, source_target_pairs={{0,16},{16,0},{32,48},{48,32},{1,17},{17,1},{33,49},{49,33},{2,18}... | collective-permute-start | bytes 393224 | tf_op jit(solution)/shard_map/ppermute | solution.py:282
  22.4 2.5 %collective-permute-done.1 = bf16[2,256,128]{2,1,0:T(8,128)(2,1)S(1)} collective-permute-done((bf16[2,256,128]{2,1,0:T(8,128)(2,1)S(1)}, bf16[2,256,128]{2,1,0:T(8,128)(2,1)S(1)}, u32[]{:S(2)}, u32[]{:S(2)}) %collective-permute-start.1) | collective-permute-done | bytes 131104 | tf_op jit(solution)/shard_map/ppermute | solution.py:282
  26.2 4.3 %collective-permute-start.3 = (bf16[4,2,256,128]{3,2,1,0:T(8,128)(2,1)S(1)}, bf16[4,2,256,128]{3,2,1,0:T(8,128)(2,1)S(1)}, u32[]{:S(2)}, u32[]{:S(2)}) collective-permute-start(bf16[4,2,256,128]{3,2,1,0:T(8,128)(2,1)S(1)} %pad_maximum_fusion.rows.mine), channel_id=1, source_target_pairs={{0,8},{8,0},{1,9},{9,1},{2,10},{10,2},{3,11},{11,3},{4,12},{12,4},... | collective-permute-start | bytes 1572872 | tf_op jit(solution)/shard_map/ppermute | solution.py:282
  32.0 1.2 shard_map.44
  33.2 17.9 %all_to_all.73 = bf16[64,8,128]{2,1,0:T(8,128)(2,1)S(1)} all-to-all(bf16[64,8,128]{2,1,0:T(8,128)(2,1)S(1)} %bitcast.24), channel_id=1, replica_groups={{260,261,262,263,256,257,258,259,324,325,326,327,320,321,322,323,388,38..., dimensions={0} | all-to-all | bytes 262144 | tf_op jit(solution)/shard_map/all_to_all | solution.py:48
  52.2 8.1 %all_to_all.74.rowmass.first = bf16[8,32,256]{2,1,0:T(8,128)(2,1)S(1)} all-to-all(bf16[8,32,256]{2,1,0:T(8,128)(2,1)S(1)} %shard_map.45), channel_id=1, replica_groups={{40,32,56,48,8,0,24,16},{41,33,57,49,9,1,25,17},{42,34,58,50,10,2,26,18..., dimensions={0} | all-to-all | bytes 262144 | tf_op jit(solution)/shard_map/all_to_all | solution.py:48
  61.1 16.4 %all_to_all.75 = bf16[64,8,128]{2,1,0:T(8,128)(2,1)S(1)} all-to-all(bf16[64,8,128]{2,1,0:T(8,128)(2,1)S(1)} %bitcast.22), channel_id=1, replica_groups={{260,261,262,263,256,257,258,259,324,325,326,327,320,321,322,323,388,38..., dimensions={0} | all-to-all | bytes 262144 | tf_op jit(solution)/shard_map/all_to_all | solution.py:48
  78.6 7.9 %all_to_all.76.rowmass = bf16[8,16,256]{2,1,0:T(8,128)(2,1)S(1)} all-to-all(bf16[8,16,256]{2,1,0:T(8,128)(2,1)S(1)} %shard_map.47), channel_id=1, replica_groups={{40,32,56,48,8,0,24,16},{41,33,57,49,9,1,25,17},{42,34,58,50,10,2,26,18..., dimensions={0} | all-to-all | bytes 131072 | tf_op jit(solution)/shard_map/all_to_all | solution.py:48
  87.3 16.4 %all_to_all.77 = bf16[64,8,128]{2,1,0:T(8,128)(2,1)S(1)} all-to-all(bf16[64,8,128]{2,1,0:T(8,128)(2,1)S(1)} %bitcast.21), channel_id=1, replica_groups={{260,261,262,263,256,257,258,259,324,325,326,327,320,321,322,323,388,38..., dimensions={0} | all-to-all | bytes 262144 | tf_op jit(solution)/shard_map/all_to_all | solution.py:48
  104.8 8.0 %all_to_all.78.last = bf16[8,16,256]{2,1,0:T(8,128)(2,1)S(1)} all-to-all(bf16[8,16,256]{2,1,0:T(8,128)(2,1)S(1)} %get-tuple-element.44), channel_id=1, replica_groups={{40,32,56,48,8,0,24,16},{41,33,57,49,9,1,25,17},{42,34,58,50,10,2,26,18..., dimensions={0} | all-to-all | bytes 131072 | tf_op jit(solution)/shard_map/all_to_all | solution.py:48
  112.9 3.2 %shard_map.50 = (bf16[2,2,128,256]{3,2,1,0:T(8,128)(2,1)S(1)}, bf16[2,2,128,256]{3,2,1,0:T(8,128)(2,1)S(1)}, bf16[2,2,128,256]{3,2,1,0:T(8,128)(2,1)S(1)}, bf16[...) custom-call(bf16[4,2,256,128]{3,2,1,0:T(8,128)(2,1)S(1)} %pad_maximum_fusion.rows.mine, ...), custom_call_target="tpu_custom_call" | custom-call | tf_op jit(solution)/shard_map/pallas_call | solution.py:53
  116.1 13.7 %all-to-all-start.7 = ((f32[64,8,128]{2,1,0:T(8,128)}), f32[64,8,128]{2,1,0:T(8,128)S(1)}, u32[]{:S(2)}, u32[]{:S(2)}) async-start(f32[64,8,128]{2,1,0:T(8,128)} %bitcast.11), calls=%async_computation.7 | async-start | bytes 524288 | tf_op jit(solution)/shard_map/all_to_all | solution.py:48
  129.8 2.6 %collective-permute-start.5 = (bf16[2,2,128,256]{3,2,1,0:T(8,128)(2,1)S(1)}, bf16[2,2,128,256]{3,2,1,0:T(8,128)(2,1)S(1)}, u32[]{:S(2)}, u32[]{:S(2)}) collective-permute-start(bf16[2,2,128,256]{3,2,1,0:T(8,128)(2,1)S(1)} %get-tuple-element.48), channel_id=1, source_target_pairs={{0,8},{8,0},{1,9},{9,1},{2,10},{10,2},{3,11},{11,3},{4,12},{12,4},... | collective-permute-start | bytes 786440 | tf_op jit(solution)/shard_map/ppermute | solution.py:282
  132.4 1.9 %collective-permute-start.4 = (bf16[2,2,128,256]{3,2,1,0:T(8,128)(2,1)S(1)}, bf16[2,2,128,256]{3,2,1,0:T(8,128)(2,1)S(1)}, u32[]{:S(2)}, u32[]{:S(2)}) collective-permute-start(bf16[2,2,128,256]{3,2,1,0:T(8,128)(2,1)S(1)} %get-tuple-element.46), channel_id=1, source_target_pairs={{0,8},{8,0},{1,9},{9,1},{2,10},{10,2},{3,11},{11,3},{4,12},{12,4},... | collective-permute-start | bytes 786440 | tf_op jit(solution)/shard_map/ppermute | solution.py:282
  134.4 3.1 %collective-permute-start.6 = (bf16[2,2,128,256]{3,2,1,0:T(8,128)(2,1)S(1)}, bf16[2,2,128,256]{3,2,1,0:T(8,128)(2,1)S(1)}, u32[]{:S(2)}, u32[]{:S(2)}) collective-permute-start(bf16[2,2,128,256]{3,2,1,0:T(8,128)(2,1)S(1)} %shard_map.51), channel_id=1, source_target_pairs={{0,16},{16,0},{32,48},{48,32},{1,17},{17,1},{33,49},{49,33},{2,18}... | collective-permute-start | bytes 786440 | tf_op jit(solution)/shard_map/ppermute | solution.py:282
  138.2 9.4 %all-to-all-start.8 = ((bf16[32,8,128]{2,1,0:T(8,128)(2,1)}), bf16[32,8,128]{2,1,0:T(8,128)(2,1)S(1)}, u32[]{:S(2)}, u32[]{:S(2)}) async-start(bf16[32,8,128]{2,1,0:T(8,128)(2,1)} %bitcast.13), calls=%async_computation.8 | async-start | bytes 131072 | tf_op jit(solution)/shard_map/all_to_all | solution.py:48
  147.7 2.2 %collective-permute-start.7 = (bf16[2,128,256]{2,1,0:T(8,128)(2,1)S(1)}, bf16[2,128,256]{2,1,0:T(8,128)(2,1)S(1)}, u32[]{:S(2)}, u32[]{:S(2)}) collective-permute-start(bf16[2,128,256]{2,1,0:T(8,128)(2,1)S(1)} %get-tuple-element.50), channel_id=1, source_target_pairs={{0,48},{16,32},{32,16},{48,0},{1,49},{17,33},{33,17},{49,1},{2,50}... | collective-permute-start | bytes 393224 | tf_op jit(solution)/shard_map/ppermute | solution.py:282
  150.0 3.4 %all_gather.7.proto = bf16[2,256,128]{2,1,0:T(8,128)(2,1)S(1)} all-gather(bf16[1,256,128]{2,1,0:T(8,128)(2,1)S(1)} %bitcast.26), channel_id=1, replica_groups=mesh['y'=8,'x'=4,'c'=2,'z'=8] {'c'}, dimensions={0}, use_global_device_ids=true | all-gather | bytes 196608 | tf_op jit(solution)/shard_map/all_gather | solution.py:375
  153.3 1.3 collective-permute-done.7.got
  154.7 1.3 shard_map.54
  (22 shorter events, 8.7 us)
Async XLA Ops:
  2.4 19.9 %all-to-all-start = ((bf16[8,64,128]{2,1,0:T(8,128)(2,1)}), bf16[8,64,128]{2,1,0:T(8,128)(2,1)S(1)}, u32[]{:S(2)}, u32[]{:S(2)}) async-start(bf16[8,64,128]{2,1,0:T(8,128)(2,1)} %get-tuple-element.29), calls=%async_computation | async-start | bytes 262144 | tf_op jit(solution)/shard_map/all_to_all | solution.py:48
  13.3 9.1 %collective-permute-start.2 = (bf16[2,256,128]{2,1,0:T(8,128)(2,1)S(1)}, bf16[2,256,128]{2,1,0:T(8,128)(2,1)S(1)}, u32[]{:S(2)}, u32[]{:S(2)}) collective-permute-start(bf16[2,256,128]{2,1,0:T(8,128)(2,1)S(1)} %get-tuple-element.28), channel_id=1, source_target_pairs={{0,48},{16,32},{32,16},{48,0},{1,49},{17,33},{33,17},{49,1},{2,50}... | collective-permute-start | bytes 393224 | tf_op jit(solution)/shard_map/ppermute | solution.py:282
  17.7 7.2 %collective-permute-start.1 = (bf16[2,256,128]{2,1,0:T(8,128)(2,1)S(1)}, bf16[2,256,128]{2,1,0:T(8,128)(2,1)S(1)}, u32[]{:S(2)}, u32[]{:S(2)}) collective-permute-start(bf16[2,256,128]{2,1,0:T(8,128)(2,1)S(1)} %get-tuple-element.28), channel_id=1, source_target_pairs={{0,32},{16,48},{32,0},{48,16},{1,33},{17,49},{33,1},{49,17},{2,34}... | collective-permute-start | bytes 393224 | tf_op jit(solution)/shard_map/ppermute | solution.py:282
  20.1 6.0 %collective-permute-start = (bf16[2,256,128]{2,1,0:T(8,128)(2,1)S(1)}, bf16[2,256,128]{2,1,0:T(8,128)(2,1)S(1)}, u32[]{:S(2)}, u32[]{:S(2)}) collective-permute-start(bf16[2,256,128]{2,1,0:T(8,128)(2,1)S(1)} %get-tuple-element.28), channel_id=1, source_target_pairs={{0,16},{16,0},{32,48},{48,32},{1,17},{17,1},{33,49},{49,33},{2,18}... | collective-permute-start | bytes 393224 | tf_op jit(solution)/shard_map/ppermute | solution.py:282
  26.2 5.8 %collective-permute-start.3 = (bf16[4,2,256,128]{3,2,1,0:T(8,128)(2,1)S(1)}, bf16[4,2,256,128]{3,2,1,0:T(8,128)(2,1)S(1)}, u32[]{:S(2)}, u32[]{:S(2)}) collective-permute-start(bf16[4,2,256,128]{3,2,1,0:T(8,128)(2,1)S(1)} %pad_maximum_fusion.rows.mine), channel_id=1, source_target_pairs={{0,8},{8,0},{1,9},{9,1},{2,10},{10,2},{3,11},{11,3},{4,12},{12,4},... | collective-permute-start | bytes 1572872 | tf_op jit(solution)/shard_map/ppermute | solution.py:282
  116.1 21.4 %all-to-all-start.7 = ((f32[64,8,128]{2,1,0:T(8,128)}), f32[64,8,128]{2,1,0:T(8,128)S(1)}, u32[]{:S(2)}, u32[]{:S(2)}) async-start(f32[64,8,128]{2,1,0:T(8,128)} %bitcast.11), calls=%async_computation.7 | async-start | bytes 524288 | tf_op jit(solution)/shard_map/all_to_all | solution.py:48
  129.8 4.5 %collective-permute-start.5 = (bf16[2,2,128,256]{3,2,1,0:T(8,128)(2,1)S(1)}, bf16[2,2,128,256]{3,2,1,0:T(8,128)(2,1)S(1)}, u32[]{:S(2)}, u32[]{:S(2)}) collective-permute-start(bf16[2,2,128,256]{3,2,1,0:T(8,128)(2,1)S(1)} %get-tuple-element.48), channel_id=1, source_target_pairs={{0,8},{8,0},{1,9},{9,1},{2,10},{10,2},{3,11},{11,3},{4,12},{12,4},... | collective-permute-start | bytes 786440 | tf_op jit(solution)/shard_map/ppermute | solution.py:282
  132.4 15.2 %collective-permute-start.4 = (bf16[2,2,128,256]{3,2,1,0:T(8,128)(2,1)S(1)}, bf16[2,2,128,256]{3,2,1,0:T(8,128)(2,1)S(1)}, u32[]{:S(2)}, u32[]{:S(2)}) collective-permute-start(bf16[2,2,128,256]{3,2,1,0:T(8,128)(2,1)S(1)} %get-tuple-element.46), channel_id=1, source_target_pairs={{0,8},{8,0},{1,9},{9,1},{2,10},{10,2},{3,11},{11,3},{4,12},{12,4},... | collective-permute-start | bytes 786440 | tf_op jit(solution)/shard_map/ppermute | solution.py:282
  134.4 13.2 %collective-permute-start.6 = (bf16[2,2,128,256]{3,2,1,0:T(8,128)(2,1)S(1)}, bf16[2,2,128,256]{3,2,1,0:T(8,128)(2,1)S(1)}, u32[]{:S(2)}, u32[]{:S(2)}) collective-permute-start(bf16[2,2,128,256]{3,2,1,0:T(8,128)(2,1)S(1)} %shard_map.51), channel_id=1, source_target_pairs={{0,16},{16,0},{32,48},{48,32},{1,17},{17,1},{33,49},{49,33},{2,18}... | collective-permute-start | bytes 786440 | tf_op jit(solution)/shard_map/ppermute | solution.py:282
  137.5 17.2 %copy-start = (bf16[2,256,128]{2,1,0:T(8,128)(2,1)S(1)}, bf16[2,256,128]{2,1,0:T(8,128)(2,1)}, u32[]{:S(2)}) copy-start(bf16[2,256,128]{2,1,0:T(8,128)(2,1)} %embeddings.3) | copy-start | bytes 393220
  138.2 11.7 %all-to-all-start.8 = ((bf16[32,8,128]{2,1,0:T(8,128)(2,1)}), bf16[32,8,128]{2,1,0:T(8,128)(2,1)S(1)}, u32[]{:S(2)}, u32[]{:S(2)}) async-start(bf16[32,8,128]{2,1,0:T(8,128)(2,1)} %bitcast.13), calls=%async_computation.8 | async-start | bytes 131072 | tf_op jit(solution)/shard_map/all_to_all | solution.py:48
  147.7 6.9 %collective-permute-start.7 = (bf16[2,128,256]{2,1,0:T(8,128)(2,1)S(1)}, bf16[2,128,256]{2,1,0:T(8,128)(2,1)S(1)}, u32[]{:S(2)}, u32[]{:S(2)}) collective-permute-start(bf16[2,128,256]{2,1,0:T(8,128)(2,1)S(1)} %get-tuple-element.50), channel_id=1, source_target_pairs={{0,48},{16,32},{32,16},{48,0},{1,49},{17,33},{33,17},{49,1},{2,50}... | collective-permute-start | bytes 393224 | tf_op jit(solution)/shard_map/ppermute | solution.py:282

commit v10 on v9

--- a/solution.py
+++ b/solution.py
@@ -26,7 +26,7 @@
 
 
 SIZES = dict(y=NY, x=NX, c=NC, z=NZ)
-FIRST = dict(y=4, x=2, c=1, z=4)
+FIRST = dict(y=4, x=2, c=1, z=5)
 GATHER_FIRST = dict(z=0)
 
 
@@ -69,16 +69,17 @@
 def prepare_kernel(
     embeddings, prototypes, unit, inverse, proto, users, columns, turned, copies, sems
 ):
+    j = lax.axis_index("x") * NC + lax.axis_index("c")
+    near = prototypes.at[:, pl.ds(pl.multiple_of(lax.div(j, 2) * 128, 128), 128)]
     fetch = [
         pltpu.make_async_copy(src, dst, sems.at[i])
-        for i, (src, dst) in enumerate(((prototypes, columns), (embeddings, users)))
+        for i, (src, dst) in enumerate(((near, columns), (embeddings, users)))
     ]
     for copy in fetch:
         copy.start()
     fetch[0].wait()
     turned[...] = columns[...].astype(f32).T
-    j = lax.axis_index("x") * NC + lax.axis_index("c")
-    own = turned[pl.ds(pl.multiple_of(j * SUB, SUB), SUB), :]
+    own = turned[pl.ds(pl.multiple_of(lax.rem(j, 2) * SUB, SUB), SUB), :]
     own = (own * lax.rsqrt(jnp.sum(own * own, -1, keepdims=True) + EPS)).astype(bf16)
     for i in range(NZ):
         copies[i] = own
@@ -156,7 +157,7 @@
             cc = jnp.concatenate([cc, cc], 1)
             return tuple(acc[g] + masses[g, v, pl.ds(at, 8), :] * cc for g in range(G))
 
-        acc = lax.fori_loop(0, COLS // 8, eight, (jnp.zeros((8, U), f32),) * G, unroll=16)
+        acc = lax.fori_loop(0, COLS // 8, eight, (jnp.zeros((8, U), f32),) * G, unroll=32)
         lines += [jnp.sum(a, 0, keepdims=True) for a in acc]
     if soft is not None:
         lines.append(soft[...])
@@ -182,7 +183,7 @@
             acc[pl.ds(v * COLS + at, 8), :] = total[:, :128] + total[:, 128:]
             return 0
 
-        lax.fori_loop(0, COLS // 8, eight, 0, unroll=16)
+        lax.fori_loop(0, COLS // 8, eight, 0, unroll=32)
     send_columns(acc, columns)
 
 
@@ -298,8 +299,8 @@
         out_specs=(VM, VM, pl.BlockSpec(memory_space=pl.ANY)),
         scratch_shapes=[
             pltpu.VMEM((2, U, 128), bf16),
-            pltpu.VMEM((128, 512), bf16),
-            pltpu.VMEM((512, 128), f32),
+            pltpu.VMEM((128, 128), bf16),
+            pltpu.VMEM((128, 128), f32),
             pltpu.VMEM((NZ, SUB, 128), bf16),
             pltpu.SemaphoreType.DMA((3,)),
         ],

time: 157 us -> 156 us (level)
  no operation moved by 1% of the time
where the time goes in v10:
time: 156 us; the launch traced here: 155 us
  blocking collectives  78.6 us (50%)
  starting transfers between devices  56.2 us (36%)
  Pallas kernels  14.2 us (9%)
  waiting for transfers between devices  4.92 us (3%)
    all_to_all x6, blocking collectives, exchange(): lax.all_to_all(x, axis, 0, 0, tiled=True, axis_index_groups=[members])  74.6 us
    all_to_all x3, starting transfers between devices, exchange(): lax.all_to_all(x, axis, 0, 0, tiled=True, axis_index_groups=[members])  33.2 us
    ppermute x8, starting transfers between devices, swap(): return lax.ppermute(x, axis, [(i, i ^ bit) for i in range(n)])  23 us
    pallas_call x13, Pallas kernels, call(): pl.pallas_call(kernel, out_shape=outs, in_specs=[VM] * len(args), out_spe...  12.5 us
    ppermute x8, waiting for transfers between devices, swap(): return lax.ppermute(x, axis, [(i, i ^ bit) for i in range(n)])  4.91 us
    all_gather x1, blocking collectives, body(): whole = lax.all_gather(whole, 'c', axis=0)  3.93 us
  transfers between devices with their start and end apart: 11, of which 4 were waited for; matrix products, arithmetic and copies ran while one was open for 0% of the time, Pallas kernels for 1%

profile of v10, /device:TPU:1, one launch (start us, length us, event | category | flops | bytes accessed | tf_op | source)
XLA Modules:
  0.0 154.8 jit_solution(3351238987942151162)
XLA Ops:
  0.6 1.7 %shard_map.41 = (bf16[2,256,128]{2,1,0:T(8,128)(2,1)S(1)}, f32[2,256,1]{2,1,0:T(8,128)S(1)}, bf16[8,64,128]{2,1,0:T(8,128)(2,1)}) custom-call(bf16[2,256,128]{2,1,0:T(8,128)(2,1)} %embeddings.3, bf16[128,512]{1,0:T(8,128)(2,1)} %prototypes.1), custom_call_target="tpu_custom_call" | custom-call | tf_op jit(solution)/shard_map/pallas_call | solution.py:291
  2.3 10.9 %all-to-all-start = ((bf16[8,64,128]{2,1,0:T(8,128)(2,1)}), bf16[8,64,128]{2,1,0:T(8,128)(2,1)S(1)}, u32[]{:S(2)}, u32[]{:S(2)}) async-start(bf16[8,64,128]{2,1,0:T(8,128)(2,1)} %get-tuple-element.29), calls=%async_computation | async-start | bytes 262144 | tf_op jit(solution)/shard_map/all_to_all | solution.py:48
  13.2 4.4 %collective-permute-start.2 = (bf16[2,256,128]{2,1,0:T(8,128)(2,1)S(1)}, bf16[2,256,128]{2,1,0:T(8,128)(2,1)S(1)}, u32[]{:S(2)}, u32[]{:S(2)}) collective-permute-start(bf16[2,256,128]{2,1,0:T(8,128)(2,1)S(1)} %get-tuple-element.28), channel_id=1, source_target_pairs={{0,48},{16,32},{32,16},{48,0},{1,49},{17,33},{33,17},{49,1},{2,50}... | collective-permute-start | bytes 393224 | tf_op jit(solution)/shard_map/ppermute | solution.py:283
  17.6 2.4 %collective-permute-start.1 = (bf16[2,256,128]{2,1,0:T(8,128)(2,1)S(1)}, bf16[2,256,128]{2,1,0:T(8,128)(2,1)S(1)}, u32[]{:S(2)}, u32[]{:S(2)}) collective-permute-start(bf16[2,256,128]{2,1,0:T(8,128)(2,1)S(1)} %get-tuple-element.28), channel_id=1, source_target_pairs={{0,32},{16,48},{32,0},{48,16},{1,33},{17,49},{33,1},{49,17},{2,34}... | collective-permute-start | bytes 393224 | tf_op jit(solution)/shard_map/ppermute | solution.py:283
  20.0 2.2 %collective-permute-start = (bf16[2,256,128]{2,1,0:T(8,128)(2,1)S(1)}, bf16[2,256,128]{2,1,0:T(8,128)(2,1)S(1)}, u32[]{:S(2)}, u32[]{:S(2)}) collective-permute-start(bf16[2,256,128]{2,1,0:T(8,128)(2,1)S(1)} %get-tuple-element.28), channel_id=1, source_target_pairs={{0,16},{16,0},{32,48},{48,32},{1,17},{17,1},{33,49},{49,33},{2,18}... | collective-permute-start | bytes 393224 | tf_op jit(solution)/shard_map/ppermute | solution.py:283
  22.3 2.5 %collective-permute-done.1 = bf16[2,256,128]{2,1,0:T(8,128)(2,1)S(1)} collective-permute-done((bf16[2,256,128]{2,1,0:T(8,128)(2,1)S(1)}, bf16[2,256,128]{2,1,0:T(8,128)(2,1)S(1)}, u32[]{:S(2)}, u32[]{:S(2)}) %collective-permute-start.1) | collective-permute-done | bytes 131104 | tf_op jit(solution)/shard_map/ppermute | solution.py:283
  24.8 1.2 collective-permute-done
  26.1 4.3 %collective-permute-start.3 = (bf16[4,2,256,128]{3,2,1,0:T(8,128)(2,1)S(1)}, bf16[4,2,256,128]{3,2,1,0:T(8,128)(2,1)S(1)}, u32[]{:S(2)}, u32[]{:S(2)}) collective-permute-start(bf16[4,2,256,128]{3,2,1,0:T(8,128)(2,1)S(1)} %pad_maximum_fusion.rows.mine), channel_id=1, source_target_pairs={{0,8},{8,0},{1,9},{9,1},{2,10},{10,2},{3,11},{11,3},{4,12},{12,4},... | collective-permute-start | bytes 1572872 | tf_op jit(solution)/shard_map/ppermute | solution.py:283
  31.9 1.2 shard_map.44
  33.1 17.6 %all_to_all.73 = bf16[64,8,128]{2,1,0:T(8,128)(2,1)S(1)} all-to-all(bf16[64,8,128]{2,1,0:T(8,128)(2,1)S(1)} %bitcast.24), channel_id=1, replica_groups={{261,262,263,256,257,258,259,260,325,326,327,320,321,322,323,324,389,39..., dimensions={0} | all-to-all | bytes 262144 | tf_op jit(solution)/shard_map/all_to_all | solution.py:48
  51.8 8.3 %all_to_all.74.rowmass.first = bf16[8,32,256]{2,1,0:T(8,128)(2,1)S(1)} all-to-all(bf16[8,32,256]{2,1,0:T(8,128)(2,1)S(1)} %shard_map.45), channel_id=1, replica_groups={{40,32,56,48,8,0,24,16},{41,33,57,49,9,1,25,17},{42,34,58,50,10,2,26,18..., dimensions={0} | all-to-all | bytes 262144 | tf_op jit(solution)/shard_map/all_to_all | solution.py:48
  60.8 16.0 %all_to_all.75 = bf16[64,8,128]{2,1,0:T(8,128)(2,1)S(1)} all-to-all(bf16[64,8,128]{2,1,0:T(8,128)(2,1)S(1)} %bitcast.22), channel_id=1, replica_groups={{261,262,263,256,257,258,259,260,325,326,327,320,321,322,323,324,389,39..., dimensions={0} | all-to-all | bytes 262144 | tf_op jit(solution)/shard_map/all_to_all | solution.py:48
  77.9 8.3 %all_to_all.76.rowmass = bf16[8,16,256]{2,1,0:T(8,128)(2,1)S(1)} all-to-all(bf16[8,16,256]{2,1,0:T(8,128)(2,1)S(1)} %shard_map.47), channel_id=1, replica_groups={{40,32,56,48,8,0,24,16},{41,33,57,49,9,1,25,17},{42,34,58,50,10,2,26,18..., dimensions={0} | all-to-all | bytes 131072 | tf_op jit(solution)/shard_map/all_to_all | solution.py:48
  87.0 16.2 %all_to_all.77 = bf16[64,8,128]{2,1,0:T(8,128)(2,1)S(1)} all-to-all(bf16[64,8,128]{2,1,0:T(8,128)(2,1)S(1)} %bitcast.21), channel_id=1, replica_groups={{261,262,263,256,257,258,259,260,325,326,327,320,321,322,323,324,389,39..., dimensions={0} | all-to-all | bytes 262144 | tf_op jit(solution)/shard_map/all_to_all | solution.py:48
  104.3 8.2 %all_to_all.78.last = bf16[8,16,256]{2,1,0:T(8,128)(2,1)S(1)} all-to-all(bf16[8,16,256]{2,1,0:T(8,128)(2,1)S(1)} %get-tuple-element.44), channel_id=1, replica_groups={{40,32,56,48,8,0,24,16},{41,33,57,49,9,1,25,17},{42,34,58,50,10,2,26,18..., dimensions={0} | all-to-all | bytes 131072 | tf_op jit(solution)/shard_map/all_to_all | solution.py:48
  112.5 3.2 %shard_map.50 = (bf16[2,2,128,256]{3,2,1,0:T(8,128)(2,1)S(1)}, bf16[2,2,128,256]{3,2,1,0:T(8,128)(2,1)S(1)}, bf16[2,2,128,256]{3,2,1,0:T(8,128)(2,1)S(1)}, bf16[...) custom-call(bf16[4,2,256,128]{3,2,1,0:T(8,128)(2,1)S(1)} %pad_maximum_fusion.rows.mine, ...), custom_call_target="tpu_custom_call" | custom-call | tf_op jit(solution)/shard_map/pallas_call | solution.py:53
  115.7 12.9 %all-to-all-start.7 = ((f32[64,8,128]{2,1,0:T(8,128)}), f32[64,8,128]{2,1,0:T(8,128)S(1)}, u32[]{:S(2)}, u32[]{:S(2)}) async-start(f32[64,8,128]{2,1,0:T(8,128)} %bitcast.11), calls=%async_computation.7 | async-start | bytes 524288 | tf_op jit(solution)/shard_map/all_to_all | solution.py:48
  128.6 2.6 %collective-permute-start.5 = (bf16[2,2,128,256]{3,2,1,0:T(8,128)(2,1)S(1)}, bf16[2,2,128,256]{3,2,1,0:T(8,128)(2,1)S(1)}, u32[]{:S(2)}, u32[]{:S(2)}) collective-permute-start(bf16[2,2,128,256]{3,2,1,0:T(8,128)(2,1)S(1)} %get-tuple-element.48), channel_id=1, source_target_pairs={{0,8},{8,0},{1,9},{9,1},{2,10},{10,2},{3,11},{11,3},{4,12},{12,4},... | collective-permute-start | bytes 786440 | tf_op jit(solution)/shard_map/ppermute | solution.py:283
  131.2 1.9 %collective-permute-start.4 = (bf16[2,2,128,256]{3,2,1,0:T(8,128)(2,1)S(1)}, bf16[2,2,128,256]{3,2,1,0:T(8,128)(2,1)S(1)}, u32[]{:S(2)}, u32[]{:S(2)}) collective-permute-start(bf16[2,2,128,256]{3,2,1,0:T(8,128)(2,1)S(1)} %get-tuple-element.46), channel_id=1, source_target_pairs={{0,8},{8,0},{1,9},{9,1},{2,10},{10,2},{3,11},{11,3},{4,12},{12,4},... | collective-permute-start | bytes 786440 | tf_op jit(solution)/shard_map/ppermute | solution.py:283
  133.2 3.1 %collective-permute-start.6 = (bf16[2,2,128,256]{3,2,1,0:T(8,128)(2,1)S(1)}, bf16[2,2,128,256]{3,2,1,0:T(8,128)(2,1)S(1)}, u32[]{:S(2)}, u32[]{:S(2)}) collective-permute-start(bf16[2,2,128,256]{3,2,1,0:T(8,128)(2,1)S(1)} %shard_map.51), channel_id=1, source_target_pairs={{0,16},{16,0},{32,48},{48,32},{1,17},{17,1},{33,49},{49,33},{2,18}... | collective-permute-start | bytes 786440 | tf_op jit(solution)/shard_map/ppermute | solution.py:283
  137.1 9.4 %all-to-all-start.8 = ((bf16[32,8,128]{2,1,0:T(8,128)(2,1)}), bf16[32,8,128]{2,1,0:T(8,128)(2,1)S(1)}, u32[]{:S(2)}, u32[]{:S(2)}) async-start(bf16[32,8,128]{2,1,0:T(8,128)(2,1)} %bitcast.13), calls=%async_computation.8 | async-start | bytes 131072 | tf_op jit(solution)/shard_map/all_to_all | solution.py:48
  146.6 2.2 %collective-permute-start.7 = (bf16[2,128,256]{2,1,0:T(8,128)(2,1)S(1)}, bf16[2,128,256]{2,1,0:T(8,128)(2,1)S(1)}, u32[]{:S(2)}, u32[]{:S(2)}) collective-permute-start(bf16[2,128,256]{2,1,0:T(8,128)(2,1)S(1)} %get-tuple-element.50), channel_id=1, source_target_pairs={{0,48},{16,32},{32,16},{48,0},{1,49},{17,33},{33,17},{49,1},{2,50}... | collective-permute-start | bytes 393224 | tf_op jit(solution)/shard_map/ppermute | solution.py:283
  148.8 3.9 %all_gather.7.proto = bf16[2,256,128]{2,1,0:T(8,128)(2,1)S(1)} all-gather(bf16[1,256,128]{2,1,0:T(8,128)(2,1)S(1)} %bitcast.26), channel_id=1, replica_groups=mesh['y'=8,'x'=4,'c'=2,'z'=8] {'c'}, dimensions={0}, use_global_device_ids=true | all-gather | bytes 196608 | tf_op jit(solution)/shard_map/all_gather | solution.py:376
  153.5 1.3 shard_map.54
  (22 shorter events, 8.1 us)
Async XLA Ops:
  2.3 19.9 %all-to-all-start = ((bf16[8,64,128]{2,1,0:T(8,128)(2,1)}), bf16[8,64,128]{2,1,0:T(8,128)(2,1)S(1)}, u32[]{:S(2)}, u32[]{:S(2)}) async-start(bf16[8,64,128]{2,1,0:T(8,128)(2,1)} %get-tuple-element.29), calls=%async_computation | async-start | bytes 262144 | tf_op jit(solution)/shard_map/all_to_all | solution.py:48
  13.2 9.1 %collective-permute-start.2 = (bf16[2,256,128]{2,1,0:T(8,128)(2,1)S(1)}, bf16[2,256,128]{2,1,0:T(8,128)(2,1)S(1)}, u32[]{:S(2)}, u32[]{:S(2)}) collective-permute-start(bf16[2,256,128]{2,1,0:T(8,128)(2,1)S(1)} %get-tuple-element.28), channel_id=1, source_target_pairs={{0,48},{16,32},{32,16},{48,0},{1,49},{17,33},{33,17},{49,1},{2,50}... | collective-permute-start | bytes 393224 | tf_op jit(solution)/shard_map/ppermute | solution.py:283
  17.6 7.2 %collective-permute-start.1 = (bf16[2,256,128]{2,1,0:T(8,128)(2,1)S(1)}, bf16[2,256,128]{2,1,0:T(8,128)(2,1)S(1)}, u32[]{:S(2)}, u32[]{:S(2)}) collective-permute-start(bf16[2,256,128]{2,1,0:T(8,128)(2,1)S(1)} %get-tuple-element.28), channel_id=1, source_target_pairs={{0,32},{16,48},{32,0},{48,16},{1,33},{17,49},{33,1},{49,17},{2,34}... | collective-permute-start | bytes 393224 | tf_op jit(solution)/shard_map/ppermute | solution.py:283
  20.0 6.0 %collective-permute-start = (bf16[2,256,128]{2,1,0:T(8,128)(2,1)S(1)}, bf16[2,256,128]{2,1,0:T(8,128)(2,1)S(1)}, u32[]{:S(2)}, u32[]{:S(2)}) collective-permute-start(bf16[2,256,128]{2,1,0:T(8,128)(2,1)S(1)} %get-tuple-element.28), channel_id=1, source_target_pairs={{0,16},{16,0},{32,48},{48,32},{1,17},{17,1},{33,49},{49,33},{2,18}... | collective-permute-start | bytes 393224 | tf_op jit(solution)/shard_map/ppermute | solution.py:283
  26.1 5.8 %collective-permute-start.3 = (bf16[4,2,256,128]{3,2,1,0:T(8,128)(2,1)S(1)}, bf16[4,2,256,128]{3,2,1,0:T(8,128)(2,1)S(1)}, u32[]{:S(2)}, u32[]{:S(2)}) collective-permute-start(bf16[4,2,256,128]{3,2,1,0:T(8,128)(2,1)S(1)} %pad_maximum_fusion.rows.mine), channel_id=1, source_target_pairs={{0,8},{8,0},{1,9},{9,1},{2,10},{10,2},{3,11},{11,3},{4,12},{12,4},... | collective-permute-start | bytes 1572872 | tf_op jit(solution)/shard_map/ppermute | solution.py:283
  115.7 20.6 %all-to-all-start.7 = ((f32[64,8,128]{2,1,0:T(8,128)}), f32[64,8,128]{2,1,0:T(8,128)S(1)}, u32[]{:S(2)}, u32[]{:S(2)}) async-start(f32[64,8,128]{2,1,0:T(8,128)} %bitcast.11), calls=%async_computation.7 | async-start | bytes 524288 | tf_op jit(solution)/shard_map/all_to_all | solution.py:48
  128.6 4.5 %collective-permute-start.5 = (bf16[2,2,128,256]{3,2,1,0:T(8,128)(2,1)S(1)}, bf16[2,2,128,256]{3,2,1,0:T(8,128)(2,1)S(1)}, u32[]{:S(2)}, u32[]{:S(2)}) collective-permute-start(bf16[2,2,128,256]{3,2,1,0:T(8,128)(2,1)S(1)} %get-tuple-element.48), channel_id=1, source_target_pairs={{0,8},{8,0},{1,9},{9,1},{2,10},{10,2},{3,11},{11,3},{4,12},{12,4},... | collective-permute-start | bytes 786440 | tf_op jit(solution)/shard_map/ppermute | solution.py:283
  131.2 15.2 %collective-permute-start.4 = (bf16[2,2,128,256]{3,2,1,0:T(8,128)(2,1)S(1)}, bf16[2,2,128,256]{3,2,1,0:T(8,128)(2,1)S(1)}, u32[]{:S(2)}, u32[]{:S(2)}) collective-permute-start(bf16[2,2,128,256]{3,2,1,0:T(8,128)(2,1)S(1)} %get-tuple-element.46), channel_id=1, source_target_pairs={{0,8},{8,0},{1,9},{9,1},{2,10},{10,2},{3,11},{11,3},{4,12},{12,4},... | collective-permute-start | bytes 786440 | tf_op jit(solution)/shard_map/ppermute | solution.py:283
  133.2 13.2 %collective-permute-start.6 = (bf16[2,2,128,256]{3,2,1,0:T(8,128)(2,1)S(1)}, bf16[2,2,128,256]{3,2,1,0:T(8,128)(2,1)S(1)}, u32[]{:S(2)}, u32[]{:S(2)}) collective-permute-start(bf16[2,2,128,256]{3,2,1,0:T(8,128)(2,1)S(1)} %shard_map.51), channel_id=1, source_target_pairs={{0,16},{16,0},{32,48},{48,32},{1,17},{17,1},{33,49},{49,33},{2,18}... | collective-permute-start | bytes 786440 | tf_op jit(solution)/shard_map/ppermute | solution.py:283
  136.4 17.2 %copy-start = (bf16[2,256,128]{2,1,0:T(8,128)(2,1)S(1)}, bf16[2,256,128]{2,1,0:T(8,128)(2,1)}, u32[]{:S(2)}) copy-start(bf16[2,256,128]{2,1,0:T(8,128)(2,1)} %embeddings.3) | copy-start | bytes 393220
  137.1 11.7 %all-to-all-start.8 = ((bf16[32,8,128]{2,1,0:T(8,128)(2,1)}), bf16[32,8,128]{2,1,0:T(8,128)(2,1)S(1)}, u32[]{:S(2)}, u32[]{:S(2)}) async-start(bf16[32,8,128]{2,1,0:T(8,128)(2,1)} %bitcast.13), calls=%async_computation.8 | async-start | bytes 131072 | tf_op jit(solution)/shard_map/all_to_all | solution.py:48
  146.6 6.9 %collective-permute-start.7 = (bf16[2,128,256]{2,1,0:T(8,128)(2,1)S(1)}, bf16[2,128,256]{2,1,0:T(8,128)(2,1)S(1)}, u32[]{:S(2)}, u32[]{:S(2)}) collective-permute-start(bf16[2,128,256]{2,1,0:T(8,128)(2,1)S(1)} %get-tuple-element.50), channel_id=1, source_target_pairs={{0,48},{16,32},{32,16},{48,0},{1,49},{17,33},{33,17},{49,1},{2,50}... | collective-permute-start | bytes 393224 | tf_op jit(solution)/shard_map/ppermute | solution.py:283

commit v11 on v10

--- a/solution.py
+++ b/solution.py
@@ -209,7 +209,6 @@
     wide,
     ab,
     slopes,
-    units,
 ):
     acc[...] = jnp.zeros_like(acc)
     turned = jnp.concatenate([scale[...] * (1.0 / SHARP)] * 16, 0).T
@@ -235,15 +234,13 @@
                 ).astype(bf16)
         made = jnp.dot(flat[...], slope[...], preferred_element_type=f32).astype(bf16)
         for v in range(2):
-            units[half, slot, v] = made[:, v * U : (v + 1) * U]
+            out = (give_stay, give_near) if half else (stay, near)
+            out[slot // 2][v, slot % 2] = made[:, v * U : (v + 1) * U]
         acc[...] += jnp.dot(slope[...], rows[r].reshape(2 * U, 128), preferred_element_type=f32)
 
     for half, rows in enumerate((mine, other)):
-        members(lambda r, half=half, rows=rows: group(half, r, rows))
-    for i in range(2):
-        for v in range(2):
-            stay[v, i], near[v, i] = units[0, i, v], units[0, 2 + i, v]
-            give_stay[v, i], give_near[v, i] = units[1, i, v], units[1, 2 + i, v]
+        for r in range(NX):
+            group(half, r, rows)
     for i, (y, z) in enumerate(order(("y", "z"))):
         at = (z - GATHER_FIRST["z"]) % NZ * SUB + y * 8
         parts[i * 8 : (i + 1) * 8, :] = acc[at : at + 8, :]
@@ -364,7 +361,6 @@
             acc,
             pltpu.VMEM((4 * G, U), f32),
             pltpu.VMEM((2, COLS, 2 * U), bf16),
-            pltpu.VMEM((NC, NX, 2, 128, U), bf16),
         ],
     )
     pieces = exchange(parts, ("y", "z"))

time: 156 us -> 156 us (level)
  no operation moved by 1% of the time
where the time goes in v11:
time: 156 us; the launch traced here: 155 us
  blocking collectives  78.6 us (50%)
  starting transfers between devices  56.2 us (36%)
  Pallas kernels  14.2 us (9%)
  waiting for transfers between devices  4.92 us (3%)
    all_to_all x6, blocking collectives, exchange(): lax.all_to_all(x, axis, 0, 0, tiled=True, axis_index_groups=[members])  74.6 us
    all_to_all x3, starting transfers between devices, exchange(): lax.all_to_all(x, axis, 0, 0, tiled=True, axis_index_groups=[members])  33.2 us
    ppermute x8, starting transfers between devices, swap(): return lax.ppermute(x, axis, [(i, i ^ bit) for i in range(n)])  23 us
    pallas_call x13, Pallas kernels, call(): pl.pallas_call(kernel, out_shape=outs, in_specs=[VM] * len(args), out_spe...  12.5 us
    ppermute x8, waiting for transfers between devices, swap(): return lax.ppermute(x, axis, [(i, i ^ bit) for i in range(n)])  4.91 us
    all_gather x1, blocking collectives, body(): whole = lax.all_gather(whole, 'c', axis=0)  3.93 us
  transfers between devices with their start and end apart: 11, of which 4 were waited for; matrix products, arithmetic and copies ran while one was open for 0% of the time, Pallas kernels for 1%

profile of v11, /device:TPU:1, one launch (start us, length us, event | category | flops | bytes accessed | tf_op | source)
XLA Modules:
  0.0 154.8 jit_solution(3351238987942151162)
XLA Ops:
  0.6 1.7 %shard_map.41 = (bf16[2,256,128]{2,1,0:T(8,128)(2,1)S(1)}, f32[2,256,1]{2,1,0:T(8,128)S(1)}, bf16[8,64,128]{2,1,0:T(8,128)(2,1)}) custom-call(bf16[2,256,128]{2,1,0:T(8,128)(2,1)} %embeddings.3, bf16[128,512]{1,0:T(8,128)(2,1)} %prototypes.1), custom_call_target="tpu_custom_call" | custom-call | tf_op jit(solution)/shard_map/pallas_call | solution.py:288
  2.3 10.9 %all-to-all-start = ((bf16[8,64,128]{2,1,0:T(8,128)(2,1)}), bf16[8,64,128]{2,1,0:T(8,128)(2,1)S(1)}, u32[]{:S(2)}, u32[]{:S(2)}) async-start(bf16[8,64,128]{2,1,0:T(8,128)(2,1)} %get-tuple-element.29), calls=%async_computation | async-start | bytes 262144 | tf_op jit(solution)/shard_map/all_to_all | solution.py:48
  13.2 4.4 %collective-permute-start.2 = (bf16[2,256,128]{2,1,0:T(8,128)(2,1)S(1)}, bf16[2,256,128]{2,1,0:T(8,128)(2,1)S(1)}, u32[]{:S(2)}, u32[]{:S(2)}) collective-permute-start(bf16[2,256,128]{2,1,0:T(8,128)(2,1)S(1)} %get-tuple-element.28), channel_id=1, source_target_pairs={{0,48},{16,32},{32,16},{48,0},{1,49},{17,33},{33,17},{49,1},{2,50}... | collective-permute-start | bytes 393224 | tf_op jit(solution)/shard_map/ppermute | solution.py:280
  17.6 2.4 %collective-permute-start.1 = (bf16[2,256,128]{2,1,0:T(8,128)(2,1)S(1)}, bf16[2,256,128]{2,1,0:T(8,128)(2,1)S(1)}, u32[]{:S(2)}, u32[]{:S(2)}) collective-permute-start(bf16[2,256,128]{2,1,0:T(8,128)(2,1)S(1)} %get-tuple-element.28), channel_id=1, source_target_pairs={{0,32},{16,48},{32,0},{48,16},{1,33},{17,49},{33,1},{49,17},{2,34}... | collective-permute-start | bytes 393224 | tf_op jit(solution)/shard_map/ppermute | solution.py:280
  20.0 2.2 %collective-permute-start = (bf16[2,256,128]{2,1,0:T(8,128)(2,1)S(1)}, bf16[2,256,128]{2,1,0:T(8,128)(2,1)S(1)}, u32[]{:S(2)}, u32[]{:S(2)}) collective-permute-start(bf16[2,256,128]{2,1,0:T(8,128)(2,1)S(1)} %get-tuple-element.28), channel_id=1, source_target_pairs={{0,16},{16,0},{32,48},{48,32},{1,17},{17,1},{33,49},{49,33},{2,18}... | collective-permute-start | bytes 393224 | tf_op jit(solution)/shard_map/ppermute | solution.py:280
  22.3 2.5 %collective-permute-done.1 = bf16[2,256,128]{2,1,0:T(8,128)(2,1)S(1)} collective-permute-done((bf16[2,256,128]{2,1,0:T(8,128)(2,1)S(1)}, bf16[2,256,128]{2,1,0:T(8,128)(2,1)S(1)}, u32[]{:S(2)}, u32[]{:S(2)}) %collective-permute-start.1) | collective-permute-done | bytes 131104 | tf_op jit(solution)/shard_map/ppermute | solution.py:280
  24.8 1.2 collective-permute-done
  26.1 4.3 %collective-permute-start.3 = (bf16[4,2,256,128]{3,2,1,0:T(8,128)(2,1)S(1)}, bf16[4,2,256,128]{3,2,1,0:T(8,128)(2,1)S(1)}, u32[]{:S(2)}, u32[]{:S(2)}) collective-permute-start(bf16[4,2,256,128]{3,2,1,0:T(8,128)(2,1)S(1)} %pad_maximum_fusion.rows.mine), channel_id=1, source_target_pairs={{0,8},{8,0},{1,9},{9,1},{2,10},{10,2},{3,11},{11,3},{4,12},{12,4},... | collective-permute-start | bytes 1572872 | tf_op jit(solution)/shard_map/ppermute | solution.py:280
  31.9 1.2 shard_map.44
  33.1 17.6 %all_to_all.73 = bf16[64,8,128]{2,1,0:T(8,128)(2,1)S(1)} all-to-all(bf16[64,8,128]{2,1,0:T(8,128)(2,1)S(1)} %bitcast.24), channel_id=1, replica_groups={{261,262,263,256,257,258,259,260,325,326,327,320,321,322,323,324,389,39..., dimensions={0} | all-to-all | bytes 262144 | tf_op jit(solution)/shard_map/all_to_all | solution.py:48
  51.8 8.3 %all_to_all.74.rowmass.first = bf16[8,32,256]{2,1,0:T(8,128)(2,1)S(1)} all-to-all(bf16[8,32,256]{2,1,0:T(8,128)(2,1)S(1)} %shard_map.45), channel_id=1, replica_groups={{40,32,56,48,8,0,24,16},{41,33,57,49,9,1,25,17},{42,34,58,50,10,2,26,18..., dimensions={0} | all-to-all | bytes 262144 | tf_op jit(solution)/shard_map/all_to_all | solution.py:48
  60.8 16.0 %all_to_all.75 = bf16[64,8,128]{2,1,0:T(8,128)(2,1)S(1)} all-to-all(bf16[64,8,128]{2,1,0:T(8,128)(2,1)S(1)} %bitcast.22), channel_id=1, replica_groups={{261,262,263,256,257,258,259,260,325,326,327,320,321,322,323,324,389,39..., dimensions={0} | all-to-all | bytes 262144 | tf_op jit(solution)/shard_map/all_to_all | solution.py:48
  77.9 8.3 %all_to_all.76.rowmass = bf16[8,16,256]{2,1,0:T(8,128)(2,1)S(1)} all-to-all(bf16[8,16,256]{2,1,0:T(8,128)(2,1)S(1)} %shard_map.47), channel_id=1, replica_groups={{40,32,56,48,8,0,24,16},{41,33,57,49,9,1,25,17},{42,34,58,50,10,2,26,18..., dimensions={0} | all-to-all | bytes 131072 | tf_op jit(solution)/shard_map/all_to_all | solution.py:48
  87.0 16.2 %all_to_all.77 = bf16[64,8,128]{2,1,0:T(8,128)(2,1)S(1)} all-to-all(bf16[64,8,128]{2,1,0:T(8,128)(2,1)S(1)} %bitcast.21), channel_id=1, replica_groups={{261,262,263,256,257,258,259,260,325,326,327,320,321,322,323,324,389,39..., dimensions={0} | all-to-all | bytes 262144 | tf_op jit(solution)/shard_map/all_to_all | solution.py:48
  104.3 8.2 %all_to_all.78.last = bf16[8,16,256]{2,1,0:T(8,128)(2,1)S(1)} all-to-all(bf16[8,16,256]{2,1,0:T(8,128)(2,1)S(1)} %get-tuple-element.44), channel_id=1, replica_groups={{40,32,56,48,8,0,24,16},{41,33,57,49,9,1,25,17},{42,34,58,50,10,2,26,18..., dimensions={0} | all-to-all | bytes 131072 | tf_op jit(solution)/shard_map/all_to_all | solution.py:48
  112.5 3.2 %shard_map.50 = (bf16[2,2,128,256]{3,2,1,0:T(8,128)(2,1)S(1)}, bf16[2,2,128,256]{3,2,1,0:T(8,128)(2,1)S(1)}, bf16[2,2,128,256]{3,2,1,0:T(8,128)(2,1)S(1)}, bf16[...) custom-call(bf16[4,2,256,128]{3,2,1,0:T(8,128)(2,1)S(1)} %pad_maximum_fusion.rows.mine, ...), custom_call_target="tpu_custom_call" | custom-call | tf_op jit(solution)/shard_map/pallas_call | solution.py:53
  115.7 12.9 %all-to-all-start.7 = ((f32[64,8,128]{2,1,0:T(8,128)}), f32[64,8,128]{2,1,0:T(8,128)S(1)}, u32[]{:S(2)}, u32[]{:S(2)}) async-start(f32[64,8,128]{2,1,0:T(8,128)} %bitcast.11), calls=%async_computation.7 | async-start | bytes 524288 | tf_op jit(solution)/shard_map/all_to_all | solution.py:48
  128.6 2.6 %collective-permute-start.5 = (bf16[2,2,128,256]{3,2,1,0:T(8,128)(2,1)S(1)}, bf16[2,2,128,256]{3,2,1,0:T(8,128)(2,1)S(1)}, u32[]{:S(2)}, u32[]{:S(2)}) collective-permute-start(bf16[2,2,128,256]{3,2,1,0:T(8,128)(2,1)S(1)} %get-tuple-element.48), channel_id=1, source_target_pairs={{0,8},{8,0},{1,9},{9,1},{2,10},{10,2},{3,11},{11,3},{4,12},{12,4},... | collective-permute-start | bytes 786440 | tf_op jit(solution)/shard_map/ppermute | solution.py:280
  131.2 1.9 %collective-permute-start.4 = (bf16[2,2,128,256]{3,2,1,0:T(8,128)(2,1)S(1)}, bf16[2,2,128,256]{3,2,1,0:T(8,128)(2,1)S(1)}, u32[]{:S(2)}, u32[]{:S(2)}) collective-permute-start(bf16[2,2,128,256]{3,2,1,0:T(8,128)(2,1)S(1)} %get-tuple-element.46), channel_id=1, source_target_pairs={{0,8},{8,0},{1,9},{9,1},{2,10},{10,2},{3,11},{11,3},{4,12},{12,4},... | collective-permute-start | bytes 786440 | tf_op jit(solution)/shard_map/ppermute | solution.py:280
  133.2 3.1 %collective-permute-start.6 = (bf16[2,2,128,256]{3,2,1,0:T(8,128)(2,1)S(1)}, bf16[2,2,128,256]{3,2,1,0:T(8,128)(2,1)S(1)}, u32[]{:S(2)}, u32[]{:S(2)}) collective-permute-start(bf16[2,2,128,256]{3,2,1,0:T(8,128)(2,1)S(1)} %shard_map.51), channel_id=1, source_target_pairs={{0,16},{16,0},{32,48},{48,32},{1,17},{17,1},{33,49},{49,33},{2,18}... | collective-permute-start | bytes 786440 | tf_op jit(solution)/shard_map/ppermute | solution.py:280
  137.1 9.4 %all-to-all-start.8 = ((bf16[32,8,128]{2,1,0:T(8,128)(2,1)}), bf16[32,8,128]{2,1,0:T(8,128)(2,1)S(1)}, u32[]{:S(2)}, u32[]{:S(2)}) async-start(bf16[32,8,128]{2,1,0:T(8,128)(2,1)} %bitcast.13), calls=%async_computation.8 | async-start | bytes 131072 | tf_op jit(solution)/shard_map/all_to_all | solution.py:48
  146.6 2.2 %collective-permute-start.7 = (bf16[2,128,256]{2,1,0:T(8,128)(2,1)S(1)}, bf16[2,128,256]{2,1,0:T(8,128)(2,1)S(1)}, u32[]{:S(2)}, u32[]{:S(2)}) collective-permute-start(bf16[2,128,256]{2,1,0:T(8,128)(2,1)S(1)} %get-tuple-element.50), channel_id=1, source_target_pairs={{0,48},{16,32},{32,16},{48,0},{1,49},{17,33},{33,17},{49,1},{2,50}... | collective-permute-start | bytes 393224 | tf_op jit(solution)/shard_map/ppermute | solution.py:280
  148.8 3.9 %all_gather.7.proto = bf16[2,256,128]{2,1,0:T(8,128)(2,1)S(1)} all-gather(bf16[1,256,128]{2,1,0:T(8,128)(2,1)S(1)} %bitcast.26), channel_id=1, replica_groups=mesh['y'=8,'x'=4,'c'=2,'z'=8] {'c'}, dimensions={0}, use_global_device_ids=true | all-gather | bytes 196608 | tf_op jit(solution)/shard_map/all_gather | solution.py:372
  153.5 1.3 shard_map.54
  (22 shorter events, 8.1 us)
Async XLA Ops:
  2.3 19.9 %all-to-all-start = ((bf16[8,64,128]{2,1,0:T(8,128)(2,1)}), bf16[8,64,128]{2,1,0:T(8,128)(2,1)S(1)}, u32[]{:S(2)}, u32[]{:S(2)}) async-start(bf16[8,64,128]{2,1,0:T(8,128)(2,1)} %get-tuple-element.29), calls=%async_computation | async-start | bytes 262144 | tf_op jit(solution)/shard_map/all_to_all | solution.py:48
  13.2 9.1 %collective-permute-start.2 = (bf16[2,256,128]{2,1,0:T(8,128)(2,1)S(1)}, bf16[2,256,128]{2,1,0:T(8,128)(2,1)S(1)}, u32[]{:S(2)}, u32[]{:S(2)}) collective-permute-start(bf16[2,256,128]{2,1,0:T(8,128)(2,1)S(1)} %get-tuple-element.28), channel_id=1, source_target_pairs={{0,48},{16,32},{32,16},{48,0},{1,49},{17,33},{33,17},{49,1},{2,50}... | collective-permute-start | bytes 393224 | tf_op jit(solution)/shard_map/ppermute | solution.py:280
  17.6 7.2 %collective-permute-start.1 = (bf16[2,256,128]{2,1,0:T(8,128)(2,1)S(1)}, bf16[2,256,128]{2,1,0:T(8,128)(2,1)S(1)}, u32[]{:S(2)}, u32[]{:S(2)}) collective-permute-start(bf16[2,256,128]{2,1,0:T(8,128)(2,1)S(1)} %get-tuple-element.28), channel_id=1, source_target_pairs={{0,32},{16,48},{32,0},{48,16},{1,33},{17,49},{33,1},{49,17},{2,34}... | collective-permute-start | bytes 393224 | tf_op jit(solution)/shard_map/ppermute | solution.py:280
  20.0 6.0 %collective-permute-start = (bf16[2,256,128]{2,1,0:T(8,128)(2,1)S(1)}, bf16[2,256,128]{2,1,0:T(8,128)(2,1)S(1)}, u32[]{:S(2)}, u32[]{:S(2)}) collective-permute-start(bf16[2,256,128]{2,1,0:T(8,128)(2,1)S(1)} %get-tuple-element.28), channel_id=1, source_target_pairs={{0,16},{16,0},{32,48},{48,32},{1,17},{17,1},{33,49},{49,33},{2,18}... | collective-permute-start | bytes 393224 | tf_op jit(solution)/shard_map/ppermute | solution.py:280
  26.1 5.8 %collective-permute-start.3 = (bf16[4,2,256,128]{3,2,1,0:T(8,128)(2,1)S(1)}, bf16[4,2,256,128]{3,2,1,0:T(8,128)(2,1)S(1)}, u32[]{:S(2)}, u32[]{:S(2)}) collective-permute-start(bf16[4,2,256,128]{3,2,1,0:T(8,128)(2,1)S(1)} %pad_maximum_fusion.rows.mine), channel_id=1, source_target_pairs={{0,8},{8,0},{1,9},{9,1},{2,10},{10,2},{3,11},{11,3},{4,12},{12,4},... | collective-permute-start | bytes 1572872 | tf_op jit(solution)/shard_map/ppermute | solution.py:280
  115.7 20.6 %all-to-all-start.7 = ((f32[64,8,128]{2,1,0:T(8,128)}), f32[64,8,128]{2,1,0:T(8,128)S(1)}, u32[]{:S(2)}, u32[]{:S(2)}) async-start(f32[64,8,128]{2,1,0:T(8,128)} %bitcast.11), calls=%async_computation.7 | async-start | bytes 524288 | tf_op jit(solution)/shard_map/all_to_all | solution.py:48
  128.6 4.5 %collective-permute-start.5 = (bf16[2,2,128,256]{3,2,1,0:T(8,128)(2,1)S(1)}, bf16[2,2,128,256]{3,2,1,0:T(8,128)(2,1)S(1)}, u32[]{:S(2)}, u32[]{:S(2)}) collective-permute-start(bf16[2,2,128,256]{3,2,1,0:T(8,128)(2,1)S(1)} %get-tuple-element.48), channel_id=1, source_target_pairs={{0,8},{8,0},{1,9},{9,1},{2,10},{10,2},{3,11},{11,3},{4,12},{12,4},... | collective-permute-start | bytes 786440 | tf_op jit(solution)/shard_map/ppermute | solution.py:280
  131.2 15.2 %collective-permute-start.4 = (bf16[2,2,128,256]{3,2,1,0:T(8,128)(2,1)S(1)}, bf16[2,2,128,256]{3,2,1,0:T(8,128)(2,1)S(1)}, u32[]{:S(2)}, u32[]{:S(2)}) collective-permute-start(bf16[2,2,128,256]{3,2,1,0:T(8,128)(2,1)S(1)} %get-tuple-element.46), channel_id=1, source_target_pairs={{0,8},{8,0},{1,9},{9,1},{2,10},{10,2},{3,11},{11,3},{4,12},{12,4},... | collective-permute-start | bytes 786440 | tf_op jit(solution)/shard_map/ppermute | solution.py:280
  133.2 13.2 %collective-permute-start.6 = (bf16[2,2,128,256]{3,2,1,0:T(8,128)(2,1)S(1)}, bf16[2,2,128,256]{3,2,1,0:T(8,128)(2,1)S(1)}, u32[]{:S(2)}, u32[]{:S(2)}) collective-permute-start(bf16[2,2,128,256]{3,2,1,0:T(8,128)(2,1)S(1)} %shard_map.51), channel_id=1, source_target_pairs={{0,16},{16,0},{32,48},{48,32},{1,17},{17,1},{33,49},{49,33},{2,18}... | collective-permute-start | bytes 786440 | tf_op jit(solution)/shard_map/ppermute | solution.py:280
  136.4 17.2 %copy-start = (bf16[2,256,128]{2,1,0:T(8,128)(2,1)S(1)}, bf16[2,256,128]{2,1,0:T(8,128)(2,1)}, u32[]{:S(2)}) copy-start(bf16[2,256,128]{2,1,0:T(8,128)(2,1)} %embeddings.3) | copy-start | bytes 393220
  137.1 11.7 %all-to-all-start.8 = ((bf16[32,8,128]{2,1,0:T(8,128)(2,1)}), bf16[32,8,128]{2,1,0:T(8,128)(2,1)S(1)}, u32[]{:S(2)}, u32[]{:S(2)}) async-start(bf16[32,8,128]{2,1,0:T(8,128)(2,1)} %bitcast.13), calls=%async_computation.8 | async-start | bytes 131072 | tf_op jit(solution)/shard_map/all_to_all | solution.py:48
  146.6 6.9 %collective-permute-start.7 = (bf16[2,128,256]{2,1,0:T(8,128)(2,1)S(1)}, bf16[2,128,256]{2,1,0:T(8,128)(2,1)S(1)}, u32[]{:S(2)}, u32[]{:S(2)}) collective-permute-start(bf16[2,128,256]{2,1,0:T(8,128)(2,1)S(1)} %get-tuple-element.50), channel_id=1, source_target_pairs={{0,48},{16,32},{32,16},{48,0},{1,49},{17,33},{33,17},{49,1},{2,50}... | collective-permute-start | bytes 393224 | tf_op jit(solution)/shard_map/ppermute | solution.py:280

commit v12 on v11

--- a/solution.py
+++ b/solution.py
@@ -26,7 +26,7 @@
 
 
 SIZES = dict(y=NY, x=NX, c=NC, z=NZ)
-FIRST = dict(y=4, x=2, c=1, z=5)
+FIRST = dict(y=5, x=2, c=1, z=5)
 GATHER_FIRST = dict(z=0)
 
 

time: 156 us -> 156 us (level)
  no operation moved by 1% of the time
where the time goes in v12:
time: 156 us; the launch traced here: 154 us
  blocking collectives  78.7 us (50%)
  starting transfers between devices  54.9 us (35%)
  Pallas kernels  14.2 us (9%)
  waiting for transfers between devices  5.05 us (3%)
    all_to_all x6, blocking collectives, exchange(): lax.all_to_all(x, axis, 0, 0, tiled=True, axis_index_groups=[members])  74.6 us
    all_to_all x3, starting transfers between devices, exchange(): lax.all_to_all(x, axis, 0, 0, tiled=True, axis_index_groups=[members])  31.9 us
    ppermute x8, starting transfers between devices, swap(): return lax.ppermute(x, axis, [(i, i ^ bit) for i in range(n)])  23 us
    pallas_call x13, Pallas kernels, call(): pl.pallas_call(kernel, out_shape=outs, in_specs=[VM] * len(args), out_spe...  12.5 us
    ppermute x8, waiting for transfers between devices, swap(): return lax.ppermute(x, axis, [(i, i ^ bit) for i in range(n)])  4.13 us
    all_gather x1, blocking collectives, body(): whole = lax.all_gather(whole, 'c', axis=0)  4.03 us
  transfers between devices with their start and end apart: 11, of which 4 were waited for; matrix products, arithmetic and copies ran while one was open for 0% of the time, Pallas kernels for 1%

profile of v12, /device:TPU:1, one launch (start us, length us, event | category | flops | bytes accessed | tf_op | source)
XLA Modules:
  0.0 153.7 jit_solution(8520506287777901260)
XLA Ops:
  0.6 1.7 %shard_map.41 = (bf16[2,256,128]{2,1,0:T(8,128)(2,1)S(1)}, f32[2,256,1]{2,1,0:T(8,128)S(1)}, bf16[8,64,128]{2,1,0:T(8,128)(2,1)}) custom-call(bf16[2,256,128]{2,1,0:T(8,128)(2,1)} %embeddings.3, bf16[128,512]{1,0:T(8,128)(2,1)} %prototypes.1), custom_call_target="tpu_custom_call" | custom-call | tf_op jit(solution)/shard_map/pallas_call | solution.py:288
  2.3 10.9 %all-to-all-start = ((bf16[8,64,128]{2,1,0:T(8,128)(2,1)}), bf16[8,64,128]{2,1,0:T(8,128)(2,1)S(1)}, u32[]{:S(2)}, u32[]{:S(2)}) async-start(bf16[8,64,128]{2,1,0:T(8,128)(2,1)} %get-tuple-element.29), calls=%async_computation | async-start | bytes 262144 | tf_op jit(solution)/shard_map/all_to_all | solution.py:48
  13.2 4.4 %collective-permute-start.2 = (bf16[2,256,128]{2,1,0:T(8,128)(2,1)S(1)}, bf16[2,256,128]{2,1,0:T(8,128)(2,1)S(1)}, u32[]{:S(2)}, u32[]{:S(2)}) collective-permute-start(bf16[2,256,128]{2,1,0:T(8,128)(2,1)S(1)} %get-tuple-element.28), channel_id=1, source_target_pairs={{0,48},{16,32},{32,16},{48,0},{1,49},{17,33},{33,17},{49,1},{2,50}... | collective-permute-start | bytes 393224 | tf_op jit(solution)/shard_map/ppermute | solution.py:280
  17.6 2.4 %collective-permute-start.1 = (bf16[2,256,128]{2,1,0:T(8,128)(2,1)S(1)}, bf16[2,256,128]{2,1,0:T(8,128)(2,1)S(1)}, u32[]{:S(2)}, u32[]{:S(2)}) collective-permute-start(bf16[2,256,128]{2,1,0:T(8,128)(2,1)S(1)} %get-tuple-element.28), channel_id=1, source_target_pairs={{0,32},{16,48},{32,0},{48,16},{1,33},{17,49},{33,1},{49,17},{2,34}... | collective-permute-start | bytes 393224 | tf_op jit(solution)/shard_map/ppermute | solution.py:280
  20.0 2.2 %collective-permute-start = (bf16[2,256,128]{2,1,0:T(8,128)(2,1)S(1)}, bf16[2,256,128]{2,1,0:T(8,128)(2,1)S(1)}, u32[]{:S(2)}, u32[]{:S(2)}) collective-permute-start(bf16[2,256,128]{2,1,0:T(8,128)(2,1)S(1)} %get-tuple-element.28), channel_id=1, source_target_pairs={{0,16},{16,0},{32,48},{48,32},{1,17},{17,1},{33,49},{49,33},{2,18}... | collective-permute-start | bytes 393224 | tf_op jit(solution)/shard_map/ppermute | solution.py:280
  22.3 2.5 %collective-permute-done.1 = bf16[2,256,128]{2,1,0:T(8,128)(2,1)S(1)} collective-permute-done((bf16[2,256,128]{2,1,0:T(8,128)(2,1)S(1)}, bf16[2,256,128]{2,1,0:T(8,128)(2,1)S(1)}, u32[]{:S(2)}, u32[]{:S(2)}) %collective-permute-start.1) | collective-permute-done | bytes 131104 | tf_op jit(solution)/shard_map/ppermute | solution.py:280
  24.8 1.2 collective-permute-done
  26.1 4.3 %collective-permute-start.3 = (bf16[4,2,256,128]{3,2,1,0:T(8,128)(2,1)S(1)}, bf16[4,2,256,128]{3,2,1,0:T(8,128)(2,1)S(1)}, u32[]{:S(2)}, u32[]{:S(2)}) collective-permute-start(bf16[4,2,256,128]{3,2,1,0:T(8,128)(2,1)S(1)} %pad_maximum_fusion.rows.mine), channel_id=1, source_target_pairs={{0,8},{8,0},{1,9},{9,1},{2,10},{10,2},{3,11},{11,3},{4,12},{12,4},... | collective-permute-start | bytes 1572872 | tf_op jit(solution)/shard_map/ppermute | solution.py:280
  31.9 1.2 shard_map.44
  33.1 17.7 %all_to_all.73 = bf16[64,8,128]{2,1,0:T(8,128)(2,1)S(1)} all-to-all(bf16[64,8,128]{2,1,0:T(8,128)(2,1)S(1)} %bitcast.24), channel_id=1, replica_groups={{325,326,327,320,321,322,323,324,389,390,391,384,385,386,387,388,453,45..., dimensions={0} | all-to-all | bytes 262144 | tf_op jit(solution)/shard_map/all_to_all | solution.py:48
  51.9 8.7 %all_to_all.74.rowmass.first = bf16[8,32,256]{2,1,0:T(8,128)(2,1)S(1)} all-to-all(bf16[8,32,256]{2,1,0:T(8,128)(2,1)S(1)} %shard_map.45), channel_id=1, replica_groups={{40,32,56,48,8,0,24,16},{41,33,57,49,9,1,25,17},{42,34,58,50,10,2,26,18..., dimensions={0} | all-to-all | bytes 262144 | tf_op jit(solution)/shard_map/all_to_all | solution.py:48
  61.4 16.0 %all_to_all.75 = bf16[64,8,128]{2,1,0:T(8,128)(2,1)S(1)} all-to-all(bf16[64,8,128]{2,1,0:T(8,128)(2,1)S(1)} %bitcast.22), channel_id=1, replica_groups={{325,326,327,320,321,322,323,324,389,390,391,384,385,386,387,388,453,45..., dimensions={0} | all-to-all | bytes 262144 | tf_op jit(solution)/shard_map/all_to_all | solution.py:48
  78.4 8.0 %all_to_all.76.rowmass = bf16[8,16,256]{2,1,0:T(8,128)(2,1)S(1)} all-to-all(bf16[8,16,256]{2,1,0:T(8,128)(2,1)S(1)} %shard_map.47), channel_id=1, replica_groups={{40,32,56,48,8,0,24,16},{41,33,57,49,9,1,25,17},{42,34,58,50,10,2,26,18..., dimensions={0} | all-to-all | bytes 131072 | tf_op jit(solution)/shard_map/all_to_all | solution.py:48
  87.3 15.9 %all_to_all.77 = bf16[64,8,128]{2,1,0:T(8,128)(2,1)S(1)} all-to-all(bf16[64,8,128]{2,1,0:T(8,128)(2,1)S(1)} %bitcast.21), channel_id=1, replica_groups={{325,326,327,320,321,322,323,324,389,390,391,384,385,386,387,388,453,45..., dimensions={0} | all-to-all | bytes 262144 | tf_op jit(solution)/shard_map/all_to_all | solution.py:48
  104.2 8.3 %all_to_all.78.last = bf16[8,16,256]{2,1,0:T(8,128)(2,1)S(1)} all-to-all(bf16[8,16,256]{2,1,0:T(8,128)(2,1)S(1)} %get-tuple-element.44), channel_id=1, replica_groups={{40,32,56,48,8,0,24,16},{41,33,57,49,9,1,25,17},{42,34,58,50,10,2,26,18..., dimensions={0} | all-to-all | bytes 131072 | tf_op jit(solution)/shard_map/all_to_all | solution.py:48
  112.5 3.2 %shard_map.50 = (bf16[2,2,128,256]{3,2,1,0:T(8,128)(2,1)S(1)}, bf16[2,2,128,256]{3,2,1,0:T(8,128)(2,1)S(1)}, bf16[2,2,128,256]{3,2,1,0:T(8,128)(2,1)S(1)}, bf16[...) custom-call(bf16[4,2,256,128]{3,2,1,0:T(8,128)(2,1)S(1)} %pad_maximum_fusion.rows.mine, ...), custom_call_target="tpu_custom_call" | custom-call | tf_op jit(solution)/shard_map/pallas_call | solution.py:53
  115.7 11.6 %all-to-all-start.7 = ((f32[64,8,128]{2,1,0:T(8,128)}), f32[64,8,128]{2,1,0:T(8,128)S(1)}, u32[]{:S(2)}, u32[]{:S(2)}) async-start(f32[64,8,128]{2,1,0:T(8,128)} %bitcast.11), calls=%async_computation.7 | async-start | bytes 524288 | tf_op jit(solution)/shard_map/all_to_all | solution.py:48
  127.3 2.6 %collective-permute-start.5 = (bf16[2,2,128,256]{3,2,1,0:T(8,128)(2,1)S(1)}, bf16[2,2,128,256]{3,2,1,0:T(8,128)(2,1)S(1)}, u32[]{:S(2)}, u32[]{:S(2)}) collective-permute-start(bf16[2,2,128,256]{3,2,1,0:T(8,128)(2,1)S(1)} %get-tuple-element.48), channel_id=1, source_target_pairs={{0,8},{8,0},{1,9},{9,1},{2,10},{10,2},{3,11},{11,3},{4,12},{12,4},... | collective-permute-start | bytes 786440 | tf_op jit(solution)/shard_map/ppermute | solution.py:280
  129.9 1.9 %collective-permute-start.4 = (bf16[2,2,128,256]{3,2,1,0:T(8,128)(2,1)S(1)}, bf16[2,2,128,256]{3,2,1,0:T(8,128)(2,1)S(1)}, u32[]{:S(2)}, u32[]{:S(2)}) collective-permute-start(bf16[2,2,128,256]{3,2,1,0:T(8,128)(2,1)S(1)} %get-tuple-element.46), channel_id=1, source_target_pairs={{0,8},{8,0},{1,9},{9,1},{2,10},{10,2},{3,11},{11,3},{4,12},{12,4},... | collective-permute-start | bytes 786440 | tf_op jit(solution)/shard_map/ppermute | solution.py:280
  131.9 3.1 %collective-permute-start.6 = (bf16[2,2,128,256]{3,2,1,0:T(8,128)(2,1)S(1)}, bf16[2,2,128,256]{3,2,1,0:T(8,128)(2,1)S(1)}, u32[]{:S(2)}, u32[]{:S(2)}) collective-permute-start(bf16[2,2,128,256]{3,2,1,0:T(8,128)(2,1)S(1)} %shard_map.51), channel_id=1, source_target_pairs={{0,16},{16,0},{32,48},{48,32},{1,17},{17,1},{33,49},{49,33},{2,18}... | collective-permute-start | bytes 786440 | tf_op jit(solution)/shard_map/ppermute | solution.py:280
  135.7 9.4 %all-to-all-start.8 = ((bf16[32,8,128]{2,1,0:T(8,128)(2,1)}), bf16[32,8,128]{2,1,0:T(8,128)(2,1)S(1)}, u32[]{:S(2)}, u32[]{:S(2)}) async-start(bf16[32,8,128]{2,1,0:T(8,128)(2,1)} %bitcast.13), calls=%async_computation.8 | async-start | bytes 131072 | tf_op jit(solution)/shard_map/all_to_all | solution.py:48
  145.3 2.2 %collective-permute-start.7 = (bf16[2,128,256]{2,1,0:T(8,128)(2,1)S(1)}, bf16[2,128,256]{2,1,0:T(8,128)(2,1)S(1)}, u32[]{:S(2)}, u32[]{:S(2)}) collective-permute-start(bf16[2,128,256]{2,1,0:T(8,128)(2,1)S(1)} %get-tuple-element.50), channel_id=1, source_target_pairs={{0,48},{16,32},{32,16},{48,0},{1,49},{17,33},{33,17},{49,1},{2,50}... | collective-permute-start | bytes 393224 | tf_op jit(solution)/shard_map/ppermute | solution.py:280
  148.4 4.0 %all_gather.7.proto = bf16[2,256,128]{2,1,0:T(8,128)(2,1)S(1)} all-gather(bf16[1,256,128]{2,1,0:T(8,128)(2,1)S(1)} %bitcast.26), channel_id=1, replica_groups=mesh['y'=8,'x'=4,'c'=2,'z'=8] {'c'}, dimensions={0}, use_global_device_ids=true | all-gather | bytes 196608 | tf_op jit(solution)/shard_map/all_gather | solution.py:372
  152.4 1.3 shard_map.54
  (22 shorter events, 8.2 us)
Async XLA Ops:
  2.3 19.9 %all-to-all-start = ((bf16[8,64,128]{2,1,0:T(8,128)(2,1)}), bf16[8,64,128]{2,1,0:T(8,128)(2,1)S(1)}, u32[]{:S(2)}, u32[]{:S(2)}) async-start(bf16[8,64,128]{2,1,0:T(8,128)(2,1)} %get-tuple-element.29), calls=%async_computation | async-start | bytes 262144 | tf_op jit(solution)/shard_map/all_to_all | solution.py:48
  13.2 9.1 %collective-permute-start.2 = (bf16[2,256,128]{2,1,0:T(8,128)(2,1)S(1)}, bf16[2,256,128]{2,1,0:T(8,128)(2,1)S(1)}, u32[]{:S(2)}, u32[]{:S(2)}) collective-permute-start(bf16[2,256,128]{2,1,0:T(8,128)(2,1)S(1)} %get-tuple-element.28), channel_id=1, source_target_pairs={{0,48},{16,32},{32,16},{48,0},{1,49},{17,33},{33,17},{49,1},{2,50}... | collective-permute-start | bytes 393224 | tf_op jit(solution)/shard_map/ppermute | solution.py:280
  17.6 7.2 %collective-permute-start.1 = (bf16[2,256,128]{2,1,0:T(8,128)(2,1)S(1)}, bf16[2,256,128]{2,1,0:T(8,128)(2,1)S(1)}, u32[]{:S(2)}, u32[]{:S(2)}) collective-permute-start(bf16[2,256,128]{2,1,0:T(8,128)(2,1)S(1)} %get-tuple-element.28), channel_id=1, source_target_pairs={{0,32},{16,48},{32,0},{48,16},{1,33},{17,49},{33,1},{49,17},{2,34}... | collective-permute-start | bytes 393224 | tf_op jit(solution)/shard_map/ppermute | solution.py:280
  20.0 6.0 %collective-permute-start = (bf16[2,256,128]{2,1,0:T(8,128)(2,1)S(1)}, bf16[2,256,128]{2,1,0:T(8,128)(2,1)S(1)}, u32[]{:S(2)}, u32[]{:S(2)}) collective-permute-start(bf16[2,256,128]{2,1,0:T(8,128)(2,1)S(1)} %get-tuple-element.28), channel_id=1, source_target_pairs={{0,16},{16,0},{32,48},{48,32},{1,17},{17,1},{33,49},{49,33},{2,18}... | collective-permute-start | bytes 393224 | tf_op jit(solution)/shard_map/ppermute | solution.py:280
  26.1 5.8 %collective-permute-start.3 = (bf16[4,2,256,128]{3,2,1,0:T(8,128)(2,1)S(1)}, bf16[4,2,256,128]{3,2,1,0:T(8,128)(2,1)S(1)}, u32[]{:S(2)}, u32[]{:S(2)}) collective-permute-start(bf16[4,2,256,128]{3,2,1,0:T(8,128)(2,1)S(1)} %pad_maximum_fusion.rows.mine), channel_id=1, source_target_pairs={{0,8},{8,0},{1,9},{9,1},{2,10},{10,2},{3,11},{11,3},{4,12},{12,4},... | collective-permute-start | bytes 1572872 | tf_op jit(solution)/shard_map/ppermute | solution.py:280
  115.7 19.3 %all-to-all-start.7 = ((f32[64,8,128]{2,1,0:T(8,128)}), f32[64,8,128]{2,1,0:T(8,128)S(1)}, u32[]{:S(2)}, u32[]{:S(2)}) async-start(f32[64,8,128]{2,1,0:T(8,128)} %bitcast.11), calls=%async_computation.7 | async-start | bytes 524288 | tf_op jit(solution)/shard_map/all_to_all | solution.py:48
  127.3 4.5 %collective-permute-start.5 = (bf16[2,2,128,256]{3,2,1,0:T(8,128)(2,1)S(1)}, bf16[2,2,128,256]{3,2,1,0:T(8,128)(2,1)S(1)}, u32[]{:S(2)}, u32[]{:S(2)}) collective-permute-start(bf16[2,2,128,256]{3,2,1,0:T(8,128)(2,1)S(1)} %get-tuple-element.48), channel_id=1, source_target_pairs={{0,8},{8,0},{1,9},{9,1},{2,10},{10,2},{3,11},{11,3},{4,12},{12,4},... | collective-permute-start | bytes 786440 | tf_op jit(solution)/shard_map/ppermute | solution.py:280
  129.9 15.3 %collective-permute-start.4 = (bf16[2,2,128,256]{3,2,1,0:T(8,128)(2,1)S(1)}, bf16[2,2,128,256]{3,2,1,0:T(8,128)(2,1)S(1)}, u32[]{:S(2)}, u32[]{:S(2)}) collective-permute-start(bf16[2,2,128,256]{3,2,1,0:T(8,128)(2,1)S(1)} %get-tuple-element.46), channel_id=1, source_target_pairs={{0,8},{8,0},{1,9},{9,1},{2,10},{10,2},{3,11},{11,3},{4,12},{12,4},... | collective-permute-start | bytes 786440 | tf_op jit(solution)/shard_map/ppermute | solution.py:280
  131.9 13.3 %collective-permute-start.6 = (bf16[2,2,128,256]{3,2,1,0:T(8,128)(2,1)S(1)}, bf16[2,2,128,256]{3,2,1,0:T(8,128)(2,1)S(1)}, u32[]{:S(2)}, u32[]{:S(2)}) collective-permute-start(bf16[2,2,128,256]{3,2,1,0:T(8,128)(2,1)S(1)} %shard_map.51), channel_id=1, source_target_pairs={{0,16},{16,0},{32,48},{48,32},{1,17},{17,1},{33,49},{49,33},{2,18}... | collective-permute-start | bytes 786440 | tf_op jit(solution)/shard_map/ppermute | solution.py:280
  135.0 17.4 %copy-start = (bf16[2,256,128]{2,1,0:T(8,128)(2,1)S(1)}, bf16[2,256,128]{2,1,0:T(8,128)(2,1)}, u32[]{:S(2)}) copy-start(bf16[2,256,128]{2,1,0:T(8,128)(2,1)} %embeddings.3) | copy-start | bytes 393220
  135.7 12.7 %all-to-all-start.8 = ((bf16[32,8,128]{2,1,0:T(8,128)(2,1)}), bf16[32,8,128]{2,1,0:T(8,128)(2,1)S(1)}, u32[]{:S(2)}, u32[]{:S(2)}) async-start(bf16[32,8,128]{2,1,0:T(8,128)(2,1)} %bitcast.13), calls=%async_computation.8 | async-start | bytes 131072 | tf_op jit(solution)/shard_map/all_to_all | solution.py:48
  145.3 7.1 %collective-permute-start.7 = (bf16[2,128,256]{2,1,0:T(8,128)(2,1)S(1)}, bf16[2,128,256]{2,1,0:T(8,128)(2,1)S(1)}, u32[]{:S(2)}, u32[]{:S(2)}) collective-permute-start(bf16[2,128,256]{2,1,0:T(8,128)(2,1)S(1)} %get-tuple-element.50), channel_id=1, source_target_pairs={{0,48},{16,32},{32,16},{48,0},{1,49},{17,33},{33,17},{49,1},{2,50}... | collective-permute-start | bytes 393224 | tf_op jit(solution)/shard_map/ppermute | solution.py:280
